TPU v7x, 256 devices: a whole 4x4x8 slice. The times are simulated.
256 devices in a mesh: mesh: 64 (over x_hi, z, y), tx: 4 (over x_lo, core).
Axes of the slice: x: 4 (x_hi: 2, x_lo: 2; x = x_hi * 2 + x_lo), y: 4, z: 8, core: 2. Of those that a mesh axis runs over, the one named last changes fastest.
Arguments:
- tx_field: float32 [2, 400, 49152], P(None, 'tx', 'mesh'), may hold values from -6 to 6
- rx_field: float32 [2, 2048, 49152], P(None, 'tx', 'mesh'), may hold values from -6 to 6
- misfit_weight: float32 [2, 400, 2048], P(None, None, 'mesh'), may hold values from -0.0068359375 to 0.0068359375
- incidence: int32 [49152, 4], P('mesh'), may hold values from 0 to 32767, as said below
- component: int32 [49152], P('mesh'), may hold values from 0 to 2
Outputs:
- gradient: float32 [3, 32768], P(None, ('mesh', 'tx'))
Inputs may be any that keep to these rules, and one draw needn't show every extreme that they name: `incidence`: the edges of tile i (edges i * 768 to (i + 1) * 768 - 1) name only cells of tiles i - 1, i and i + 1, where tile i holds cells i * 512 to (i + 1) * 512 - 1.
All inputs are finite; a program needn't handle non-finite values.
Results may differ from a plain program's by a relative error of at most 0.00014.
Values sent between devices are 32-bit elements; how exact they have to be, the bound alone decides.
No kernel may reach another device: no remote copies, remote signals or barrier semaphores. Data moves between devices by JAX's collectives and lax.ppermute only.
A program may use at most 64 MiB of HBM per device.

v0:
```python
import jax
import jax.numpy as jnp
from jax import lax
from jax.sharding import PartitionSpec as P

CELL_TILE = 512


def passed_along(block, axis, distance):
    devices = range(lax.axis_size(axis))
    route = [(i - distance, i) for i in devices if i - distance in devices]
    return lax.ppermute(block, axis, route)


def complex_product(weight_real, weight_imag, field_real, field_imag):
    high = lax.Precision.HIGHEST
    q_real = jnp.dot(weight_real, field_real, precision=high) - jnp.dot(
        weight_imag, field_imag, precision=high
    )
    q_imag = jnp.dot(weight_real, field_imag, precision=high) + jnp.dot(
        weight_imag, field_real, precision=high
    )
    return jnp.stack([q_real, q_imag], axis=1)


def cell_partials(edge_term, incidence, component, cells):
    flat_index = component[:, None] * cells + incidence
    values = jnp.broadcast_to(0.25 * edge_term[:, None], flat_index.shape)
    summed = jax.ops.segment_sum(values.reshape(-1), flat_index.reshape(-1), num_segments=3 * cells)
    return summed.reshape(3, cells)


def tile_block(edge_term, incidence, component, tile_cells):
    mesh_index = lax.axis_index("mesh")
    local_index = incidence - (mesh_index - 1) * tile_cells
    partial_value = cell_partials(edge_term, local_index, component, 3 * tile_cells)
    lower_part = partial_value[:, :tile_cells]
    upper_part = partial_value[:, 2 * tile_cells :]
    from_upper = passed_along(lower_part, "mesh", -1)
    from_lower = passed_along(upper_part, "mesh", 1)
    return partial_value[:, tile_cells : 2 * tile_cells] + from_upper + from_lower


def shards(tx_field, rx_field, misfit_weight, incidence, component):
    group = tx_field.shape[1]
    tx_index = lax.axis_index("tx")
    own_rows = lax.dynamic_slice_in_dim(misfit_weight, tx_index * group, group, 1)
    group_weight = lax.all_gather(own_rows, "mesh", axis=2, tiled=True)
    piece = lax.all_gather(rx_field, "tx", axis=1, tiled=True)
    weighted = complex_product(group_weight[0], group_weight[1], piece[0], piece[1])
    edge_local = jnp.sum(tx_field[0] * weighted[:, 0, :] - tx_field[1] * weighted[:, 1, :], axis=0)
    tile_cells = CELL_TILE
    quarter = tile_cells // lax.axis_size("tx")
    edge_total = lax.psum(edge_local, "tx")
    own_block = tile_block(edge_total, incidence, component, tile_cells)
    return lax.dynamic_slice_in_dim(own_block, tx_index * quarter, quarter, 1)


def solution(mesh):
    return jax.shard_map(
        shards,
        mesh=mesh,
        in_specs=(
            P(None, "tx", "mesh"),
            P(None, "tx", "mesh"),
            P(None, None, "mesh"),
            P("mesh", None),
            P("mesh"),
        ),
        out_specs=P(None, ("mesh", "tx")),
        check_vma=False,
    )
```

profile of v0, /device:TPU:7, one launch (start us, length us, event | category | flops | bytes accessed | tf_op | source)
XLA Modules:
  0.0 319.3 jit_solution(13958764440898954816)
XLA Ops:
  6.5 0.9 copy-done
  7.4 0.7 constant_dynamic-slice_fusion
  8.1 0.0 all-gather.3.cloned.1.call-update
  8.1 0.0 all-gather.5.cloned.1.call-start
  8.2 0.7 all-gather.5.cloned.1.call-update
  8.9 0.7 broadcast_multiply_fusion.1
  9.6 0.7 subtract_add_fusion
  10.3 0.2 copy.8
  10.5 0.2 reshape.14
  10.7 1.8 fusion.12
  12.6 114.3 %all-gather.3.cloned.1.call-done = f32[2,100,2048]{1,2,0:T(8,128)} async-done(((f32[2,100,32]{1,2,0:T(8,128)}), f32[2,100,2048]{1,2,0:T(8,128)}) %all-gather.3.cloned.1.call-update) | async-done | bytes 1638416 | tf_op jit(solution)/shard_map/all_gather | solution.py:48
  126.9 122.2 %all-gather.5.cloned.1.call-done = f32[2,2048,768]{2,1,0:T(8,128)} async-done(((f32[2,512,768]{2,1,0:T(8,128)}), f32[2,2048,768]{2,1,0:T(8,128)}) %all-gather.5.cloned.1.call-update) | async-done | bytes 12582928 | tf_op jit(solution)/shard_map/all_gather | solution.py:49
  249.1 6.9 %fusion = f32[100,768]{1,0:T(8,128)S(1)} fusion(f32[2,2048,768]{2,1,0:T(8,128)} %all-gather.5.cloned.1.call-done, f32[2,100,2048]{1,2,0:T(8,128)} %all-gather.3.cloned.1.call-done), kind=kOutput, calls=%fused_computation.3 | convolution fusion | flops 1887436800 | bytes 7647232 | tf_op jit(solution)/shard_map/dot_general | solution.py:20
  256.0 6.4 %fusion.1 = f32[100,768]{1,0:T(8,128)S(1)} fusion(f32[2,2048,768]{2,1,0:T(8,128)} %all-gather.5.cloned.1.call-done, f32[2,100,2048]{1,2,0:T(8,128)S(1)} %copy-done.2), kind=kOutput, calls=%fused_computation.4 | convolution fusion | flops 1887436800 | bytes 7647232 | tf_op jit(solution)/shard_map/dot_general | solution.py:17
  262.5 3.7 %fusion.8 = f32[100,768]{1,0:T(8,128)S(1)} fusion(f32[100,768]{1,0:T(8,128)S(1)} %fusion, f32[2,2048,768]{2,1,0:T(8,128)S(1)} %copy-done.1, f32[2,100,2048]{1,2,0:T(8,128)S(1)} %copy-done.2, f32[1,100,768]{2,0,1:T(1,128)S(1)} %get-tuple-element.6), kind=kOutput, calls=%fused_computation.11 | convolution fusion | flops 1887590400 | bytes 8273920 | tf_op jit(solution)/shard_map/dot_general | solution.py:20
  266.2 3.8 %fusion.9 = f32[768]{0:T(1024)S(1)} fusion(f32[100,768]{1,0:T(8,128)S(1)} %fusion.8, f32[100,768]{1,0:T(8,128)S(1)} %fusion.1, f32[2,2048,768]{2,1,0:T(8,128)S(1)} %copy-done.1, f32[2,100,2048]{1,2,0:T(8,128)S(1)} %copy-done.2, f32[1,100,768]{2,0,1:T(1,128)S(1)} %get-tuple-element.5), kind=kOutput, calls=%fused_computation.12 | convolution fusion | flops 1887743232 | bytes 8289280 | tf_op jit(solution)/shard_map/dot_general | solution.py:17
  270.0 5.1 %psum.7 = f32[768]{0:T(1024)S(1)} all-reduce(f32[768]{0:T(1024)S(1)} %fusion.9), channel_id=1, replica_groups=mesh['mesh'=64,'tx'=4] {'tx'}, use_global_device_ids=true, to_apply=%region_1.0 | all-reduce | flops 768 | bytes 6144 | tf_op jit(solution)/shard_map/psum | solution.py:54
  275.2 0.2 broadcast_in_dim.5
  275.3 0.2 reshape.16
  275.5 18.7 %scatter_custom_fusion = f32[4608]{0:T(1024)S(1)} fusion(s32[3072]{0:T(1024)S(1)} %reshape.14, f32[3072]{0:T(1024)S(1)} %reshape.16, f32[]{:T(128)} %constant.12.clone.1), kind=kCustom, calls=%fused_computation.18 | custom fusion | flops 3072 | bytes 18436 | tf_op jit(solution)/shard_map/scatter-add | solution.py:29
  294.3 7.5 %collective-permute-start = (f32[3,512]{1,0:T(4,128)S(1)}, f32[3,512]{1,0:T(4,128)S(1)}, u32[]{:S(2)}, u32[]{:S(2)}) collective-permute-start(f32[3,512]{1,0:T(4,128)S(1)} %get-tuple-element.9), channel_id=1, source_target_pairs={{4,0},{8,4},{12,8},{16,12},{20,16},{24,20},{28,24},{32,28},{36,32}... | collective-permute-start | bytes 18440 | tf_op jit(solution)/shard_map/ppermute | solution.py:12
  301.8 1.9 collective-permute-start.1
  303.7 8.2 %collective-permute-done.1 = f32[3,512]{1,0:T(4,128)S(1)} collective-permute-done((f32[3,512]{1,0:T(4,128)S(1)}, f32[3,512]{1,0:T(4,128)S(1)}, u32[]{:S(2)}, u32[]{:S(2)}) %collective-permute-start.1) | collective-permute-done | bytes 6176 | tf_op jit(solution)/shard_map/ppermute | solution.py:12
  311.9 0.6 dynamic-slice_add_fusion
  (10 shorter events, 0.0 us)
Async XLA Ops:
  6.5 0.9 copy-start
  6.5 120.4 %all-gather.3.cloned.1.call-start = ((), (), s32[]{:S(2)}) async-start(), calls=%async_computation | async-start | bytes 2129920 | tf_op jit(solution)/shard_map/all_gather | solution.py:48
  8.1 241.0 %all-gather.5.cloned.1.call-start = ((), (), s32[]{:S(2)}) async-start(), calls=%async_computation.1 | async-start | bytes 15728640 | tf_op jit(solution)/shard_map/all_gather | solution.py:49
  126.9 129.1 %copy-start.2 = (f32[2,100,2048]{1,2,0:T(8,128)S(1)}, f32[2,100,2048]{1,2,0:T(8,128)}, u32[]{:S(2)}) copy-start(f32[2,100,2048]{1,2,0:T(8,128)} %all-gather.3.cloned.1.call-done) | copy-start | bytes 4915204
  249.1 13.4 %copy-start.1 = (f32[2,2048,768]{2,1,0:T(8,128)S(1)}, f32[2,2048,768]{2,1,0:T(8,128)}, u32[]{:S(2)}) copy-start(f32[2,2048,768]{2,1,0:T(8,128)} %all-gather.5.cloned.1.call-done) | copy-start | bytes 37748740
  294.3 9.4 %collective-permute-start = (f32[3,512]{1,0:T(4,128)S(1)}, f32[3,512]{1,0:T(4,128)S(1)}, u32[]{:S(2)}, u32[]{:S(2)}) collective-permute-start(f32[3,512]{1,0:T(4,128)S(1)} %get-tuple-element.9), channel_id=1, source_target_pairs={{4,0},{8,4},{12,8},{16,12},{20,16},{24,20},{28,24},{32,28},{36,32}... | collective-permute-start | bytes 18440 | tf_op jit(solution)/shard_map/ppermute | solution.py:12
  301.8 10.1 %collective-permute-start.1 = (f32[3,512]{1,0:T(4,128)S(1)}, f32[3,512]{1,0:T(4,128)S(1)}, u32[]{:S(2)}, u32[]{:S(2)}) collective-permute-start(f32[3,512]{1,0:T(4,128)S(1)} %get-tuple-element.8), channel_id=1, source_target_pairs={{0,4},{4,8},{8,12},{12,16},{16,20},{20,24},{24,28},{28,32},{32,36}... | collective-permute-start | bytes 18440 | tf_op jit(solution)/shard_map/ppermute | solution.py:12
Sparse Core Ops, SparseCore 0:
  10.9 115.9 all-gather.2
  128.7 120.3 all-gather.4
where the time goes:
time: 323 us; the launch traced here: 319 us
  waiting for transfers between devices  245 us (76%)
  matrix products  20.9 us (6%)
  other arithmetic  20.7 us (6%)
  between operations  13.5 us (4%)
  starting transfers between devices  9.47 us (3%)
  blocking collectives  5.13 us (2%)
  local copies, waits for them, and re-layouts  4.22 us (1%)
    all_gather x1, waiting for transfers between devices, shards(): piece = lax.all_gather(rx_field, 'tx', axis=1, tiled=True)  122 us
    all_gather x1, waiting for transfers between devices, shards(): group_weight = lax.all_gather(own_rows, 'mesh', axis=2, tiled=True)  114 us
    scatter-add x1, other arithmetic, cell_partials(): jax.ops.segment_sum(values.reshape(-1), flat_index.reshape(-1), num_segme...  18.7 us
    ppermute x2, starting transfers between devices, passed_along(): return lax.ppermute(block, axis, route)  9.42 us
    ppermute x2, waiting for transfers between devices, passed_along(): return lax.ppermute(block, axis, route)  8.18 us
    dot_general x1, matrix products, complex_product(): jnp.dot(weight_imag, field_real, precision=high)  6.91 us
  transfers between devices with their start and end apart: 4, of which 3 were waited for; matrix products, arithmetic and copies ran while one was open for 1% of the time, Pallas kernels for 0%

commit v1 on v0

v1 whole, which is shorter than its diff:
```python
import functools

import jax
import jax.numpy as jnp
from jax import lax
from jax.experimental import pallas as pl
from jax.experimental.pallas import tpu as pltpu
from jax.sharding import PartitionSpec as P

CELL_TILE = 512
AXES = ("mesh", "tx")
SIZE_Z, SIZE_Y = 8, 4
ROWS = 104
VMEM_LIMIT = 48 * 1024 * 1024


def coords(device):
    mesh_index, tx_index = divmod(device, 4)
    return mesh_index // 32, (mesh_index // 4) % 8, mesh_index % 4, tx_index // 2, tx_index % 2


def device_at(x_hi, z, y, x_lo, core):
    return ((x_hi % 2) * 32 + (z % 8) * 4 + y % 4) * 4 + (x_lo % 2) * 2 + core % 2


def fetch(block, source_of):
    route = [(device_at(*source_of(*coords(d))), d) for d in range(256)]
    return lax.ppermute(block, AXES, route)


def pack_kernel(w_ref, o_ref):
    for part in range(2):
        pieces = [w_ref[part, 100 * g : 100 * (g + 1), :] for g in range(4)]
        o_ref[part, 0:100, :] = jnp.concatenate(pieces, axis=1)
        o_ref[part, 100:ROWS, :] = jnp.zeros((ROWS - 100, 128), jnp.float32)


def pack_weight(misfit_weight):
    return pl.pallas_call(
        pack_kernel,
        out_shape=jax.ShapeDtypeStruct((2, ROWS, 128), jnp.float32),
        name="pack_weight",
    )(misfit_weight)


def split(value):
    high = value.astype(jnp.bfloat16)
    low = (value - high.astype(jnp.float32)).astype(jnp.bfloat16)
    return high, low


def prepare_kernel(place_ref, rx_ref, o_ref):
    real, imag = rx_ref[0], rx_ref[1]
    for n, value in enumerate((real, imag - real, real + imag)):
        high, low = split(value)
        o_ref[0, n, 0] = low
        o_ref[0, n, 1] = high


def prepare_fields(places, rx_field):
    edges = rx_field.shape[2]
    return pl.pallas_call(
        prepare_kernel,
        grid_spec=pltpu.PrefetchScalarGridSpec(
            num_scalar_prefetch=1,
            grid=(16,),
            in_specs=[pl.BlockSpec((2, 32, edges), lambda i, place: (0, place[i], 0))],
            out_specs=pl.BlockSpec((1, 3, 2, 32, edges), lambda i, place: (i // 8, 0, 0, i % 8, 0)),
        ),
        out_shape=jax.ShapeDtypeStruct((2, 3, 2, 256, edges), jnp.bfloat16),
        cost_estimate=pl.CostEstimate(flops=10_000_000, bytes_accessed=8_000_000, transcendentals=0),
        name="prepare_fields",
    )(places, rx_field)


def lane_group():
    return lax.broadcasted_iota(jnp.int32, (ROWS, 128), 1) // 32


def product_kernel(
    index_ref, own0, own1, above, below, far0, far1, t0, t1, t2, t3, field, before, o_ref, w_scr, wh_scr, wl_scr
):
    tx_index = index_ref[0]
    group = lane_group()
    own, far, txs = (own0, own1), (far0, far1), (t0, t1, t2, t3)
    for part in range(2):
        for k in range(2):
            blocks = [own[k][part], above[k, part], far[k][part], below[k, part]]
            rolled = [b if s == 0 else pltpu.roll(b, 32 * s, 1) for s, b in enumerate(blocks)]
            for g in range(4):
                mixed = rolled[(0 - g) % 4]
                for lane in range(1, 4):
                    mixed = jnp.where(group == lane, rolled[(lane - g) % 4], mixed)
                if g:
                    mixed = pltpu.roll(mixed, 128 - 32 * g, 1)
                row = pl.multiple_of(jnp.bitwise_xor(tx_index, g) * ROWS, 8)
                w_scr[part, pl.ds(row, ROWS), 128 * k : 128 * (k + 1)] = mixed
    real, imag = w_scr[0], w_scr[1]
    for n, value in enumerate((real + imag, real, imag)):
        high, low = split(value)
        wh_scr[n, :, 0:256] = high
        wh_scr[n, :, 256:512] = high
        wl_scr[n] = low
    for tile in range(field.shape[4] // 256):
        cols = slice(256 * tile, 256 * (tile + 1))
        products = []
        for n in range(3):
            both = field[0, n, :, :, cols].reshape(512, 256)
            high = field[0, n, 1, :, cols]
            products.append(
                jnp.dot(wh_scr[n], both, preferred_element_type=jnp.float32)
                + jnp.dot(wl_scr[n], high, preferred_element_type=jnp.float32)
            )
        total = before[:, cols]
        for g in range(4):
            rows = slice(ROWS * g, ROWS * g + 100)
            a, b = txs[g][0, :, cols], txs[g][1, :, cols]
            term = (a - b) * products[0][rows] - b * products[1][rows] - a * products[2][rows]
            total = total + jnp.sum(term, axis=0, keepdims=True)
        o_ref[:, cols] = total


def product(index, blocks, txs, fields, group, before):
    edges = fields.shape[4]
    whole = pl.BlockSpec(memory_space=pltpu.VMEM)
    return pl.pallas_call(
        product_kernel,
        grid_spec=pltpu.PrefetchScalarGridSpec(
            num_scalar_prefetch=1,
            grid=(1,),
            in_specs=[whole] * 10 + [pl.BlockSpec((1, 3, 2, 256, edges), lambda i, s: (group, 0, 0, 0, 0)), whole],
            out_specs=whole,
            scratch_shapes=[
                pltpu.VMEM((2, 4 * ROWS, 256), jnp.float32),
                pltpu.VMEM((3, 4 * ROWS, 512), jnp.bfloat16),
                pltpu.VMEM((3, 4 * ROWS, 256), jnp.bfloat16),
            ],
        ),
        out_shape=jax.ShapeDtypeStruct((1, edges), jnp.float32),
        compiler_params=pltpu.CompilerParams(vmem_limit_bytes=VMEM_LIMIT),
        cost_estimate=pl.CostEstimate(flops=3_000_000_000, bytes_accessed=6_000_000, transcendentals=0),
        name="product",
    )(index, *blocks, *txs, fields, before)


def onehot_kernel(index_ref, cells_ref, cells_t_ref, component_ref, hot_ref, row_ref):
    base, tx_index = index_ref[1], index_ref[0]
    lanes = lax.broadcasted_iota(jnp.int32, (cells_ref.shape[0], 128), 1)
    for j in range(4):
        lane = jnp.bitwise_and(cells_ref[:, j : j + 1], 127)
        hot_ref[j] = jnp.where(lanes == lane, 1.0, 0.0).astype(jnp.bfloat16)
    block = (cells_t_ref[...] - base) >> 7
    row = component_ref[...] * 3 + (block >> 2)
    row_ref[...] = jnp.where(jnp.bitwise_and(block, 3) == tx_index, row, -1)


def onehots(index, incidence, component):
    edges = incidence.shape[0]
    whole = pl.BlockSpec(memory_space=pltpu.VMEM)
    return pl.pallas_call(
        onehot_kernel,
        in_specs=[pl.BlockSpec(memory_space=pltpu.SMEM), whole, whole, whole],
        out_shape=(
            jax.ShapeDtypeStruct((4, edges, 128), jnp.bfloat16),
            jax.ShapeDtypeStruct((4, edges), jnp.int32),
        ),
        name="onehots",
    )(index, incidence, incidence.T, component[None, :])


def scatter_kernel(e0, e1, e2, e3, hot_ref, row_ref, low_ref, mid_ref, high_ref):
    total = 0.25 * ((e0[...] + e1[...]) + (e2[...] + e3[...]))
    edges = total.shape[1]
    rows = lax.broadcasted_iota(jnp.int32, (16, edges), 0)
    first = total.astype(jnp.bfloat16).astype(jnp.float32)
    rest = total - first
    second = rest.astype(jnp.bfloat16).astype(jnp.float32)
    third = rest - second
    summed = jnp.zeros((48, 128), jnp.float32)
    for j in range(4):
        hit = rows == row_ref[j : j + 1, :]
        left = jnp.concatenate([jnp.where(hit, v, 0.0) for v in (first, second, third)], axis=0)
        summed += jnp.dot(left.astype(jnp.bfloat16), hot_ref[j], preferred_element_type=jnp.float32)
    cells = (summed[0:16] + summed[16:32]) + summed[32:48]
    for k in range(3):
        low_ref[k : k + 1, :] = cells[3 * k : 3 * k + 1, :]
        mid_ref[k : k + 1, :] = cells[3 * k + 1 : 3 * k + 2, :]
        high_ref[k : k + 1, :] = cells[3 * k + 2 : 3 * k + 3, :]


def scatter(terms, hot, row):
    return pl.pallas_call(
        scatter_kernel,
        out_shape=[jax.ShapeDtypeStruct((3, 128), jnp.float32)] * 3,
        name="scatter_cells",
    )(*terms, hot, row)


def passed_along(block, distance):
    route = [((i - distance) * 4 + j, i * 4 + j) for i in range(64) for j in range(4) if 0 <= i - distance < 64]
    return lax.ppermute(block, AXES, route)


def flip_x(x_hi, z, y, x_lo, core):
    return x_hi, z, y, 1 - x_lo, core


def flip_core(x_hi, z, y, x_lo, core):
    return x_hi, z, y, x_lo, 1 - core


def flip_both(x_hi, z, y, x_lo, core):
    return x_hi, z, y, 1 - x_lo, 1 - core


def z_source(k):
    return lambda x_hi, z, y, x_lo, core: (x_lo, 4 * core + (z + k) % 4, y, x_hi, z // 4)


def y_source(step):
    return lambda x_hi, z, y, x_lo, core: (x_hi, z, y + step, x_lo, core)


def shards(tx_field, rx_field, misfit_weight, incidence, component):
    mesh_index = lax.axis_index("mesh")
    tx_index = lax.axis_index("tx")
    z, y = (mesh_index // 4) % 8, mesh_index % 4
    packed = pack_weight(misfit_weight)
    tx_x = fetch(tx_field, flip_x)
    from_z = [fetch(packed, z_source(k)) for k in range(4)]
    tx_c = fetch(tx_field, flip_core)
    tx_xc = fetch(tx_x, flip_core)
    txs = [tx_field, tx_c, tx_x, tx_xc]

    steps = jnp.arange(16, dtype=jnp.int32)
    places = ((z + steps // 4) % 4) * 4 + (y + steps % 4) % 4
    fields = prepare_fields(places.astype(jnp.int32), rx_field)
    index = jnp.stack([tx_index, (mesh_index - 1) * CELL_TILE]).astype(jnp.int32)
    hot, row = onehots(index, incidence, component)

    edge = jnp.zeros((1, tx_field.shape[2]), jnp.float32)
    for group in range(2):
        own = from_z[2 * group : 2 * group + 2]
        stacked = jnp.stack(own)
        above = fetch(stacked, y_source(1))
        below = fetch(stacked, y_source(-1))
        far0 = fetch(above[0], y_source(1))
        far1 = fetch(below[1], y_source(-1))
        blocks = [own[0], own[1], above, below, far0, far1]
        edge = product(index, blocks, txs, fields, group, edge)
    terms = [edge, fetch(edge, flip_core), fetch(edge, flip_x), fetch(edge, flip_both)]
    low, mid, high = scatter(terms, hot, row)
    return mid + passed_along(low, -1) + passed_along(high, 1)


def solution(mesh):
    return jax.shard_map(
        shards,
        mesh=mesh,
        in_specs=(
            P(None, "tx", "mesh"),
            P(None, "tx", "mesh"),
            P(None, None, "mesh"),
            P("mesh", None),
            P("mesh"),
        ),
        out_specs=P(None, ("mesh", "tx")),
        check_vma=False,
    )
```

time: 323 us -> 90.1 us (0.28)
  waiting for transfers between devices: 245 us -> 16.9 us
  starting transfers between devices: 9.47 us -> 38.2 us
  Pallas kernels: 0 us -> 26 us
  matrix products: 20.9 us -> 0 us
  other arithmetic: 20.7 us -> 1.88 us
  between operations: 13.5 us -> 0.25 us
  blocking collectives: 5.13 us -> 0 us
    all_gather x2 -> x0, waiting for transfers between devices: 237 us -> none  [the longest x1 122 us: shards(): piece = lax.all_gather(rx_field, 'tx', axis=1, tiled=True)]
    ppermute x2 -> x20, starting transfers between devices: 9.42 us -> 38.2 us  [the longest x18 28 us: fetch(): return lax.ppermute(block, AXES, route)]
    pallas_call x0 -> x6, Pallas kernels: none -> 26 us  [the longest x1 11 us: prepare_fields(): pl.pallas_call(prepare_kernel, grid_spec=pltpu.PrefetchScalarGridSpec(num...]
    dot_general x4 -> x0, matrix products: 20.9 us -> none  [the longest x1 6.91 us: complex_product(): jnp.dot(weight_imag, field_real, precision=high)]
    scatter-add x1 -> x0, other arithmetic: 18.7 us -> none  [cell_partials(): jax.ops.segment_sum(values.reshape(-1), flat_index.reshape(-1), num_segme...]
    ppermute x2 -> x20, waiting for transfers between devices: 8.18 us -> 16.9 us  [the longest x18 8.6 us: fetch(): return lax.ppermute(block, AXES, route)]
    psum x1 -> x0, blocking collectives: 5.13 us -> none  [shards(): edge_total = lax.psum(edge_local, 'tx')]
    unnamed x6 -> x19, local copies, waits for them, and re-layouts: 0.91 us -> 4.52 us
  transfers between devices with their start and end apart: 4 -> 20, of which waited for: 3 -> 6; matrix products, arithmetic and copies ran while one was open for 1% -> 4% of each run, Pallas kernels for 0% -> 20%
where the time goes in v1:
time: 90.1 us; the launch traced here: 88.5 us
  starting transfers between devices  38.2 us (42%)
  Pallas kernels  26 us (29%)
  waiting for transfers between devices  16.9 us (19%)
  local copies, waits for them, and re-layouts  5.29 us (6%)
  other arithmetic  1.88 us (2%)
    ppermute x18, starting transfers between devices, fetch(): return lax.ppermute(block, AXES, route)  28 us
    pallas_call x1, Pallas kernels, prepare_fields(): pl.pallas_call(prepare_kernel, grid_spec=pltpu.PrefetchScalarGridSpec(num...  11 us
    ppermute x2, starting transfers between devices, passed_along(): return lax.ppermute(block, AXES, route)  10.2 us
    pallas_call x2, Pallas kernels, product(): pl.pallas_call(product_kernel, grid_spec=pltpu.PrefetchScalarGridSpec(num...  8.71 us
    ppermute x18, waiting for transfers between devices, fetch(): return lax.ppermute(block, AXES, route)  8.6 us
    ppermute x2, waiting for transfers between devices, passed_along(): return lax.ppermute(block, AXES, route)  8.33 us
    unnamed x19, local copies, waits for them, and re-layouts  4.52 us
    pallas_call x1, Pallas kernels, onehots(): pl.pallas_call(onehot_kernel, in_specs=[pl.BlockSpec(memory_space=pltpu.S...  2.39 us
  transfers between devices with their start and end apart: 20, of which 6 were waited for; matrix products, arithmetic and copies ran while one was open for 4% of the time, Pallas kernels for 20%

profile of v1, /device:TPU:7, one launch (start us, length us, event | category | flops | bytes accessed | tf_op | source)
XLA Modules:
  0.0 88.5 jit_solution(17906103175429876625)
XLA Ops:
  0.0 1.9 %copy.12.w_ref = f32[2,400,32]{2,1,0:T(8,128)} copy(f32[2,400,32]{1,2,0:T(8,128)} %param.7) | data formatting | bytes 204800 | tf_op args[2]
  1.9 1.8 %pack_weight.1 = f32[2,104,128]{2,1,0:T(8,128)} custom-call(f32[2,400,32]{2,1,0:T(8,128)} %copy.12.w_ref), custom_call_target="tpu_custom_call" | custom-call | tf_op jit(solution)/shard_map/pack_weight/pallas_call | solution.py:39
  3.7 9.5 %collective-permute-start.9 = (f32[2,104,128]{2,1,0:T(8,128)}, f32[2,104,128]{2,1,0:T(8,128)S(1)}, u32[]{:S(2)}, u32[]{:S(2)}) collective-permute-start(f32[2,104,128]{2,1,0:T(8,128)} %pack_weight.1), channel_id=1, source_target_pairs={{0,0},{64,1},{128,2},{192,3},{4,4},{68,5},{132,6},{196,7},{8,8},{7... | collective-permute-start | bytes 319496 | tf_op jit(solution)/shard_map/ppermute | solution.py:28
  14.3 5.0 %collective-permute-start = (f32[2,104,128]{2,1,0:T(8,128)}, f32[2,104,128]{2,1,0:T(8,128)S(1)}, u32[]{:S(2)}, u32[]{:S(2)}) collective-permute-start(f32[2,104,128]{2,1,0:T(8,128)} %pack_weight.1), channel_id=1, source_target_pairs={{32,0},{96,1},{160,2},{224,3},{36,4},{100,5},{164,6},{228,7},{40,8... | collective-permute-start | bytes 319496 | tf_op jit(solution)/shard_map/ppermute | solution.py:28
  19.8 1.1 %copy.17.t0 = f32[2,100,768]{2,1,0:T(8,128)S(1)} copy(f32[2,100,768]{2,0,1:T(2,128)} %param.5) | data formatting | bytes 1228800 | tf_op args[0]
  21.0 11.0 %prepare_fields.1.field = bf16[2,3,2,256,768]{4,3,2,1,0:T(8,128)(2,1)} custom-call(s32[16]{0:T(128)} %fusion.1.place_ref, f32[2,512,768]{2,1,0:T(8,128)} %rx_ref.1), custom_call_target="tpu_custom_call" | custom-call | flops 10000000 | bytes 8000000 | tf_op jit(solution)/shard_map/prepare_fields/pallas_call | solution.py:62
  32.5 2.8 %collective-permute-start.11 = (f32[2,2,104,128]{3,2,1,0:T(8,128)S(1)}, f32[2,2,104,128]{3,2,1,0:T(8,128)S(1)}, u32[]{:S(2)}, u32[]{:S(2)}) collective-permute-start(f32[2,2,104,128]{3,2,1,0:T(8,128)S(1)} %pad_maximum_fusion.1), channel_id=1, source_target_pairs={{4,0},{5,1},{6,2},{7,3},{8,4},{9,5},{10,6},{11,7},{12,8},{13,9},{1... | collective-permute-start | bytes 638984 | tf_op jit(solution)/shard_map/ppermute | solution.py:28
  35.4 2.2 %collective-permute-done.1.own1 = f32[2,104,128]{2,1,0:T(8,128)S(1)} collective-permute-done((f32[2,104,128]{2,1,0:T(8,128)S(1)}, f32[2,104,128]{2,1,0:T(8,128)S(1)}, u32[]{:S(2)}, u32[]{:S(2)}) %collective-permute-start.1) | collective-permute-done | bytes 106528 | tf_op jit(solution)/shard_map/ppermute | solution.py:28
  37.7 2.5 %collective-permute-start.2 = (f32[2,2,104,128]{3,2,1,0:T(8,128)S(1)}, f32[2,2,104,128]{3,2,1,0:T(8,128)S(1)}, u32[]{:S(2)}, u32[]{:S(2)}) collective-permute-start(f32[2,2,104,128]{3,2,1,0:T(8,128)S(1)} %pad_maximum_fusion), channel_id=1, source_target_pairs={{4,0},{5,1},{6,2},{7,3},{8,4},{9,5},{10,6},{11,7},{12,8},{13,9},{1... | collective-permute-start | bytes 638984 | tf_op jit(solution)/shard_map/ppermute | solution.py:28
  40.2 1.6 %collective-permute-done.12.below = f32[2,2,104,128]{3,2,1,0:T(8,128)S(1)} collective-permute-done((f32[2,2,104,128]{3,2,1,0:T(8,128)S(1)}, f32[2,2,104,128]{3,2,1,0:T(8,128)S(1)}, u32[]{:S(2)}, u32[]{:S(2)}) %collective-permute-start.12) | collective-permute-done | bytes 213024 | tf_op jit(solution)/shard_map/ppermute | solution.py:28
  41.8 1.1 %collective-permute-start.13 = (f32[2,104,128]{2,1,0:T(8,128)S(1)}, f32[2,104,128]{2,1,0:T(8,128)S(1)}, u32[]{:S(2)}, u32[]{:S(2)}) collective-permute-start(f32[2,104,128]{2,1,0:T(8,128)S(1)} %slice_bitcast_fusion.1), channel_id=1, source_target_pairs={{4,0},{5,1},{6,2},{7,3},{8,4},{9,5},{10,6},{11,7},{12,8},{13,9},{1... | collective-permute-start | bytes 319496 | tf_op jit(solution)/shard_map/ppermute | solution.py:28
  43.0 1.6 %collective-permute-done.2.above = f32[2,2,104,128]{3,2,1,0:T(8,128)S(1)} collective-permute-done((f32[2,2,104,128]{3,2,1,0:T(8,128)S(1)}, f32[2,2,104,128]{3,2,1,0:T(8,128)S(1)}, u32[]{:S(2)}, u32[]{:S(2)}) %collective-permute-start.2) | collective-permute-done | bytes 213024 | tf_op jit(solution)/shard_map/ppermute | solution.py:28
  45.1 1.8 %collective-permute-done.3.below = f32[2,2,104,128]{3,2,1,0:T(8,128)S(1)} collective-permute-done((f32[2,2,104,128]{3,2,1,0:T(8,128)S(1)}, f32[2,2,104,128]{3,2,1,0:T(8,128)S(1)}, u32[]{:S(2)}, u32[]{:S(2)}) %collective-permute-start.3) | collective-permute-done | bytes 213024 | tf_op jit(solution)/shard_map/ppermute | solution.py:28
  46.9 1.2 %collective-permute-start.4 = (f32[2,104,128]{2,1,0:T(8,128)S(1)}, f32[2,104,128]{2,1,0:T(8,128)S(1)}, u32[]{:S(2)}, u32[]{:S(2)}) collective-permute-start(f32[2,104,128]{2,1,0:T(8,128)S(1)} %slice_bitcast_fusion.3), channel_id=1, source_target_pairs={{4,0},{5,1},{6,2},{7,3},{8,4},{9,5},{10,6},{11,7},{12,8},{13,9},{1... | collective-permute-start | bytes 319496 | tf_op jit(solution)/shard_map/ppermute | solution.py:28
  48.8 1.3 %collective-permute-done.14.far1 = f32[2,104,128]{2,1,0:T(8,128)S(1)} collective-permute-done((f32[2,104,128]{2,1,0:T(8,128)S(1)}, f32[2,104,128]{2,1,0:T(8,128)S(1)}, u32[]{:S(2)}, u32[]{:S(2)}) %collective-permute-start.14) | collective-permute-done | bytes 106528 | tf_op jit(solution)/shard_map/ppermute | solution.py:28
  50.1 4.3 %product.2.before = f32[1,768]{1,0:T(1,128)S(1)} custom-call(s32[2]{0:T(128)S(1)} %pad_add_fusion.index_ref, f32[2,104,128]{2,1,0:T(8,128)S(1)} %collective-permute-done.9.own0, f32[2,104,128]{2,1,0:T(8,128)S(1)} %collective-permute-done.10.own1, f32[2,2,104,128]{3,2,1,0:T(8,128)S(1)} %collective-permute-done.11.above, ...), custom_call_target="tpu_custom_call" | custom-call | flops 3000000000 | bytes 6000000 | tf_op jit(solution)/shard_map/product/pallas_call | solution.py:126
  54.5 4.4 %product.3.e0 = f32[1,768]{1,0:T(1,128)S(1)} custom-call(s32[2]{0:T(128)S(1)} %pad_add_fusion.index_ref, f32[2,104,128]{2,1,0:T(8,128)S(1)} %collective-permute-done.own0, f32[2,104,128]{2,1,0:T(8,128)S(1)} %collective-permute-done.1.own1, f32[2,2,104,128]{3,2,1,0:T(8,128)S(1)} %collective-permute-done.2.above, ...), custom_call_target="tpu_custom_call" | custom-call | flops 3000000000 | bytes 6000000 | tf_op jit(solution)/shard_map/product/pallas_call | solution.py:126
  59.1 2.9 %collective-permute-start.16 = (f32[1,768]{1,0:T(1,128)S(1)}, f32[1,768]{1,0:T(1,128)S(1)}, u32[]{:S(2)}, u32[]{:S(2)}) collective-permute-start(f32[1,768]{1,0:T(1,128)S(1)} %product.3.e0), channel_id=1, source_target_pairs={{2,0},{3,1},{0,2},{1,3},{6,4},{7,5},{4,6},{5,7},{10,8},{11,9},{8,1... | collective-permute-start | bytes 9224 | tf_op jit(solution)/shard_map/ppermute | solution.py:28
  63.7 2.4 %onehots.1 = (bf16[4,768,128]{2,1,0:T(8,128)(2,1)}, s32[4,768]{1,0:T(4,128)}) custom-call(s32[2]{0:T(128)} %copy-done.1, s32[768,4]{1,0:T(8,128)} %copy.21.cells_ref, s32[4,768]{1,0:T(4,128)} %bitcast.19, s32[1,768]{1,0:T(1,128)} %broadcast_in_dim.7.component_ref), custom_call_target="tpu_custom_call" | custom-call | tf_op jit(solution)/shard_map/onehots/pallas_call | solution.py:160
  66.7 2.0 %scatter_cells.1 = (f32[3,128]{1,0:T(4,128)}, f32[3,128]{1,0:T(4,128)}, f32[3,128]{1,0:T(4,128)}) custom-call(f32[1,768]{1,0:T(1,128)} %copy-done, f32[1,768]{1,0:T(1,128)} %copy-done.5, f32[1,768]{1,0:T(1,128)} %copy-done.6, f32[1,768]{1,0:T(1,128)} %copy-done.7, bf16[4,768,128]{2,1,0:T(8,128)(2,1)} %get-tuple-element.10.hot_ref, ...), custom_call_target="tpu_custom_call" | custom-call | tf_op jit(solution)/shard_map/scatter_cells/pallas_call | solution.py:192
  68.7 8.3 %collective-permute-start.18 = (f32[3,128]{1,0:T(4,128)}, f32[3,128]{1,0:T(4,128)S(1)}, u32[]{:S(2)}, u32[]{:S(2)}) collective-permute-start(f32[3,128]{1,0:T(4,128)} %get-tuple-element.13), channel_id=1, source_target_pairs={{4,0},{5,1},{6,2},{7,3},{8,4},{9,5},{10,6},{11,7},{12,8},{13,9},{1... | collective-permute-start | bytes 4616 | tf_op jit(solution)/shard_map/ppermute | solution.py:201
  77.0 1.9 %collective-permute-start.19 = (f32[3,128]{1,0:T(4,128)}, f32[3,128]{1,0:T(4,128)S(1)}, u32[]{:S(2)}, u32[]{:S(2)}) collective-permute-start(f32[3,128]{1,0:T(4,128)} %get-tuple-element.14), channel_id=1, source_target_pairs={{0,4},{1,5},{2,6},{3,7},{4,8},{5,9},{6,10},{7,11},{8,12},{9,13},{1... | collective-permute-start | bytes 4616 | tf_op jit(solution)/shard_map/ppermute | solution.py:201
  78.9 8.3 %collective-permute-done.19 = f32[3,128]{1,0:T(4,128)S(1)} collective-permute-done((f32[3,128]{1,0:T(4,128)}, f32[3,128]{1,0:T(4,128)S(1)}, u32[]{:S(2)}, u32[]{:S(2)}) %collective-permute-start.19) | collective-permute-done | bytes 1568 | tf_op jit(solution)/shard_map/ppermute | solution.py:201
  87.2 1.3 %add_add_fusion = f32[3,128]{1,0:T(4,128)} fusion(f32[3,128]{1,0:T(4,128)S(1)} %collective-permute-done.19, f32[3,128]{1,0:T(4,128)} %get-tuple-element.12, f32[3,128]{1,0:T(4,128)S(1)} %collective-permute-done.18), kind=kLoop, calls=%fused_computation.10 | loop fusion | flops 768 | bytes 6144 | tf_op jit(solution)/shard_map/add | solution.py:253
  (55 shorter events, 5.8 us)
Async XLA Ops:
  3.7 28.3 %copy-start.2 = (f32[2,104,128]{2,1,0:T(8,128)S(1)}, f32[2,104,128]{2,1,0:T(8,128)}, u32[]{:S(2)}) copy-start(f32[2,104,128]{2,1,0:T(8,128)} %pack_weight.1) | copy-start | bytes 319492
  3.7 28.3 %collective-permute-start.9 = (f32[2,104,128]{2,1,0:T(8,128)}, f32[2,104,128]{2,1,0:T(8,128)S(1)}, u32[]{:S(2)}, u32[]{:S(2)}) collective-permute-start(f32[2,104,128]{2,1,0:T(8,128)} %pack_weight.1), channel_id=1, source_target_pairs={{0,0},{64,1},{128,2},{192,3},{4,4},{68,5},{132,6},{196,7},{8,8},{7... | collective-permute-start | bytes 319496 | tf_op jit(solution)/shard_map/ppermute | solution.py:28
  13.2 19.3 %collective-permute-start.10 = (f32[2,104,128]{2,1,0:T(8,128)}, f32[2,104,128]{2,1,0:T(8,128)S(1)}, u32[]{:S(2)}, u32[]{:S(2)}) collective-permute-start(f32[2,104,128]{2,1,0:T(8,128)} %pack_weight.1), channel_id=1, source_target_pairs={{16,0},{80,1},{144,2},{208,3},{20,4},{84,5},{148,6},{212,7},{24,8}... | collective-permute-start | bytes 319496 | tf_op jit(solution)/shard_map/ppermute | solution.py:28
  13.3 29.7 %collective-permute-start.7 = (f32[2,100,768]{2,0,1:T(2,128)}, f32[2,100,768]{2,0,1:T(2,128)S(1)}, u32[]{:S(2)}, u32[]{:S(2)}) collective-permute-start(f32[2,100,768]{2,0,1:T(2,128)} %param.5), channel_id=1, source_target_pairs={{2,0},{3,1},{0,2},{1,3},{6,4},{7,5},{4,6},{5,7},{10,8},{11,9},{8,1... | collective-permute-start | bytes 1843208 | tf_op jit(solution)/shard_map/ppermute | solution.py:28
  14.3 33.9 %collective-permute-start.6 = (f32[2,100,768]{2,0,1:T(2,128)}, f32[2,100,768]{2,0,1:T(2,128)S(1)}, u32[]{:S(2)}, u32[]{:S(2)}) collective-permute-start(f32[2,100,768]{2,0,1:T(2,128)} %param.5), channel_id=1, source_target_pairs={{1,0},{0,1},{3,2},{2,3},{5,4},{4,5},{7,6},{6,7},{9,8},{8,9},{11,10... | collective-permute-start | bytes 1843208 | tf_op jit(solution)/shard_map/ppermute | solution.py:28
  14.3 21.1 %collective-permute-start = (f32[2,104,128]{2,1,0:T(8,128)}, f32[2,104,128]{2,1,0:T(8,128)S(1)}, u32[]{:S(2)}, u32[]{:S(2)}) collective-permute-start(f32[2,104,128]{2,1,0:T(8,128)} %pack_weight.1), channel_id=1, source_target_pairs={{32,0},{96,1},{160,2},{224,3},{36,4},{100,5},{164,6},{228,7},{40,8... | collective-permute-start | bytes 319496 | tf_op jit(solution)/shard_map/ppermute | solution.py:28
  32.0 5.6 %collective-permute-start.1 = (f32[2,104,128]{2,1,0:T(8,128)S(1)}, f32[2,104,128]{2,1,0:T(8,128)S(1)}, u32[]{:S(2)}, u32[]{:S(2)}) collective-permute-start(f32[2,104,128]{2,1,0:T(8,128)S(1)} %copy-done.2), channel_id=1, source_target_pairs={{48,0},{112,1},{176,2},{240,3},{52,4},{116,5},{180,6},{244,7},{56,... | collective-permute-start | bytes 319496 | tf_op jit(solution)/shard_map/ppermute | solution.py:28
  32.5 7.7 %collective-permute-start.11 = (f32[2,2,104,128]{3,2,1,0:T(8,128)S(1)}, f32[2,2,104,128]{3,2,1,0:T(8,128)S(1)}, u32[]{:S(2)}, u32[]{:S(2)}) collective-permute-start(f32[2,2,104,128]{3,2,1,0:T(8,128)S(1)} %pad_maximum_fusion.1), channel_id=1, source_target_pairs={{4,0},{5,1},{6,2},{7,3},{8,4},{9,5},{10,6},{11,7},{12,8},{13,9},{1... | collective-permute-start | bytes 638984 | tf_op jit(solution)/shard_map/ppermute | solution.py:28
  35.4 19.1 %copy-start.1 = (s32[2]{0:T(128)}, s32[2]{0:T(128)S(1)}, u32[]{:S(2)}) copy-start(s32[2]{0:T(128)S(1)} %pad_add_fusion.index_ref) | copy-start | bytes 28
  35.4 6.4 %collective-permute-start.12 = (f32[2,2,104,128]{3,2,1,0:T(8,128)S(1)}, f32[2,2,104,128]{3,2,1,0:T(8,128)S(1)}, u32[]{:S(2)}, u32[]{:S(2)}) collective-permute-start(f32[2,2,104,128]{3,2,1,0:T(8,128)S(1)} %pad_maximum_fusion.1), channel_id=1, source_target_pairs={{12,0},{13,1},{14,2},{15,3},{0,4},{1,5},{2,6},{3,7},{4,8},{5,9},{6... | collective-permute-start | bytes 638984 | tf_op jit(solution)/shard_map/ppermute | solution.py:28
  37.7 7.0 %collective-permute-start.2 = (f32[2,2,104,128]{3,2,1,0:T(8,128)S(1)}, f32[2,2,104,128]{3,2,1,0:T(8,128)S(1)}, u32[]{:S(2)}, u32[]{:S(2)}) collective-permute-start(f32[2,2,104,128]{3,2,1,0:T(8,128)S(1)} %pad_maximum_fusion), channel_id=1, source_target_pairs={{4,0},{5,1},{6,2},{7,3},{8,4},{9,5},{10,6},{11,7},{12,8},{13,9},{1... | collective-permute-start | bytes 638984 | tf_op jit(solution)/shard_map/ppermute | solution.py:28
  40.2 6.7 %collective-permute-start.3 = (f32[2,2,104,128]{3,2,1,0:T(8,128)S(1)}, f32[2,2,104,128]{3,2,1,0:T(8,128)S(1)}, u32[]{:S(2)}, u32[]{:S(2)}) collective-permute-start(f32[2,2,104,128]{3,2,1,0:T(8,128)S(1)} %pad_maximum_fusion), channel_id=1, source_target_pairs={{12,0},{13,1},{14,2},{15,3},{0,4},{1,5},{2,6},{3,7},{4,8},{5,9},{6... | collective-permute-start | bytes 638984 | tf_op jit(solution)/shard_map/ppermute | solution.py:28
  41.8 7.0 %collective-permute-start.13 = (f32[2,104,128]{2,1,0:T(8,128)S(1)}, f32[2,104,128]{2,1,0:T(8,128)S(1)}, u32[]{:S(2)}, u32[]{:S(2)}) collective-permute-start(f32[2,104,128]{2,1,0:T(8,128)S(1)} %slice_bitcast_fusion.1), channel_id=1, source_target_pairs={{4,0},{5,1},{6,2},{7,3},{8,4},{9,5},{10,6},{11,7},{12,8},{13,9},{1... | collective-permute-start | bytes 319496 | tf_op jit(solution)/shard_map/ppermute | solution.py:28
  43.0 5.7 %collective-permute-start.8 = (f32[2,100,768]{2,0,1:T(2,128)S(1)}, f32[2,100,768]{2,0,1:T(2,128)S(1)}, u32[]{:S(2)}, u32[]{:S(2)}) collective-permute-start(f32[2,100,768]{2,0,1:T(2,128)S(1)} %collective-permute-done.7), channel_id=1, source_target_pairs={{1,0},{0,1},{3,2},{2,3},{5,4},{4,5},{7,6},{6,7},{9,8},{8,9},{11,10... | collective-permute-start | bytes 1843208 | tf_op jit(solution)/shard_map/ppermute | solution.py:28
  44.6 5.5 %collective-permute-start.14 = (f32[2,104,128]{2,1,0:T(8,128)S(1)}, f32[2,104,128]{2,1,0:T(8,128)S(1)}, u32[]{:S(2)}, u32[]{:S(2)}) collective-permute-start(f32[2,104,128]{2,1,0:T(8,128)S(1)} %slice_bitcast_fusion), channel_id=1, source_target_pairs={{12,0},{13,1},{14,2},{15,3},{0,4},{1,5},{2,6},{3,7},{4,8},{5,9},{6... | collective-permute-start | bytes 319496 | tf_op jit(solution)/shard_map/ppermute | solution.py:28
  46.9 7.6 %collective-permute-start.4 = (f32[2,104,128]{2,1,0:T(8,128)S(1)}, f32[2,104,128]{2,1,0:T(8,128)S(1)}, u32[]{:S(2)}, u32[]{:S(2)}) collective-permute-start(f32[2,104,128]{2,1,0:T(8,128)S(1)} %slice_bitcast_fusion.3), channel_id=1, source_target_pairs={{4,0},{5,1},{6,2},{7,3},{8,4},{9,5},{10,6},{11,7},{12,8},{13,9},{1... | collective-permute-start | bytes 319496 | tf_op jit(solution)/shard_map/ppermute | solution.py:28
  48.2 6.3 %collective-permute-start.5 = (f32[2,104,128]{2,1,0:T(8,128)S(1)}, f32[2,104,128]{2,1,0:T(8,128)S(1)}, u32[]{:S(2)}, u32[]{:S(2)}) collective-permute-start(f32[2,104,128]{2,1,0:T(8,128)S(1)} %slice_bitcast_fusion.2), channel_id=1, source_target_pairs={{12,0},{13,1},{14,2},{15,3},{0,4},{1,5},{2,6},{3,7},{4,8},{5,9},{6... | collective-permute-start | bytes 319496 | tf_op jit(solution)/shard_map/ppermute | solution.py:28
  54.4 7.7 %copy-start.3 = (s32[768,4]{0,1:T(4,128)S(1)}, s32[768,4]{0,1:T(4,128)}, u32[]{:S(2)}) copy-start(s32[768,4]{0,1:T(4,128)} %param.8) | copy-start | bytes 36868
  54.4 8.6 %copy-start.4 = (s32[768]{0:T(1024)S(1)}, s32[768]{0:T(1024)}, u32[]{:S(2)}) copy-start(s32[768]{0:T(1024)} %param.9) | copy-start | bytes 9220
  58.9 7.2 %collective-permute-start.15 = (f32[1,768]{1,0:T(1,128)S(1)}, f32[1,768]{1,0:T(1,128)S(1)}, u32[]{:S(2)}, u32[]{:S(2)}) collective-permute-start(f32[1,768]{1,0:T(1,128)S(1)} %product.3.e0), channel_id=1, source_target_pairs={{1,0},{0,1},{3,2},{2,3},{5,4},{4,5},{7,6},{6,7},{9,8},{8,9},{11,10... | collective-permute-start | bytes 9224 | tf_op jit(solution)/shard_map/ppermute | solution.py:28
  59.1 7.0 %collective-permute-start.16 = (f32[1,768]{1,0:T(1,128)S(1)}, f32[1,768]{1,0:T(1,128)S(1)}, u32[]{:S(2)}, u32[]{:S(2)}) collective-permute-start(f32[1,768]{1,0:T(1,128)S(1)} %product.3.e0), channel_id=1, source_target_pairs={{2,0},{3,1},{0,2},{1,3},{6,4},{7,5},{4,6},{5,7},{10,8},{11,9},{8,1... | collective-permute-start | bytes 9224 | tf_op jit(solution)/shard_map/ppermute | solution.py:28
  62.0 4.1 %collective-permute-start.17 = (f32[1,768]{1,0:T(1,128)S(1)}, f32[1,768]{1,0:T(1,128)S(1)}, u32[]{:S(2)}, u32[]{:S(2)}) collective-permute-start(f32[1,768]{1,0:T(1,128)S(1)} %product.3.e0), channel_id=1, source_target_pairs={{3,0},{2,1},{1,2},{0,3},{7,4},{6,5},{5,6},{4,7},{11,8},{10,9},{9,1... | collective-permute-start | bytes 9224 | tf_op jit(solution)/shard_map/ppermute | solution.py:28
  68.7 10.2 %collective-permute-start.18 = (f32[3,128]{1,0:T(4,128)}, f32[3,128]{1,0:T(4,128)S(1)}, u32[]{:S(2)}, u32[]{:S(2)}) collective-permute-start(f32[3,128]{1,0:T(4,128)} %get-tuple-element.13), channel_id=1, source_target_pairs={{4,0},{5,1},{6,2},{7,3},{8,4},{9,5},{10,6},{11,7},{12,8},{13,9},{1... | collective-permute-start | bytes 4616 | tf_op jit(solution)/shard_map/ppermute | solution.py:201
  77.0 10.3 %collective-permute-start.19 = (f32[3,128]{1,0:T(4,128)}, f32[3,128]{1,0:T(4,128)S(1)}, u32[]{:S(2)}, u32[]{:S(2)}) collective-permute-start(f32[3,128]{1,0:T(4,128)} %get-tuple-element.14), channel_id=1, source_target_pairs={{0,4},{1,5},{2,6},{3,7},{4,8},{5,9},{6,10},{7,11},{8,12},{9,13},{1... | collective-permute-start | bytes 4616 | tf_op jit(solution)/shard_map/ppermute | solution.py:201
  (4 other events, 9.0 us)

commit v2 on v1

--- a/solution.py
+++ b/solution.py
@@ -30,7 +30,8 @@
 
 def pack_kernel(w_ref, o_ref):
     for part in range(2):
-        pieces = [w_ref[part, 100 * g : 100 * (g + 1), :] for g in range(4)]
+        value = w_ref[part].T
+        pieces = [value[100 * g : 100 * (g + 1), :] for g in range(4)]
         o_ref[part, 0:100, :] = jnp.concatenate(pieces, axis=1)
         o_ref[part, 100:ROWS, :] = jnp.zeros((ROWS - 100, 128), jnp.float32)
 
@@ -40,7 +41,7 @@
         pack_kernel,
         out_shape=jax.ShapeDtypeStruct((2, ROWS, 128), jnp.float32),
         name="pack_weight",
-    )(misfit_weight)
+    )(misfit_weight.transpose(0, 2, 1))
 
 
 def split(value):
@@ -50,11 +51,13 @@
 
 
 def prepare_kernel(place_ref, rx_ref, o_ref):
-    real, imag = rx_ref[0], rx_ref[1]
-    for n, value in enumerate((real, imag - real, real + imag)):
-        high, low = split(value)
-        o_ref[0, n, 0] = low
-        o_ref[0, n, 1] = high
+    for s in range(4):
+        row = pl.multiple_of(place_ref[4 + s] * 32, 32)
+        real, imag = rx_ref[0, pl.ds(row, 32), :], rx_ref[1, pl.ds(row, 32), :]
+        for n, value in enumerate((real, imag - real, real + imag)):
+            high, low = split(value)
+            o_ref[0, n, 0, 32 * s : 32 * (s + 1), :] = low
+            o_ref[0, n, 1, 32 * s : 32 * (s + 1), :] = high
 
 
 def prepare_fields(places, rx_field):
@@ -63,11 +66,12 @@
         prepare_kernel,
         grid_spec=pltpu.PrefetchScalarGridSpec(
             num_scalar_prefetch=1,
-            grid=(16,),
-            in_specs=[pl.BlockSpec((2, 32, edges), lambda i, place: (0, place[i], 0))],
-            out_specs=pl.BlockSpec((1, 3, 2, 32, edges), lambda i, place: (i // 8, 0, 0, i % 8, 0)),
+            grid=(4,),
+            in_specs=[pl.BlockSpec((2, 128, edges), lambda i, place: (0, place[i], 0))],
+            out_specs=pl.BlockSpec((1, 3, 2, 128, edges), lambda i, place: (i // 2, 0, 0, i % 2, 0)),
         ),
         out_shape=jax.ShapeDtypeStruct((2, 3, 2, 256, edges), jnp.bfloat16),
+        compiler_params=pltpu.CompilerParams(vmem_limit_bytes=VMEM_LIMIT),
         cost_estimate=pl.CostEstimate(flops=10_000_000, bytes_accessed=8_000_000, transcendentals=0),
         name="prepare_fields",
     )(places, rx_field)
@@ -143,15 +147,22 @@
     )(index, *blocks, *txs, fields, before)
 
 
-def onehot_kernel(index_ref, cells_ref, cells_t_ref, component_ref, hot_ref, row_ref):
-    base, tx_index = index_ref[1], index_ref[0]
-    lanes = lax.broadcasted_iota(jnp.int32, (cells_ref.shape[0], 128), 1)
+def onehot_kernel(index_ref, cells_ref, component_ref, hot_ref, row_ref):
+    x_lo, core, base = index_ref[1], index_ref[2], index_ref[3]
+    cells = cells_ref[...] - base
+    edges = cells.shape[1]
+    lanes = lax.broadcasted_iota(jnp.int32, (128, edges), 0)
     for j in range(4):
-        lane = jnp.bitwise_and(cells_ref[:, j : j + 1], 127)
-        hot_ref[j] = jnp.where(lanes == lane, 1.0, 0.0).astype(jnp.bfloat16)
-    block = (cells_t_ref[...] - base) >> 7
-    row = component_ref[...] * 3 + (block >> 2)
-    row_ref[...] = jnp.where(jnp.bitwise_and(block, 3) == tx_index, row, -1)
+        hit = lanes == jnp.bitwise_and(cells[j : j + 1, :], 127)
+        hot_ref[j] = jnp.where(hit, 1.0, 0.0).astype(jnp.bfloat16)
+    block = cells >> 7
+    row = component_ref[...] * 3
+    other = 8 * core + 2 * x_lo
+    row_ref[...] = jnp.where(
+        block == 4 + 2 * x_lo + core,
+        row,
+        jnp.where(block == other + core, row + 1, jnp.where(block == other + 1 - core, row + 2, -1)),
+    )
 
 
 def onehots(index, incidence, component):
@@ -159,16 +170,16 @@
     whole = pl.BlockSpec(memory_space=pltpu.VMEM)
     return pl.pallas_call(
         onehot_kernel,
-        in_specs=[pl.BlockSpec(memory_space=pltpu.SMEM), whole, whole, whole],
+        in_specs=[pl.BlockSpec(memory_space=pltpu.SMEM), whole, whole],
         out_shape=(
-            jax.ShapeDtypeStruct((4, edges, 128), jnp.bfloat16),
+            jax.ShapeDtypeStruct((4, 128, edges), jnp.bfloat16),
             jax.ShapeDtypeStruct((4, edges), jnp.int32),
         ),
         name="onehots",
-    )(index, incidence, incidence.T, component[None, :])
-
-
-def scatter_kernel(e0, e1, e2, e3, hot_ref, row_ref, low_ref, mid_ref, high_ref):
+    )(index, incidence.T, component[None, :])
+
+
+def scatter_kernel(e0, e1, e2, e3, hot_ref, row_ref, own_ref, send_ref):
     total = 0.25 * ((e0[...] + e1[...]) + (e2[...] + e3[...]))
     edges = total.shape[1]
     rows = lax.broadcasted_iota(jnp.int32, (16, edges), 0)
@@ -180,24 +191,31 @@
     for j in range(4):
         hit = rows == row_ref[j : j + 1, :]
         left = jnp.concatenate([jnp.where(hit, v, 0.0) for v in (first, second, third)], axis=0)
-        summed += jnp.dot(left.astype(jnp.bfloat16), hot_ref[j], preferred_element_type=jnp.float32)
+        summed += lax.dot_general(
+            left.astype(jnp.bfloat16), hot_ref[j], (((1,), (1,)), ((), ())), preferred_element_type=jnp.float32
+        )
     cells = (summed[0:16] + summed[16:32]) + summed[32:48]
     for k in range(3):
-        low_ref[k : k + 1, :] = cells[3 * k : 3 * k + 1, :]
-        mid_ref[k : k + 1, :] = cells[3 * k + 1 : 3 * k + 2, :]
-        high_ref[k : k + 1, :] = cells[3 * k + 2 : 3 * k + 3, :]
+        own_ref[k : k + 1, :] = cells[3 * k : 3 * k + 1, :]
+        send_ref[0, k : k + 1, :] = cells[3 * k + 1 : 3 * k + 2, :]
+        send_ref[1, k : k + 1, :] = cells[3 * k + 2 : 3 * k + 3, :]
 
 
 def scatter(terms, hot, row):
     return pl.pallas_call(
         scatter_kernel,
-        out_shape=[jax.ShapeDtypeStruct((3, 128), jnp.float32)] * 3,
+        out_shape=(jax.ShapeDtypeStruct((3, 128), jnp.float32), jax.ShapeDtypeStruct((2, 3, 128), jnp.float32)),
         name="scatter_cells",
     )(*terms, hot, row)
 
 
-def passed_along(block, distance):
-    route = [((i - distance) * 4 + j, i * 4 + j) for i in range(64) for j in range(4) if 0 <= i - distance < 64]
+def neighbour_parts(block):
+    route = []
+    for m in range(64):
+        for j in range(4):
+            source = m + 1 if j % 2 == 0 else m - 1
+            if 0 <= source < 64:
+                route.append((source * 4 + j, m * 4 + j))
     return lax.ppermute(block, AXES, route)
 
 
@@ -232,10 +250,10 @@
     tx_xc = fetch(tx_x, flip_core)
     txs = [tx_field, tx_c, tx_x, tx_xc]
 
-    steps = jnp.arange(16, dtype=jnp.int32)
-    places = ((z + steps // 4) % 4) * 4 + (y + steps % 4) % 4
-    fields = prepare_fields(places.astype(jnp.int32), rx_field)
-    index = jnp.stack([tx_index, (mesh_index - 1) * CELL_TILE]).astype(jnp.int32)
+    steps = jnp.arange(4, dtype=jnp.int32)
+    places = jnp.concatenate([(z + steps) % 4, (y + steps) % 4]).astype(jnp.int32)
+    fields = prepare_fields(places, rx_field)
+    index = jnp.stack([tx_index, tx_index // 2, tx_index % 2, (mesh_index - 1) * CELL_TILE]).astype(jnp.int32)
     hot, row = onehots(index, incidence, component)
 
     edge = jnp.zeros((1, tx_field.shape[2]), jnp.float32)
@@ -249,8 +267,9 @@
         blocks = [own[0], own[1], above, below, far0, far1]
         edge = product(index, blocks, txs, fields, group, edge)
     terms = [edge, fetch(edge, flip_core), fetch(edge, flip_x), fetch(edge, flip_both)]
-    low, mid, high = scatter(terms, hot, row)
-    return mid + passed_along(low, -1) + passed_along(high, 1)
+    own, send = scatter(terms, hot, row)
+    received = neighbour_parts(send)
+    return own + received[0] + fetch(received[1], flip_core)
 
 
 def solution(mesh):

time: 90.1 us -> 73.3 us (0.81)
  starting transfers between devices: 38.2 us -> 29.5 us
  Pallas kernels: 26 us -> 18.1 us
  waiting for transfers between devices: 16.9 us -> 18.7 us
  local copies, waits for them, and re-layouts: 5.29 us -> 4.36 us
    ppermute x2 -> x1, starting transfers between devices: 10.2 us -> 1.91 us  [neighbour_parts(): return lax.ppermute(block, AXES, route)]
    pallas_call x1, Pallas kernels: 11 us -> 3.63 us  [prepare_fields(): pl.pallas_call(prepare_kernel, grid_spec=pltpu.PrefetchScalarGridSpec(num...]
    ppermute x18 -> x19, waiting for transfers between devices: 8.6 us -> 10.4 us  [fetch(): return lax.ppermute(block, AXES, route)]
    unnamed x19 -> x17, local copies, waits for them, and re-layouts: 4.52 us -> 3.59 us
    ppermute x18 -> x19, starting transfers between devices: 28 us -> 27.6 us  [fetch(): return lax.ppermute(block, AXES, route)]
    ppermute x2 -> x1, waiting for transfers between devices: 8.33 us -> 8.36 us  [neighbour_parts(): return lax.ppermute(block, AXES, route)]
  transfers between devices with their start and end apart: 20 -> 20, of which waited for: 6 -> 8; matrix products, arithmetic and copies ran while one was open for 4% -> 3% of each run, Pallas kernels for 20% -> 13%
where the time goes in v2:
time: 73.3 us; the launch traced here: 72.4 us
  starting transfers between devices  29.5 us (40%)
  waiting for transfers between devices  18.7 us (26%)
  Pallas kernels  18.1 us (25%)
  local copies, waits for them, and re-layouts  4.36 us (6%)
  other arithmetic  1.46 us (2%)
    ppermute x19, starting transfers between devices, fetch(): return lax.ppermute(block, AXES, route)  27.6 us
    ppermute x19, waiting for transfers between devices, fetch(): return lax.ppermute(block, AXES, route)  10.4 us
    pallas_call x2, Pallas kernels, product(): pl.pallas_call(product_kernel, grid_spec=pltpu.PrefetchScalarGridSpec(num...  8.71 us
    ppermute x1, waiting for transfers between devices, neighbour_parts(): return lax.ppermute(block, AXES, route)  8.36 us
    pallas_call x1, Pallas kernels, prepare_fields(): pl.pallas_call(prepare_kernel, grid_spec=pltpu.PrefetchScalarGridSpec(num...  3.63 us
    unnamed x17, local copies, waits for them, and re-layouts  3.59 us
    pallas_call x1, Pallas kernels, scatter(): pl.pallas_call(scatter_kernel, out_shape=(jax.ShapeDtypeStruct((3, 128),...  2.1 us
    ppermute x1, starting transfers between devices, neighbour_parts(): return lax.ppermute(block, AXES, route)  1.91 us
  transfers between devices with their start and end apart: 20, of which 8 were waited for; matrix products, arithmetic and copies ran while one was open for 3% of the time, Pallas kernels for 13%

profile of v2, /device:TPU:7, one launch (start us, length us, event | category | flops | bytes accessed | tf_op | source)
XLA Modules:
  0.0 72.4 jit_solution(4316722787695536929)
XLA Ops:
  0.0 1.9 %pack_weight.1 = f32[2,104,128]{2,1,0:T(8,128)} custom-call(f32[2,32,400]{2,1,0:T(8,128)} %bitcast.30), custom_call_target="tpu_custom_call" | custom-call | tf_op jit(solution)/shard_map/pack_weight/pallas_call | solution.py:40
  1.9 6.1 %collective-permute-start.10 = (f32[2,104,128]{2,1,0:T(8,128)}, f32[2,104,128]{2,1,0:T(8,128)S(1)}, u32[]{:S(2)}, u32[]{:S(2)}) collective-permute-start(f32[2,104,128]{2,1,0:T(8,128)} %pack_weight.1), channel_id=1, source_target_pairs={{16,0},{80,1},{144,2},{208,3},{20,4},{84,5},{148,6},{212,7},{24,8}... | collective-permute-start | bytes 319496 | tf_op jit(solution)/shard_map/ppermute | solution.py:28
  8.0 3.4 %collective-permute-start.9 = (f32[2,104,128]{2,1,0:T(8,128)}, f32[2,104,128]{2,1,0:T(8,128)S(1)}, u32[]{:S(2)}, u32[]{:S(2)}) collective-permute-start(f32[2,104,128]{2,1,0:T(8,128)} %pack_weight.1), channel_id=1, source_target_pairs={{0,0},{64,1},{128,2},{192,3},{4,4},{68,5},{132,6},{196,7},{8,8},{7... | collective-permute-start | bytes 319496 | tf_op jit(solution)/shard_map/ppermute | solution.py:28
  12.3 5.0 %collective-permute-start = (f32[2,104,128]{2,1,0:T(8,128)}, f32[2,104,128]{2,1,0:T(8,128)S(1)}, u32[]{:S(2)}, u32[]{:S(2)}) collective-permute-start(f32[2,104,128]{2,1,0:T(8,128)} %pack_weight.1), channel_id=1, source_target_pairs={{32,0},{96,1},{160,2},{224,3},{36,4},{100,5},{164,6},{228,7},{40,8... | collective-permute-start | bytes 319496 | tf_op jit(solution)/shard_map/ppermute | solution.py:28
  18.6 1.9 %copy-done = f32[2,512,768]{2,1,0:T(8,128)S(1)} copy-done((f32[2,512,768]{2,1,0:T(8,128)S(1)}, f32[2,512,768]{2,1,0:T(8,128)}, u32[]{:S(2)}) %copy-start) | copy-done | bytes 3145752
  20.5 3.6 %prepare_fields.1.field = bf16[2,3,2,256,768]{4,3,2,1,0:T(8,128)(2,1)} custom-call(s32[8]{0:T(128)S(1)} %pad_add_fusion.1.place_ref, f32[2,512,768]{2,1,0:T(8,128)S(1)} %copy-done), custom_call_target="tpu_custom_call" | custom-call | flops 10000000 | bytes 8000000 | tf_op jit(solution)/shard_map/prepare_fields/pallas_call | solution.py:65
  24.6 2.8 %collective-permute-start.11 = (f32[2,2,104,128]{3,2,1,0:T(8,128)S(1)}, f32[2,2,104,128]{3,2,1,0:T(8,128)S(1)}, u32[]{:S(2)}, u32[]{:S(2)}) collective-permute-start(f32[2,2,104,128]{3,2,1,0:T(8,128)S(1)} %pad_maximum_fusion.1), channel_id=1, source_target_pairs={{4,0},{5,1},{6,2},{7,3},{8,4},{9,5},{10,6},{11,7},{12,8},{13,9},{1... | collective-permute-start | bytes 638984 | tf_op jit(solution)/shard_map/ppermute | solution.py:28
  27.6 2.2 %collective-permute-done.1.own1 = f32[2,104,128]{2,1,0:T(8,128)S(1)} collective-permute-done((f32[2,104,128]{2,1,0:T(8,128)S(1)}, f32[2,104,128]{2,1,0:T(8,128)S(1)}, u32[]{:S(2)}, u32[]{:S(2)}) %collective-permute-start.1) | collective-permute-done | bytes 106528 | tf_op jit(solution)/shard_map/ppermute | solution.py:28
  29.8 2.5 %collective-permute-start.2 = (f32[2,2,104,128]{3,2,1,0:T(8,128)S(1)}, f32[2,2,104,128]{3,2,1,0:T(8,128)S(1)}, u32[]{:S(2)}, u32[]{:S(2)}) collective-permute-start(f32[2,2,104,128]{3,2,1,0:T(8,128)S(1)} %pad_maximum_fusion), channel_id=1, source_target_pairs={{4,0},{5,1},{6,2},{7,3},{8,4},{9,5},{10,6},{11,7},{12,8},{13,9},{1... | collective-permute-start | bytes 638984 | tf_op jit(solution)/shard_map/ppermute | solution.py:28
  32.3 1.6 %collective-permute-done.12.below = f32[2,2,104,128]{3,2,1,0:T(8,128)S(1)} collective-permute-done((f32[2,2,104,128]{3,2,1,0:T(8,128)S(1)}, f32[2,2,104,128]{3,2,1,0:T(8,128)S(1)}, u32[]{:S(2)}, u32[]{:S(2)}) %collective-permute-start.12) | collective-permute-done | bytes 213024 | tf_op jit(solution)/shard_map/ppermute | solution.py:28
  34.0 1.1 %collective-permute-start.13 = (f32[2,104,128]{2,1,0:T(8,128)S(1)}, f32[2,104,128]{2,1,0:T(8,128)S(1)}, u32[]{:S(2)}, u32[]{:S(2)}) collective-permute-start(f32[2,104,128]{2,1,0:T(8,128)S(1)} %slice_bitcast_fusion.1), channel_id=1, source_target_pairs={{4,0},{5,1},{6,2},{7,3},{8,4},{9,5},{10,6},{11,7},{12,8},{13,9},{1... | collective-permute-start | bytes 319496 | tf_op jit(solution)/shard_map/ppermute | solution.py:28
  35.1 1.7 %collective-permute-done.2.above = f32[2,2,104,128]{3,2,1,0:T(8,128)S(1)} collective-permute-done((f32[2,2,104,128]{3,2,1,0:T(8,128)S(1)}, f32[2,2,104,128]{3,2,1,0:T(8,128)S(1)}, u32[]{:S(2)}, u32[]{:S(2)}) %collective-permute-start.2) | collective-permute-done | bytes 213024 | tf_op jit(solution)/shard_map/ppermute | solution.py:28
  37.2 1.8 %collective-permute-done.3.below = f32[2,2,104,128]{3,2,1,0:T(8,128)S(1)} collective-permute-done((f32[2,2,104,128]{3,2,1,0:T(8,128)S(1)}, f32[2,2,104,128]{3,2,1,0:T(8,128)S(1)}, u32[]{:S(2)}, u32[]{:S(2)}) %collective-permute-start.3) | collective-permute-done | bytes 213024 | tf_op jit(solution)/shard_map/ppermute | solution.py:28
  39.0 1.2 %collective-permute-start.4 = (f32[2,104,128]{2,1,0:T(8,128)S(1)}, f32[2,104,128]{2,1,0:T(8,128)S(1)}, u32[]{:S(2)}, u32[]{:S(2)}) collective-permute-start(f32[2,104,128]{2,1,0:T(8,128)S(1)} %slice_bitcast_fusion.3), channel_id=1, source_target_pairs={{4,0},{5,1},{6,2},{7,3},{8,4},{9,5},{10,6},{11,7},{12,8},{13,9},{1... | collective-permute-start | bytes 319496 | tf_op jit(solution)/shard_map/ppermute | solution.py:28
  40.9 1.3 %collective-permute-done.14.far1 = f32[2,104,128]{2,1,0:T(8,128)S(1)} collective-permute-done((f32[2,104,128]{2,1,0:T(8,128)S(1)}, f32[2,104,128]{2,1,0:T(8,128)S(1)}, u32[]{:S(2)}, u32[]{:S(2)}) %collective-permute-start.14) | collective-permute-done | bytes 106528 | tf_op jit(solution)/shard_map/ppermute | solution.py:28
  42.2 4.3 %product.2.before = f32[1,768]{1,0:T(1,128)S(1)} custom-call(s32[4]{0:T(128)S(1)} %pad_add_fusion.index_ref, f32[2,104,128]{2,1,0:T(8,128)S(1)} %collective-permute-done.9.own0, f32[2,104,128]{2,1,0:T(8,128)S(1)} %collective-permute-done.10.own1, f32[2,2,104,128]{3,2,1,0:T(8,128)S(1)} %collective-permute-done.11.above, ...), custom_call_target="tpu_custom_call" | custom-call | flops 3000000000 | bytes 6000000 | tf_op jit(solution)/shard_map/product/pallas_call | solution.py:130
  46.6 4.4 %product.3.e0 = f32[1,768]{1,0:T(1,128)S(1)} custom-call(s32[4]{0:T(128)S(1)} %pad_add_fusion.index_ref, f32[2,104,128]{2,1,0:T(8,128)S(1)} %collective-permute-done.own0, f32[2,104,128]{2,1,0:T(8,128)S(1)} %collective-permute-done.1.own1, f32[2,2,104,128]{3,2,1,0:T(8,128)S(1)} %collective-permute-done.2.above, ...), custom_call_target="tpu_custom_call" | custom-call | flops 3000000000 | bytes 6000000 | tf_op jit(solution)/shard_map/product/pallas_call | solution.py:130
  51.2 2.8 %collective-permute-start.16 = (f32[1,768]{1,0:T(1,128)S(1)}, f32[1,768]{1,0:T(1,128)S(1)}, u32[]{:S(2)}, u32[]{:S(2)}) collective-permute-start(f32[1,768]{1,0:T(1,128)S(1)} %product.3.e0), channel_id=1, source_target_pairs={{2,0},{3,1},{0,2},{1,3},{6,4},{7,5},{4,6},{5,7},{10,8},{11,9},{8,1... | collective-permute-start | bytes 9224 | tf_op jit(solution)/shard_map/ppermute | solution.py:28
  54.6 1.8 %onehots.1 = (bf16[4,128,768]{2,1,0:T(8,128)(2,1)}, s32[4,768]{1,0:T(4,128)}) custom-call(s32[4]{0:T(128)} %copy-done.2, s32[4,768]{1,0:T(4,128)} %bitcast.31, s32[1,768]{1,0:T(1,128)} %broadcast_in_dim.7.component_ref), custom_call_target="tpu_custom_call" | custom-call | tf_op jit(solution)/shard_map/onehots/pallas_call | solution.py:171
  57.6 2.1 %scatter_cells.1 = (f32[3,128]{1,0:T(4,128)}, f32[2,3,128]{2,1,0:T(4,128)}) custom-call(f32[1,768]{1,0:T(1,128)} %copy-done.1, f32[1,768]{1,0:T(1,128)} %copy-done.5, f32[1,768]{1,0:T(1,128)} %copy-done.6, f32[1,768]{1,0:T(1,128)} %copy-done.7, bf16[4,128,768]{2,1,0:T(8,128)(2,1)} %get-tuple-element.9.hot_ref, s32[4,768]{1,0:T(4,128)} %get-tuple-element.10.row_ref), custom_call_target="tpu_custom_call" | custom-call | tf_op jit(solution)/shard_map/scatter_cells/pallas_call | solution.py:205
  59.7 1.9 %collective-permute-start.18 = (f32[2,3,128]{2,1,0:T(4,128)}, f32[2,3,128]{2,1,0:T(4,128)S(1)}, u32[]{:S(2)}, u32[]{:S(2)}) collective-permute-start(f32[2,3,128]{2,1,0:T(4,128)} %get-tuple-element.12), channel_id=1, source_target_pairs={{4,0},{6,2},{8,4},{1,5},{10,6},{3,7},{12,8},{5,9},{14,10},{7,11},{... | collective-permute-start | bytes 9224 | tf_op jit(solution)/shard_map/ppermute | solution.py:219
  61.6 8.4 %collective-permute-done.18 = f32[2,3,128]{2,1,0:T(4,128)S(1)} collective-permute-done((f32[2,3,128]{2,1,0:T(4,128)}, f32[2,3,128]{2,1,0:T(4,128)S(1)}, u32[]{:S(2)}, u32[]{:S(2)}) %collective-permute-start.18) | collective-permute-done | bytes 3104 | tf_op jit(solution)/shard_map/ppermute | solution.py:219
  70.0 1.2 %collective-permute-done.19 = f32[3,128]{1,0:T(4,128)S(1)} collective-permute-done((f32[3,128]{1,0:T(4,128)S(1)}, f32[3,128]{1,0:T(4,128)S(1)}, u32[]{:S(2)}, u32[]{:S(2)}) %collective-permute-start.19) | collective-permute-done | bytes 1568 | tf_op jit(solution)/shard_map/ppermute | solution.py:28
  71.1 1.3 %fusion.1 = f32[3,128]{1,0:T(4,128)} fusion(f32[3,128]{1,0:T(4,128)S(1)} %collective-permute-done.19, f32[3,128]{1,0:T(4,128)} %get-tuple-element.11, f32[2,3,128]{2,1,0:T(4,128)S(1)} %collective-permute-done.18), kind=kLoop, calls=%fused_computation.13 | loop fusion | flops 768 | bytes 6144 | tf_op jit(solution)/shard_map/add | solution.py:272
  (55 shorter events, 5.9 us)
Async XLA Ops:
  1.9 22.3 %copy-start.3 = (f32[2,104,128]{2,1,0:T(8,128)S(1)}, f32[2,104,128]{2,1,0:T(8,128)}, u32[]{:S(2)}) copy-start(f32[2,104,128]{2,1,0:T(8,128)} %pack_weight.1) | copy-start | bytes 319492
  1.9 22.3 %collective-permute-start.10 = (f32[2,104,128]{2,1,0:T(8,128)}, f32[2,104,128]{2,1,0:T(8,128)S(1)}, u32[]{:S(2)}, u32[]{:S(2)}) collective-permute-start(f32[2,104,128]{2,1,0:T(8,128)} %pack_weight.1), channel_id=1, source_target_pairs={{16,0},{80,1},{144,2},{208,3},{20,4},{84,5},{148,6},{212,7},{24,8}... | collective-permute-start | bytes 319496 | tf_op jit(solution)/shard_map/ppermute | solution.py:28
  8.0 16.6 %collective-permute-start.9 = (f32[2,104,128]{2,1,0:T(8,128)}, f32[2,104,128]{2,1,0:T(8,128)S(1)}, u32[]{:S(2)}, u32[]{:S(2)}) collective-permute-start(f32[2,104,128]{2,1,0:T(8,128)} %pack_weight.1), channel_id=1, source_target_pairs={{0,0},{64,1},{128,2},{192,3},{4,4},{68,5},{132,6},{196,7},{8,8},{7... | collective-permute-start | bytes 319496 | tf_op jit(solution)/shard_map/ppermute | solution.py:28
  11.4 23.7 %collective-permute-start.7 = (f32[2,100,768]{2,0,1:T(2,128)}, f32[2,100,768]{2,0,1:T(2,128)S(1)}, u32[]{:S(2)}, u32[]{:S(2)}) collective-permute-start(f32[2,100,768]{2,0,1:T(2,128)} %param.5), channel_id=1, source_target_pairs={{2,0},{3,1},{0,2},{1,3},{6,4},{7,5},{4,6},{5,7},{10,8},{11,9},{8,1... | collective-permute-start | bytes 1843208 | tf_op jit(solution)/shard_map/ppermute | solution.py:28
  12.3 28.0 %collective-permute-start.6 = (f32[2,100,768]{2,0,1:T(2,128)}, f32[2,100,768]{2,0,1:T(2,128)S(1)}, u32[]{:S(2)}, u32[]{:S(2)}) collective-permute-start(f32[2,100,768]{2,0,1:T(2,128)} %param.5), channel_id=1, source_target_pairs={{1,0},{0,1},{3,2},{2,3},{5,4},{4,5},{7,6},{6,7},{9,8},{8,9},{11,10... | collective-permute-start | bytes 1843208 | tf_op jit(solution)/shard_map/ppermute | solution.py:28
  12.3 15.2 %collective-permute-start = (f32[2,104,128]{2,1,0:T(8,128)}, f32[2,104,128]{2,1,0:T(8,128)S(1)}, u32[]{:S(2)}, u32[]{:S(2)}) collective-permute-start(f32[2,104,128]{2,1,0:T(8,128)} %pack_weight.1), channel_id=1, source_target_pairs={{32,0},{96,1},{160,2},{224,3},{36,4},{100,5},{164,6},{228,7},{40,8... | collective-permute-start | bytes 319496 | tf_op jit(solution)/shard_map/ppermute | solution.py:28
  24.1 5.6 %collective-permute-start.1 = (f32[2,104,128]{2,1,0:T(8,128)S(1)}, f32[2,104,128]{2,1,0:T(8,128)S(1)}, u32[]{:S(2)}, u32[]{:S(2)}) collective-permute-start(f32[2,104,128]{2,1,0:T(8,128)S(1)} %copy-done.3), channel_id=1, source_target_pairs={{48,0},{112,1},{176,2},{240,3},{52,4},{116,5},{180,6},{244,7},{56,... | collective-permute-start | bytes 319496 | tf_op jit(solution)/shard_map/ppermute | solution.py:28
  24.6 7.7 %collective-permute-start.11 = (f32[2,2,104,128]{3,2,1,0:T(8,128)S(1)}, f32[2,2,104,128]{3,2,1,0:T(8,128)S(1)}, u32[]{:S(2)}, u32[]{:S(2)}) collective-permute-start(f32[2,2,104,128]{3,2,1,0:T(8,128)S(1)} %pad_maximum_fusion.1), channel_id=1, source_target_pairs={{4,0},{5,1},{6,2},{7,3},{8,4},{9,5},{10,6},{11,7},{12,8},{13,9},{1... | collective-permute-start | bytes 638984 | tf_op jit(solution)/shard_map/ppermute | solution.py:28
  27.5 19.1 %copy-start.2 = (s32[4]{0:T(128)}, s32[4]{0:T(128)S(1)}, u32[]{:S(2)}) copy-start(s32[4]{0:T(128)S(1)} %pad_add_fusion.index_ref) | copy-start | bytes 52
  27.5 6.5 %collective-permute-start.12 = (f32[2,2,104,128]{3,2,1,0:T(8,128)S(1)}, f32[2,2,104,128]{3,2,1,0:T(8,128)S(1)}, u32[]{:S(2)}, u32[]{:S(2)}) collective-permute-start(f32[2,2,104,128]{3,2,1,0:T(8,128)S(1)} %pad_maximum_fusion.1), channel_id=1, source_target_pairs={{12,0},{13,1},{14,2},{15,3},{0,4},{1,5},{2,6},{3,7},{4,8},{5,9},{6... | collective-permute-start | bytes 638984 | tf_op jit(solution)/shard_map/ppermute | solution.py:28
  29.8 7.0 %collective-permute-start.2 = (f32[2,2,104,128]{3,2,1,0:T(8,128)S(1)}, f32[2,2,104,128]{3,2,1,0:T(8,128)S(1)}, u32[]{:S(2)}, u32[]{:S(2)}) collective-permute-start(f32[2,2,104,128]{3,2,1,0:T(8,128)S(1)} %pad_maximum_fusion), channel_id=1, source_target_pairs={{4,0},{5,1},{6,2},{7,3},{8,4},{9,5},{10,6},{11,7},{12,8},{13,9},{1... | collective-permute-start | bytes 638984 | tf_op jit(solution)/shard_map/ppermute | solution.py:28
  32.3 6.7 %collective-permute-start.3 = (f32[2,2,104,128]{3,2,1,0:T(8,128)S(1)}, f32[2,2,104,128]{3,2,1,0:T(8,128)S(1)}, u32[]{:S(2)}, u32[]{:S(2)}) collective-permute-start(f32[2,2,104,128]{3,2,1,0:T(8,128)S(1)} %pad_maximum_fusion), channel_id=1, source_target_pairs={{12,0},{13,1},{14,2},{15,3},{0,4},{1,5},{2,6},{3,7},{4,8},{5,9},{6... | collective-permute-start | bytes 638984 | tf_op jit(solution)/shard_map/ppermute | solution.py:28
  34.0 7.0 %collective-permute-start.13 = (f32[2,104,128]{2,1,0:T(8,128)S(1)}, f32[2,104,128]{2,1,0:T(8,128)S(1)}, u32[]{:S(2)}, u32[]{:S(2)}) collective-permute-start(f32[2,104,128]{2,1,0:T(8,128)S(1)} %slice_bitcast_fusion.1), channel_id=1, source_target_pairs={{4,0},{5,1},{6,2},{7,3},{8,4},{9,5},{10,6},{11,7},{12,8},{13,9},{1... | collective-permute-start | bytes 319496 | tf_op jit(solution)/shard_map/ppermute | solution.py:28
  35.1 5.8 %collective-permute-start.8 = (f32[2,100,768]{2,0,1:T(2,128)S(1)}, f32[2,100,768]{2,0,1:T(2,128)S(1)}, u32[]{:S(2)}, u32[]{:S(2)}) collective-permute-start(f32[2,100,768]{2,0,1:T(2,128)S(1)} %collective-permute-done.7), channel_id=1, source_target_pairs={{1,0},{0,1},{3,2},{2,3},{5,4},{4,5},{7,6},{6,7},{9,8},{8,9},{11,10... | collective-permute-start | bytes 1843208 | tf_op jit(solution)/shard_map/ppermute | solution.py:28
  36.8 5.5 %collective-permute-start.14 = (f32[2,104,128]{2,1,0:T(8,128)S(1)}, f32[2,104,128]{2,1,0:T(8,128)S(1)}, u32[]{:S(2)}, u32[]{:S(2)}) collective-permute-start(f32[2,104,128]{2,1,0:T(8,128)S(1)} %slice_bitcast_fusion), channel_id=1, source_target_pairs={{12,0},{13,1},{14,2},{15,3},{0,4},{1,5},{2,6},{3,7},{4,8},{5,9},{6... | collective-permute-start | bytes 319496 | tf_op jit(solution)/shard_map/ppermute | solution.py:28
  39.0 7.6 %collective-permute-start.4 = (f32[2,104,128]{2,1,0:T(8,128)S(1)}, f32[2,104,128]{2,1,0:T(8,128)S(1)}, u32[]{:S(2)}, u32[]{:S(2)}) collective-permute-start(f32[2,104,128]{2,1,0:T(8,128)S(1)} %slice_bitcast_fusion.3), channel_id=1, source_target_pairs={{4,0},{5,1},{6,2},{7,3},{8,4},{9,5},{10,6},{11,7},{12,8},{13,9},{1... | collective-permute-start | bytes 319496 | tf_op jit(solution)/shard_map/ppermute | solution.py:28
  40.3 6.3 %collective-permute-start.5 = (f32[2,104,128]{2,1,0:T(8,128)S(1)}, f32[2,104,128]{2,1,0:T(8,128)S(1)}, u32[]{:S(2)}, u32[]{:S(2)}) collective-permute-start(f32[2,104,128]{2,1,0:T(8,128)S(1)} %slice_bitcast_fusion.2), channel_id=1, source_target_pairs={{12,0},{13,1},{14,2},{15,3},{0,4},{1,5},{2,6},{3,7},{4,8},{5,9},{6... | collective-permute-start | bytes 319496 | tf_op jit(solution)/shard_map/ppermute | solution.py:28
  46.6 7.4 %copy-start.4 = (s32[768]{0:T(1024)S(1)}, s32[768]{0:T(1024)}, u32[]{:S(2)}) copy-start(s32[768]{0:T(1024)} %param.9) | copy-start | bytes 9220
  51.0 6.0 %copy-start.1 = (f32[1,768]{1,0:T(1,128)}, f32[1,768]{1,0:T(1,128)S(1)}, u32[]{:S(2)}) copy-start(f32[1,768]{1,0:T(1,128)S(1)} %product.3.e0) | copy-start | bytes 9220
  51.0 5.3 %collective-permute-start.15 = (f32[1,768]{1,0:T(1,128)S(1)}, f32[1,768]{1,0:T(1,128)S(1)}, u32[]{:S(2)}, u32[]{:S(2)}) collective-permute-start(f32[1,768]{1,0:T(1,128)S(1)} %product.3.e0), channel_id=1, source_target_pairs={{1,0},{0,1},{3,2},{2,3},{5,4},{4,5},{7,6},{6,7},{9,8},{8,9},{11,10... | collective-permute-start | bytes 9224 | tf_op jit(solution)/shard_map/ppermute | solution.py:28
  51.2 5.2 %collective-permute-start.16 = (f32[1,768]{1,0:T(1,128)S(1)}, f32[1,768]{1,0:T(1,128)S(1)}, u32[]{:S(2)}, u32[]{:S(2)}) collective-permute-start(f32[1,768]{1,0:T(1,128)S(1)} %product.3.e0), channel_id=1, source_target_pairs={{2,0},{3,1},{0,2},{1,3},{6,4},{7,5},{4,6},{5,7},{10,8},{11,9},{8,1... | collective-permute-start | bytes 9224 | tf_op jit(solution)/shard_map/ppermute | solution.py:28
  53.9 3.1 %collective-permute-start.17 = (f32[1,768]{1,0:T(1,128)S(1)}, f32[1,768]{1,0:T(1,128)S(1)}, u32[]{:S(2)}, u32[]{:S(2)}) collective-permute-start(f32[1,768]{1,0:T(1,128)S(1)} %product.3.e0), channel_id=1, source_target_pairs={{3,0},{2,1},{1,2},{0,3},{7,4},{6,5},{5,6},{4,7},{11,8},{10,9},{9,1... | collective-permute-start | bytes 9224 | tf_op jit(solution)/shard_map/ppermute | solution.py:28
  59.7 10.3 %collective-permute-start.18 = (f32[2,3,128]{2,1,0:T(4,128)}, f32[2,3,128]{2,1,0:T(4,128)S(1)}, u32[]{:S(2)}, u32[]{:S(2)}) collective-permute-start(f32[2,3,128]{2,1,0:T(4,128)} %get-tuple-element.12), channel_id=1, source_target_pairs={{4,0},{6,2},{8,4},{1,5},{10,6},{3,7},{12,8},{5,9},{14,10},{7,11},{... | collective-permute-start | bytes 9224 | tf_op jit(solution)/shard_map/ppermute | solution.py:219
  70.0 1.2 %collective-permute-start.19 = (f32[3,128]{1,0:T(4,128)S(1)}, f32[3,128]{1,0:T(4,128)S(1)}, u32[]{:S(2)}, u32[]{:S(2)}) collective-permute-start(f32[3,128]{1,0:T(4,128)S(1)} %slice_bitcast_fusion.4), channel_id=1, source_target_pairs={{1,0},{0,1},{3,2},{2,3},{5,4},{4,5},{7,6},{6,7},{9,8},{8,9},{11,10... | collective-permute-start | bytes 4616 | tf_op jit(solution)/shard_map/ppermute | solution.py:28
  (4 other events, 3.7 us)

commit v3 on v2

--- a/solution.py
+++ b/solution.py
@@ -11,7 +11,13 @@
 AXES = ("mesh", "tx")
 SIZE_Z, SIZE_Y = 8, 4
 ROWS = 104
-VMEM_LIMIT = 48 * 1024 * 1024
+MIB = 1024 * 1024
+WHOLE = pl.BlockSpec(memory_space=pltpu.VMEM)
+SCALARS = pl.BlockSpec(memory_space=pltpu.SMEM)
+
+
+def limit(mib):
+    return pltpu.CompilerParams(vmem_limit_bytes=mib * MIB)
 
 
 def coords(device):
@@ -39,7 +45,10 @@
 def pack_weight(misfit_weight):
     return pl.pallas_call(
         pack_kernel,
+        in_specs=[WHOLE],
+        out_specs=WHOLE,
         out_shape=jax.ShapeDtypeStruct((2, ROWS, 128), jnp.float32),
+        compiler_params=limit(2),
         name="pack_weight",
     )(misfit_weight.transpose(0, 2, 1))
 
@@ -51,38 +60,52 @@
 
 
 def prepare_kernel(place_ref, rx_ref, o_ref):
-    for s in range(4):
-        row = pl.multiple_of(place_ref[4 + s] * 32, 32)
-        real, imag = rx_ref[0, pl.ds(row, 32), :], rx_ref[1, pl.ds(row, 32), :]
-        for n, value in enumerate((real, imag - real, real + imag)):
-            high, low = split(value)
-            o_ref[0, n, 0, 32 * s : 32 * (s + 1), :] = low
-            o_ref[0, n, 1, 32 * s : 32 * (s + 1), :] = high
+    for k in range(4):
+        for s in range(4):
+            row = pl.multiple_of(place_ref[k] * 128 + place_ref[4 + s] * 32, 32)
+            real, imag = rx_ref[0, pl.ds(row, 32), :], rx_ref[1, pl.ds(row, 32), :]
+            rows = slice(128 * (k % 2) + 32 * s, 128 * (k % 2) + 32 * (s + 1))
+            for n, value in enumerate((real, imag - real, real + imag)):
+                high, low = split(value)
+                o_ref[k // 2, n, 0, rows, :] = low
+                o_ref[k // 2, n, 1, rows, :] = high
 
 
 def prepare_fields(places, rx_field):
     edges = rx_field.shape[2]
     return pl.pallas_call(
         prepare_kernel,
-        grid_spec=pltpu.PrefetchScalarGridSpec(
-            num_scalar_prefetch=1,
-            grid=(4,),
-            in_specs=[pl.BlockSpec((2, 128, edges), lambda i, place: (0, place[i], 0))],
-            out_specs=pl.BlockSpec((1, 3, 2, 128, edges), lambda i, place: (i // 2, 0, 0, i % 2, 0)),
-        ),
+        in_specs=[SCALARS, WHOLE],
+        out_specs=WHOLE,
         out_shape=jax.ShapeDtypeStruct((2, 3, 2, 256, edges), jnp.bfloat16),
-        compiler_params=pltpu.CompilerParams(vmem_limit_bytes=VMEM_LIMIT),
+        compiler_params=limit(4),
         cost_estimate=pl.CostEstimate(flops=10_000_000, bytes_accessed=8_000_000, transcendentals=0),
         name="prepare_fields",
     )(places, rx_field)
 
 
+def arrange_kernel(after_ref, tx_ref, o_ref):
+    o_ref[0] = tx_ref[:, 0, :]
+    o_ref[1] = tx_ref[:, 1, :]
+
+
+def arrange(after, tx_field):
+    return pl.pallas_call(
+        arrange_kernel,
+        in_specs=[pl.BlockSpec(memory_space=pl.ANY), WHOLE],
+        out_specs=WHOLE,
+        out_shape=jax.ShapeDtypeStruct(tx_field.shape, jnp.float32),
+        compiler_params=limit(4),
+        name="arrange",
+    )(after, tx_field.transpose(1, 0, 2))
+
+
 def lane_group():
     return lax.broadcasted_iota(jnp.int32, (ROWS, 128), 1) // 32
 
 
 def product_kernel(
-    index_ref, own0, own1, above, below, far0, far1, t0, t1, t2, t3, field, before, o_ref, w_scr, wh_scr, wl_scr
+    group_index, index_ref, own0, own1, above, below, far0, far1, t0, t1, t2, t3, field, before, o_ref, w_scr, wh_scr, wl_scr
 ):
     tx_index = index_ref[0]
     group = lane_group()
@@ -109,8 +132,8 @@
         cols = slice(256 * tile, 256 * (tile + 1))
         products = []
         for n in range(3):
-            both = field[0, n, :, :, cols].reshape(512, 256)
-            high = field[0, n, 1, :, cols]
+            both = field[group_index, n, :, :, cols].reshape(512, 256)
+            high = field[group_index, n, 1, :, cols]
             products.append(
                 jnp.dot(wh_scr[n], both, preferred_element_type=jnp.float32)
                 + jnp.dot(wl_scr[n], high, preferred_element_type=jnp.float32)
@@ -126,22 +149,17 @@
 
 def product(index, blocks, txs, fields, group, before):
     edges = fields.shape[4]
-    whole = pl.BlockSpec(memory_space=pltpu.VMEM)
-    return pl.pallas_call(
-        product_kernel,
-        grid_spec=pltpu.PrefetchScalarGridSpec(
-            num_scalar_prefetch=1,
-            grid=(1,),
-            in_specs=[whole] * 10 + [pl.BlockSpec((1, 3, 2, 256, edges), lambda i, s: (group, 0, 0, 0, 0)), whole],
-            out_specs=whole,
-            scratch_shapes=[
-                pltpu.VMEM((2, 4 * ROWS, 256), jnp.float32),
-                pltpu.VMEM((3, 4 * ROWS, 512), jnp.bfloat16),
-                pltpu.VMEM((3, 4 * ROWS, 256), jnp.bfloat16),
-            ],
-        ),
+    return pl.pallas_call(
+        functools.partial(product_kernel, group),
+        in_specs=[SCALARS] + [WHOLE] * 12,
+        out_specs=WHOLE,
+        scratch_shapes=[
+            pltpu.VMEM((2, 4 * ROWS, 256), jnp.float32),
+            pltpu.VMEM((3, 4 * ROWS, 512), jnp.bfloat16),
+            pltpu.VMEM((3, 4 * ROWS, 256), jnp.bfloat16),
+        ],
         out_shape=jax.ShapeDtypeStruct((1, edges), jnp.float32),
-        compiler_params=pltpu.CompilerParams(vmem_limit_bytes=VMEM_LIMIT),
+        compiler_params=limit(12),
         cost_estimate=pl.CostEstimate(flops=3_000_000_000, bytes_accessed=6_000_000, transcendentals=0),
         name="product",
     )(index, *blocks, *txs, fields, before)
@@ -167,10 +185,11 @@
 
 def onehots(index, incidence, component):
     edges = incidence.shape[0]
-    whole = pl.BlockSpec(memory_space=pltpu.VMEM)
     return pl.pallas_call(
         onehot_kernel,
-        in_specs=[pl.BlockSpec(memory_space=pltpu.SMEM), whole, whole],
+        in_specs=[SCALARS, WHOLE, WHOLE],
+        out_specs=(WHOLE, WHOLE),
+        compiler_params=limit(2),
         out_shape=(
             jax.ShapeDtypeStruct((4, 128, edges), jnp.bfloat16),
             jax.ShapeDtypeStruct((4, edges), jnp.int32),
@@ -204,9 +223,27 @@
 def scatter(terms, hot, row):
     return pl.pallas_call(
         scatter_kernel,
+        in_specs=[WHOLE] * 6,
+        out_specs=(WHOLE, WHOLE),
+        compiler_params=limit(4),
         out_shape=(jax.ShapeDtypeStruct((3, 128), jnp.float32), jax.ShapeDtypeStruct((2, 3, 128), jnp.float32)),
         name="scatter_cells",
     )(*terms, hot, row)
+
+
+def total_kernel(own_ref, received_ref, passed_ref, o_ref):
+    o_ref[...] = own_ref[...] + received_ref[0] + passed_ref[...]
+
+
+def total(own, received, passed):
+    return pl.pallas_call(
+        total_kernel,
+        in_specs=[WHOLE] * 3,
+        out_specs=WHOLE,
+        compiler_params=limit(2),
+        out_shape=jax.ShapeDtypeStruct(own.shape, jnp.float32),
+        name="total",
+    )(own, received, passed)
 
 
 def neighbour_parts(block):
@@ -246,13 +283,11 @@
     packed = pack_weight(misfit_weight)
     tx_x = fetch(tx_field, flip_x)
     from_z = [fetch(packed, z_source(k)) for k in range(4)]
-    tx_c = fetch(tx_field, flip_core)
-    tx_xc = fetch(tx_x, flip_core)
-    txs = [tx_field, tx_c, tx_x, tx_xc]
-
     steps = jnp.arange(4, dtype=jnp.int32)
     places = jnp.concatenate([(z + steps) % 4, (y + steps) % 4]).astype(jnp.int32)
     fields = prepare_fields(places, rx_field)
+    tx_own = arrange(fields, tx_field)
+    txs = [tx_own, fetch(tx_own, flip_core), tx_x, fetch(tx_x, flip_core)]
     index = jnp.stack([tx_index, tx_index // 2, tx_index % 2, (mesh_index - 1) * CELL_TILE]).astype(jnp.int32)
     hot, row = onehots(index, incidence, component)
 
@@ -269,7 +304,7 @@
     terms = [edge, fetch(edge, flip_core), fetch(edge, flip_x), fetch(edge, flip_both)]
     own, send = scatter(terms, hot, row)
     received = neighbour_parts(send)
-    return own + received[0] + fetch(received[1], flip_core)
+    return total(own, received, fetch(received[1], flip_core))
 
 
 def solution(mesh):

time: 73.3 us -> 67.4 us (0.920)
  Pallas kernels: 18.1 us -> 8.75 us
  starting transfers between devices: 29.5 us -> 36.2 us
  waiting for transfers between devices: 18.7 us -> 15.7 us
  other arithmetic: 1.46 us -> 0.2 us
  local copies, waits for them, and re-layouts: 4.36 us -> 5.44 us
    pallas_call x6 -> x8, Pallas kernels: 18.1 us -> 8.75 us  [the longest x2 5.49 us: product(): pl.pallas_call(functools.partial(product_kernel, group), in_specs=[SCALAR...]
    ppermute x19, starting transfers between devices: 27.6 us -> 34.2 us  [fetch(): return lax.ppermute(block, AXES, route)]
    ppermute x19, waiting for transfers between devices: 10.4 us -> 7.54 us  [fetch(): return lax.ppermute(block, AXES, route)]
    unnamed x17 -> x14, local copies, waits for them, and re-layouts: 3.59 us -> 4.95 us
    add x1 -> x0, other arithmetic: 1.26 us -> none  [shards(): return own + received[0] + fetch(received[1], flip_core)]
  transfers between devices with their start and end apart: 20 -> 20, of which waited for: 8 -> 7; matrix products, arithmetic and copies ran while one was open for 3% -> 1% of each run, Pallas kernels for 13% -> 7%
where the time goes in v3:
time: 67.4 us; the launch traced here: 66.6 us
  starting transfers between devices  36.2 us (54%)
  waiting for transfers between devices  15.7 us (23%)
  Pallas kernels  8.75 us (13%)
  local copies, waits for them, and re-layouts  5.44 us (8%)
    ppermute x19, starting transfers between devices, fetch(): return lax.ppermute(block, AXES, route)  34.2 us
    ppermute x1, waiting for transfers between devices, neighbour_parts(): return lax.ppermute(block, AXES, route)  8.15 us
    ppermute x19, waiting for transfers between devices, fetch(): return lax.ppermute(block, AXES, route)  7.54 us
    pallas_call x2, Pallas kernels, product(): pl.pallas_call(functools.partial(product_kernel, group), in_specs=[SCALAR...  5.49 us
    unnamed x14, local copies, waits for them, and re-layouts  4.95 us
    ppermute x1, starting transfers between devices, neighbour_parts(): return lax.ppermute(block, AXES, route)  1.94 us
  transfers between devices with their start and end apart: 20, of which 7 were waited for; matrix products, arithmetic and copies ran while one was open for 1% of the time, Pallas kernels for 7%

profile of v3, /device:TPU:7, one launch (start us, length us, event | category | flops | bytes accessed | tf_op | source)
XLA Modules:
  0.0 66.6 jit_solution(3796354459881002703)
XLA Ops:
  0.0 0.9 %copy-done.4 = f32[2,400,32]{1,2,0:T(8,128)S(1)} copy-done((f32[2,400,32]{1,2,0:T(8,128)S(1)}, f32[2,400,32]{1,2,0:T(8,128)}, u32[]{:S(2)}) %copy-start.4) | copy-done | bytes 102424
  1.2 9.4 %collective-permute-start.9 = (f32[2,104,128]{2,1,0:T(8,128)S(1)}, f32[2,104,128]{2,1,0:T(8,128)S(1)}, u32[]{:S(2)}, u32[]{:S(2)}) collective-permute-start(f32[2,104,128]{2,1,0:T(8,128)S(1)} %pack_weight.1), channel_id=1, source_target_pairs={{0,0},{64,1},{128,2},{192,3},{4,4},{68,5},{132,6},{196,7},{8,8},{7... | collective-permute-start | bytes 319496 | tf_op jit(solution)/shard_map/ppermute | solution.py:34
  10.7 4.3 %collective-permute-start = (f32[2,104,128]{2,1,0:T(8,128)S(1)}, f32[2,104,128]{2,1,0:T(8,128)S(1)}, u32[]{:S(2)}, u32[]{:S(2)}) collective-permute-start(f32[2,104,128]{2,1,0:T(8,128)S(1)} %pack_weight.1), channel_id=1, source_target_pairs={{32,0},{96,1},{160,2},{224,3},{36,4},{100,5},{164,6},{228,7},{40,8... | collective-permute-start | bytes 319496 | tf_op jit(solution)/shard_map/ppermute | solution.py:34
  15.4 1.4 %collective-permute-start.7 = (f32[2,100,768]{2,0,1:T(2,128)}, f32[2,100,768]{2,0,1:T(2,128)S(1)}, u32[]{:S(2)}, u32[]{:S(2)}) collective-permute-start(f32[2,100,768]{2,0,1:T(2,128)} %param.5), channel_id=1, source_target_pairs={{2,0},{3,1},{0,2},{1,3},{6,4},{7,5},{4,6},{5,7},{10,8},{11,9},{8,1... | collective-permute-start | bytes 1843208 | tf_op jit(solution)/shard_map/ppermute | solution.py:34
  16.9 1.9 %copy-done.2 = f32[2,512,768]{2,1,0:T(8,128)S(1)} copy-done((f32[2,512,768]{2,1,0:T(8,128)S(1)}, f32[2,512,768]{2,1,0:T(8,128)}, u32[]{:S(2)}) %copy-start.2) | copy-done | bytes 3145752
  18.8 1.2 %prepare_fields.1.after_ref.field = bf16[2,3,2,256,768]{4,3,2,1,0:T(8,128)(2,1)S(1)} custom-call(s32[8]{0:T(128)S(1)} %pad_add_fusion.1.place_ref, f32[2,512,768]{2,1,0:T(8,128)S(1)} %copy-done.2), custom_call_target="tpu_custom_call" | custom-call | flops 10000000 | bytes 8000000 | tf_op jit(solution)/shard_map/prepare_fields/pallas_call | solution.py:76
  20.2 2.1 %copy-done = bf16[2,3,2,256,768]{4,3,2,1,0:T(8,128)(2,1)} copy-done((bf16[2,3,2,256,768]{4,3,2,1,0:T(8,128)(2,1)}, bf16[2,3,2,256,768]{4,3,2,1,0:T(8,128)(2,1)S(1)}, u32[]{:S(2)}) %copy-start) | copy-done | bytes 4718616
  22.9 2.8 %collective-permute-start.11 = (f32[2,2,104,128]{3,2,1,0:T(8,128)S(1)}, f32[2,2,104,128]{3,2,1,0:T(8,128)S(1)}, u32[]{:S(2)}, u32[]{:S(2)}) collective-permute-start(f32[2,2,104,128]{3,2,1,0:T(8,128)S(1)} %pad_maximum_fusion.1), channel_id=1, source_target_pairs={{4,0},{5,1},{6,2},{7,3},{8,4},{9,5},{10,6},{11,7},{12,8},{13,9},{1... | collective-permute-start | bytes 638984 | tf_op jit(solution)/shard_map/ppermute | solution.py:34
  25.8 2.7 %collective-permute-start.2 = (f32[2,2,104,128]{3,2,1,0:T(8,128)S(1)}, f32[2,2,104,128]{3,2,1,0:T(8,128)S(1)}, u32[]{:S(2)}, u32[]{:S(2)}) collective-permute-start(f32[2,2,104,128]{3,2,1,0:T(8,128)S(1)} %pad_maximum_fusion), channel_id=1, source_target_pairs={{4,0},{5,1},{6,2},{7,3},{8,4},{9,5},{10,6},{11,7},{12,8},{13,9},{1... | collective-permute-start | bytes 638984 | tf_op jit(solution)/shard_map/ppermute | solution.py:34
  28.6 1.3 %collective-permute-done.11.above = f32[2,2,104,128]{3,2,1,0:T(8,128)S(1)} collective-permute-done((f32[2,2,104,128]{3,2,1,0:T(8,128)S(1)}, f32[2,2,104,128]{3,2,1,0:T(8,128)S(1)}, u32[]{:S(2)}, u32[]{:S(2)}) %collective-permute-start.11) | collective-permute-done | bytes 213024 | tf_op jit(solution)/shard_map/ppermute | solution.py:34
  29.8 0.8 %collective-permute-start.3 = (f32[2,2,104,128]{3,2,1,0:T(8,128)S(1)}, f32[2,2,104,128]{3,2,1,0:T(8,128)S(1)}, u32[]{:S(2)}, u32[]{:S(2)}) collective-permute-start(f32[2,2,104,128]{3,2,1,0:T(8,128)S(1)} %pad_maximum_fusion), channel_id=1, source_target_pairs={{12,0},{13,1},{14,2},{15,3},{0,4},{1,5},{2,6},{3,7},{4,8},{5,9},{6... | collective-permute-start | bytes 638984 | tf_op jit(solution)/shard_map/ppermute | solution.py:34
  30.6 2.4 %collective-permute-done.12.below = f32[2,2,104,128]{3,2,1,0:T(8,128)S(1)} collective-permute-done((f32[2,2,104,128]{3,2,1,0:T(8,128)S(1)}, f32[2,2,104,128]{3,2,1,0:T(8,128)S(1)}, u32[]{:S(2)}, u32[]{:S(2)}) %collective-permute-start.12) | collective-permute-done | bytes 213024 | tf_op jit(solution)/shard_map/ppermute | solution.py:34
  33.4 2.5 %collective-permute-start.8 = (f32[2,100,768]{2,0,1:T(2,128)S(1)}, f32[2,100,768]{2,0,1:T(2,128)S(1)}, u32[]{:S(2)}, u32[]{:S(2)}) collective-permute-start(f32[2,100,768]{2,0,1:T(2,128)S(1)} %collective-permute-done.7), channel_id=1, source_target_pairs={{1,0},{0,1},{3,2},{2,3},{5,4},{4,5},{7,6},{6,7},{9,8},{8,9},{11,10... | collective-permute-start | bytes 1843208 | tf_op jit(solution)/shard_map/ppermute | solution.py:34
  36.5 2.2 %collective-permute-start.4 = (f32[2,104,128]{2,1,0:T(8,128)S(1)}, f32[2,104,128]{2,1,0:T(8,128)S(1)}, u32[]{:S(2)}, u32[]{:S(2)}) collective-permute-start(f32[2,104,128]{2,1,0:T(8,128)S(1)} %slice_bitcast_fusion.3), channel_id=1, source_target_pairs={{4,0},{5,1},{6,2},{7,3},{8,4},{9,5},{10,6},{11,7},{12,8},{13,9},{1... | collective-permute-start | bytes 319496 | tf_op jit(solution)/shard_map/ppermute | solution.py:34
  39.2 1.5 %collective-permute-done.14.far1 = f32[2,104,128]{2,1,0:T(8,128)S(1)} collective-permute-done((f32[2,104,128]{2,1,0:T(8,128)S(1)}, f32[2,104,128]{2,1,0:T(8,128)S(1)}, u32[]{:S(2)}, u32[]{:S(2)}) %collective-permute-start.14) | collective-permute-done | bytes 106528 | tf_op jit(solution)/shard_map/ppermute | solution.py:34
  40.8 2.7 %product.2.before = f32[1,768]{1,0:T(1,128)S(1)} custom-call(s32[4]{0:T(128)S(1)} %pad_add_fusion.index_ref, f32[2,104,128]{2,1,0:T(8,128)S(1)} %collective-permute-done.9.own0, f32[2,104,128]{2,1,0:T(8,128)S(1)} %collective-permute-done.10.own1, f32[2,2,104,128]{3,2,1,0:T(8,128)S(1)} %collective-permute-done.11.above, ...), custom_call_target="tpu_custom_call" | custom-call | flops 3000000000 | bytes 6000000 | tf_op jit(solution)/shard_map/product/pallas_call | solution.py:152
  43.9 2.7 %product.3.e0 = f32[1,768]{1,0:T(1,128)S(1)} custom-call(s32[4]{0:T(128)S(1)} %pad_add_fusion.index_ref, f32[2,104,128]{2,1,0:T(8,128)S(1)} %collective-permute-done.own0, f32[2,104,128]{2,1,0:T(8,128)S(1)} %collective-permute-done.1.own1, f32[2,2,104,128]{3,2,1,0:T(8,128)S(1)} %collective-permute-done.2.above, ...), custom_call_target="tpu_custom_call" | custom-call | flops 3000000000 | bytes 6000000 | tf_op jit(solution)/shard_map/product/pallas_call | solution.py:152
  46.6 4.5 %collective-permute-start.15 = (f32[1,768]{1,0:T(1,128)S(1)}, f32[1,768]{1,0:T(1,128)S(1)}, u32[]{:S(2)}, u32[]{:S(2)}) collective-permute-start(f32[1,768]{1,0:T(1,128)S(1)} %product.3.e0), channel_id=1, source_target_pairs={{1,0},{0,1},{3,2},{2,3},{5,4},{4,5},{7,6},{6,7},{9,8},{8,9},{11,10... | collective-permute-start | bytes 9224 | tf_op jit(solution)/shard_map/ppermute | solution.py:34
  51.1 1.7 %collective-permute-start.17 = (f32[1,768]{1,0:T(1,128)S(1)}, f32[1,768]{1,0:T(1,128)S(1)}, u32[]{:S(2)}, u32[]{:S(2)}) collective-permute-start(f32[1,768]{1,0:T(1,128)S(1)} %product.3.e0), channel_id=1, source_target_pairs={{3,0},{2,1},{1,2},{0,3},{7,4},{6,5},{5,6},{4,7},{11,8},{10,9},{9,1... | collective-permute-start | bytes 9224 | tf_op jit(solution)/shard_map/ppermute | solution.py:34
  52.8 0.7 %onehots.1 = (bf16[4,128,768]{2,1,0:T(8,128)(2,1)S(1)}, s32[4,768]{1,0:T(4,128)S(1)}) custom-call(s32[4]{0:T(128)S(1)} %pad_add_fusion.index_ref, s32[4,768]{1,0:T(4,128)S(1)} %bitcast.27, s32[1,768]{1,0:T(1,128)S(1)} %broadcast_in_dim.7.component_ref), custom_call_target="tpu_custom_call" | custom-call | tf_op jit(solution)/shard_map/onehots/pallas_call | solution.py:188
  53.6 0.8 %collective-permute-done.17.e3 = f32[1,768]{1,0:T(1,128)S(1)} collective-permute-done((f32[1,768]{1,0:T(1,128)S(1)}, f32[1,768]{1,0:T(1,128)S(1)}, u32[]{:S(2)}, u32[]{:S(2)}) %collective-permute-start.17) | collective-permute-done | bytes 3104 | tf_op jit(solution)/shard_map/ppermute | solution.py:34
  54.7 1.9 %collective-permute-start.18 = (f32[2,3,128]{2,1,0:T(4,128)S(1)}, f32[2,3,128]{2,1,0:T(4,128)S(1)}, u32[]{:S(2)}, u32[]{:S(2)}) collective-permute-start(f32[2,3,128]{2,1,0:T(4,128)S(1)} %get-tuple-element.12), channel_id=1, source_target_pairs={{4,0},{6,2},{8,4},{1,5},{10,6},{3,7},{12,8},{5,9},{14,10},{7,11},{... | collective-permute-start | bytes 9224 | tf_op jit(solution)/shard_map/ppermute | solution.py:256
  56.7 8.1 %collective-permute-done.18.received_ref = f32[2,3,128]{2,1,0:T(4,128)S(1)} collective-permute-done((f32[2,3,128]{2,1,0:T(4,128)S(1)}, f32[2,3,128]{2,1,0:T(4,128)S(1)}, u32[]{:S(2)}, u32[]{:S(2)}) %collective-permute-start.18) | collective-permute-done | bytes 3104 | tf_op jit(solution)/shard_map/ppermute | solution.py:256
  64.8 1.2 %collective-permute-done.19.passed_ref = f32[3,128]{1,0:T(4,128)S(1)} collective-permute-done((f32[3,128]{1,0:T(4,128)S(1)}, f32[3,128]{1,0:T(4,128)S(1)}, u32[]{:S(2)}, u32[]{:S(2)}) %collective-permute-start.19) | collective-permute-done | bytes 1568 | tf_op jit(solution)/shard_map/ppermute | solution.py:34
  (54 shorter events, 4.3 us)
Async XLA Ops:
  1.2 21.5 %collective-permute-start.9 = (f32[2,104,128]{2,1,0:T(8,128)S(1)}, f32[2,104,128]{2,1,0:T(8,128)S(1)}, u32[]{:S(2)}, u32[]{:S(2)}) collective-permute-start(f32[2,104,128]{2,1,0:T(8,128)S(1)} %pack_weight.1), channel_id=1, source_target_pairs={{0,0},{64,1},{128,2},{192,3},{4,4},{68,5},{132,6},{196,7},{8,8},{7... | collective-permute-start | bytes 319496 | tf_op jit(solution)/shard_map/ppermute | solution.py:34
  10.6 12.3 %collective-permute-start.10 = (f32[2,104,128]{2,1,0:T(8,128)S(1)}, f32[2,104,128]{2,1,0:T(8,128)S(1)}, u32[]{:S(2)}, u32[]{:S(2)}) collective-permute-start(f32[2,104,128]{2,1,0:T(8,128)S(1)} %pack_weight.1), channel_id=1, source_target_pairs={{16,0},{80,1},{144,2},{208,3},{20,4},{84,5},{148,6},{212,7},{24,8}... | collective-permute-start | bytes 319496 | tf_op jit(solution)/shard_map/ppermute | solution.py:34
  10.7 15.1 %collective-permute-start = (f32[2,104,128]{2,1,0:T(8,128)S(1)}, f32[2,104,128]{2,1,0:T(8,128)S(1)}, u32[]{:S(2)}, u32[]{:S(2)}) collective-permute-start(f32[2,104,128]{2,1,0:T(8,128)S(1)} %pack_weight.1), channel_id=1, source_target_pairs={{32,0},{96,1},{160,2},{224,3},{36,4},{100,5},{164,6},{228,7},{40,8... | collective-permute-start | bytes 319496 | tf_op jit(solution)/shard_map/ppermute | solution.py:34
  15.0 10.8 %collective-permute-start.1 = (f32[2,104,128]{2,1,0:T(8,128)S(1)}, f32[2,104,128]{2,1,0:T(8,128)S(1)}, u32[]{:S(2)}, u32[]{:S(2)}) collective-permute-start(f32[2,104,128]{2,1,0:T(8,128)S(1)} %pack_weight.1), channel_id=1, source_target_pairs={{48,0},{112,1},{176,2},{240,3},{52,4},{116,5},{180,6},{244,7},{56,... | collective-permute-start | bytes 319496 | tf_op jit(solution)/shard_map/ppermute | solution.py:34
  15.4 17.9 %collective-permute-start.7 = (f32[2,100,768]{2,0,1:T(2,128)}, f32[2,100,768]{2,0,1:T(2,128)S(1)}, u32[]{:S(2)}, u32[]{:S(2)}) collective-permute-start(f32[2,100,768]{2,0,1:T(2,128)} %param.5), channel_id=1, source_target_pairs={{2,0},{3,1},{0,2},{1,3},{6,4},{7,5},{4,6},{5,7},{10,8},{11,9},{8,1... | collective-permute-start | bytes 1843208 | tf_op jit(solution)/shard_map/ppermute | solution.py:34
  20.2 2.1 %copy-start = (bf16[2,3,2,256,768]{4,3,2,1,0:T(8,128)(2,1)}, bf16[2,3,2,256,768]{4,3,2,1,0:T(8,128)(2,1)S(1)}, u32[]{:S(2)}) copy-start(bf16[2,3,2,256,768]{4,3,2,1,0:T(8,128)(2,1)S(1)} %prepare_fields.1.after_ref.field) | copy-start | bytes 14155780
  22.7 18.0 %copy-start.1 = (bf16[2,3,2,256,768]{4,3,2,1,0:T(8,128)(2,1)S(1)}, bf16[2,3,2,256,768]{4,3,2,1,0:T(8,128)(2,1)}, u32[]{:S(2)}) copy-start(bf16[2,3,2,256,768]{4,3,2,1,0:T(8,128)(2,1)} %copy-done) | copy-start | bytes 14155780
  22.8 16.1 %collective-permute-start.6 = (f32[2,100,768]{2,0,1:T(2,128)S(1)}, f32[2,100,768]{2,0,1:T(2,128)S(1)}, u32[]{:S(2)}, u32[]{:S(2)}) collective-permute-start(f32[2,100,768]{2,0,1:T(2,128)S(1)} %copy.7), channel_id=1, source_target_pairs={{1,0},{0,1},{3,2},{2,3},{5,4},{4,5},{7,6},{6,7},{9,8},{8,9},{11,10... | collective-permute-start | bytes 1843208 | tf_op jit(solution)/shard_map/ppermute | solution.py:34
  22.9 6.9 %collective-permute-start.11 = (f32[2,2,104,128]{3,2,1,0:T(8,128)S(1)}, f32[2,2,104,128]{3,2,1,0:T(8,128)S(1)}, u32[]{:S(2)}, u32[]{:S(2)}) collective-permute-start(f32[2,2,104,128]{3,2,1,0:T(8,128)S(1)} %pad_maximum_fusion.1), channel_id=1, source_target_pairs={{4,0},{5,1},{6,2},{7,3},{8,4},{9,5},{10,6},{11,7},{12,8},{13,9},{1... | collective-permute-start | bytes 638984 | tf_op jit(solution)/shard_map/ppermute | solution.py:34
  25.8 7.2 %collective-permute-start.12 = (f32[2,2,104,128]{3,2,1,0:T(8,128)S(1)}, f32[2,2,104,128]{3,2,1,0:T(8,128)S(1)}, u32[]{:S(2)}, u32[]{:S(2)}) collective-permute-start(f32[2,2,104,128]{3,2,1,0:T(8,128)S(1)} %pad_maximum_fusion.1), channel_id=1, source_target_pairs={{12,0},{13,1},{14,2},{15,3},{0,4},{1,5},{2,6},{3,7},{4,8},{5,9},{6... | collective-permute-start | bytes 638984 | tf_op jit(solution)/shard_map/ppermute | solution.py:34
  25.8 10.1 %collective-permute-start.2 = (f32[2,2,104,128]{3,2,1,0:T(8,128)S(1)}, f32[2,2,104,128]{3,2,1,0:T(8,128)S(1)}, u32[]{:S(2)}, u32[]{:S(2)}) collective-permute-start(f32[2,2,104,128]{3,2,1,0:T(8,128)S(1)} %pad_maximum_fusion), channel_id=1, source_target_pairs={{4,0},{5,1},{6,2},{7,3},{8,4},{9,5},{10,6},{11,7},{12,8},{13,9},{1... | collective-permute-start | bytes 638984 | tf_op jit(solution)/shard_map/ppermute | solution.py:34
  29.8 6.7 %collective-permute-start.3 = (f32[2,2,104,128]{3,2,1,0:T(8,128)S(1)}, f32[2,2,104,128]{3,2,1,0:T(8,128)S(1)}, u32[]{:S(2)}, u32[]{:S(2)}) collective-permute-start(f32[2,2,104,128]{3,2,1,0:T(8,128)S(1)} %pad_maximum_fusion), channel_id=1, source_target_pairs={{12,0},{13,1},{14,2},{15,3},{0,4},{1,5},{2,6},{3,7},{4,8},{5,9},{6... | collective-permute-start | bytes 638984 | tf_op jit(solution)/shard_map/ppermute | solution.py:34
  33.0 6.2 %collective-permute-start.13 = (f32[2,104,128]{2,1,0:T(8,128)S(1)}, f32[2,104,128]{2,1,0:T(8,128)S(1)}, u32[]{:S(2)}, u32[]{:S(2)}) collective-permute-start(f32[2,104,128]{2,1,0:T(8,128)S(1)} %slice_bitcast_fusion.1), channel_id=1, source_target_pairs={{4,0},{5,1},{6,2},{7,3},{8,4},{9,5},{10,6},{11,7},{12,8},{13,9},{1... | collective-permute-start | bytes 319496 | tf_op jit(solution)/shard_map/ppermute | solution.py:34
  33.4 5.8 %collective-permute-start.8 = (f32[2,100,768]{2,0,1:T(2,128)S(1)}, f32[2,100,768]{2,0,1:T(2,128)S(1)}, u32[]{:S(2)}, u32[]{:S(2)}) collective-permute-start(f32[2,100,768]{2,0,1:T(2,128)S(1)} %collective-permute-done.7), channel_id=1, source_target_pairs={{1,0},{0,1},{3,2},{2,3},{5,4},{4,5},{7,6},{6,7},{9,8},{8,9},{11,10... | collective-permute-start | bytes 1843208 | tf_op jit(solution)/shard_map/ppermute | solution.py:34
  35.9 4.8 %collective-permute-start.14 = (f32[2,104,128]{2,1,0:T(8,128)S(1)}, f32[2,104,128]{2,1,0:T(8,128)S(1)}, u32[]{:S(2)}, u32[]{:S(2)}) collective-permute-start(f32[2,104,128]{2,1,0:T(8,128)S(1)} %slice_bitcast_fusion), channel_id=1, source_target_pairs={{12,0},{13,1},{14,2},{15,3},{0,4},{1,5},{2,6},{3,7},{4,8},{5,9},{6... | collective-permute-start | bytes 319496 | tf_op jit(solution)/shard_map/ppermute | solution.py:34
  36.5 7.0 %collective-permute-start.4 = (f32[2,104,128]{2,1,0:T(8,128)S(1)}, f32[2,104,128]{2,1,0:T(8,128)S(1)}, u32[]{:S(2)}, u32[]{:S(2)}) collective-permute-start(f32[2,104,128]{2,1,0:T(8,128)S(1)} %slice_bitcast_fusion.3), channel_id=1, source_target_pairs={{4,0},{5,1},{6,2},{7,3},{8,4},{9,5},{10,6},{11,7},{12,8},{13,9},{1... | collective-permute-start | bytes 319496 | tf_op jit(solution)/shard_map/ppermute | solution.py:34
  38.8 5.0 %collective-permute-start.5 = (f32[2,104,128]{2,1,0:T(8,128)S(1)}, f32[2,104,128]{2,1,0:T(8,128)S(1)}, u32[]{:S(2)}, u32[]{:S(2)}) collective-permute-start(f32[2,104,128]{2,1,0:T(8,128)S(1)} %slice_bitcast_fusion.2), channel_id=1, source_target_pairs={{12,0},{13,1},{14,2},{15,3},{0,4},{1,5},{2,6},{3,7},{4,8},{5,9},{6... | collective-permute-start | bytes 319496 | tf_op jit(solution)/shard_map/ppermute | solution.py:34
  43.5 9.3 %copy-start.6 = (s32[768]{0:T(1024)S(1)}, s32[768]{0:T(1024)}, u32[]{:S(2)}) copy-start(s32[768]{0:T(1024)} %param.9) | copy-start | bytes 9220
  43.5 9.3 %copy-start.5 = (s32[768,4]{0,1:T(4,128)S(1)}, s32[768,4]{0,1:T(4,128)}, u32[]{:S(2)}) copy-start(s32[768,4]{0,1:T(4,128)} %param.8) | copy-start | bytes 36868
  46.6 6.9 %collective-permute-start.15 = (f32[1,768]{1,0:T(1,128)S(1)}, f32[1,768]{1,0:T(1,128)S(1)}, u32[]{:S(2)}, u32[]{:S(2)}) collective-permute-start(f32[1,768]{1,0:T(1,128)S(1)} %product.3.e0), channel_id=1, source_target_pairs={{1,0},{0,1},{3,2},{2,3},{5,4},{4,5},{7,6},{6,7},{9,8},{8,9},{11,10... | collective-permute-start | bytes 9224 | tf_op jit(solution)/shard_map/ppermute | solution.py:34
  51.1 2.5 %collective-permute-start.16 = (f32[1,768]{1,0:T(1,128)S(1)}, f32[1,768]{1,0:T(1,128)S(1)}, u32[]{:S(2)}, u32[]{:S(2)}) collective-permute-start(f32[1,768]{1,0:T(1,128)S(1)} %product.3.e0), channel_id=1, source_target_pairs={{2,0},{3,1},{0,2},{1,3},{6,4},{7,5},{4,6},{5,7},{10,8},{11,9},{8,1... | collective-permute-start | bytes 9224 | tf_op jit(solution)/shard_map/ppermute | solution.py:34
  51.1 3.3 %collective-permute-start.17 = (f32[1,768]{1,0:T(1,128)S(1)}, f32[1,768]{1,0:T(1,128)S(1)}, u32[]{:S(2)}, u32[]{:S(2)}) collective-permute-start(f32[1,768]{1,0:T(1,128)S(1)} %product.3.e0), channel_id=1, source_target_pairs={{3,0},{2,1},{1,2},{0,3},{7,4},{6,5},{5,6},{4,7},{11,8},{10,9},{9,1... | collective-permute-start | bytes 9224 | tf_op jit(solution)/shard_map/ppermute | solution.py:34
  54.7 10.1 %collective-permute-start.18 = (f32[2,3,128]{2,1,0:T(4,128)S(1)}, f32[2,3,128]{2,1,0:T(4,128)S(1)}, u32[]{:S(2)}, u32[]{:S(2)}) collective-permute-start(f32[2,3,128]{2,1,0:T(4,128)S(1)} %get-tuple-element.12), channel_id=1, source_target_pairs={{4,0},{6,2},{8,4},{1,5},{10,6},{3,7},{12,8},{5,9},{14,10},{7,11},{... | collective-permute-start | bytes 9224 | tf_op jit(solution)/shard_map/ppermute | solution.py:256
  64.8 1.2 %collective-permute-start.19 = (f32[3,128]{1,0:T(4,128)S(1)}, f32[3,128]{1,0:T(4,128)S(1)}, u32[]{:S(2)}, u32[]{:S(2)}) collective-permute-start(f32[3,128]{1,0:T(4,128)S(1)} %slice_bitcast_fusion.4), channel_id=1, source_target_pairs={{1,0},{0,1},{3,2},{2,3},{5,4},{4,5},{7,6},{6,7},{9,8},{8,9},{11,10... | collective-permute-start | bytes 4616 | tf_op jit(solution)/shard_map/ppermute | solution.py:34
  (3 other events, 4.0 us)

commit v4 on v3

--- a/solution.py
+++ b/solution.py
@@ -10,6 +10,7 @@
 CELL_TILE = 512
 AXES = ("mesh", "tx")
 SIZE_Z, SIZE_Y = 8, 4
+TURNS = (0, 1, 2, 3)
 ROWS = 104
 MIB = 1024 * 1024
 WHOLE = pl.BlockSpec(memory_space=pltpu.VMEM)
@@ -59,61 +60,80 @@
     return high, low
 
 
-def prepare_kernel(place_ref, rx_ref, o_ref):
-    for k in range(4):
-        for s in range(4):
+def prepare_kernel(place_ref, after_ref, rx_ref, o_ref):
+    for s in range(4):
+        for k in range(4):
             row = pl.multiple_of(place_ref[k] * 128 + place_ref[4 + s] * 32, 32)
             real, imag = rx_ref[0, pl.ds(row, 32), :], rx_ref[1, pl.ds(row, 32), :]
-            rows = slice(128 * (k % 2) + 32 * s, 128 * (k % 2) + 32 * (s + 1))
+            rows = slice(128 * (s % 2) + 32 * k, 128 * (s % 2) + 32 * (k + 1))
             for n, value in enumerate((real, imag - real, real + imag)):
                 high, low = split(value)
-                o_ref[k // 2, n, 0, rows, :] = low
-                o_ref[k // 2, n, 1, rows, :] = high
-
-
-def prepare_fields(places, rx_field):
+                o_ref[s // 2, n, 0, rows, :] = low
+                o_ref[s // 2, n, 1, rows, :] = high
+
+
+def prepare_fields(places, after, rx_field):
     edges = rx_field.shape[2]
     return pl.pallas_call(
         prepare_kernel,
-        in_specs=[SCALARS, WHOLE],
+        in_specs=[SCALARS, pl.BlockSpec(memory_space=pl.ANY), WHOLE],
         out_specs=WHOLE,
         out_shape=jax.ShapeDtypeStruct((2, 3, 2, 256, edges), jnp.bfloat16),
         compiler_params=limit(4),
         cost_estimate=pl.CostEstimate(flops=10_000_000, bytes_accessed=8_000_000, transcendentals=0),
         name="prepare_fields",
-    )(places, rx_field)
-
-
-def arrange_kernel(after_ref, tx_ref, o_ref):
-    o_ref[0] = tx_ref[:, 0, :]
-    o_ref[1] = tx_ref[:, 1, :]
-
-
-def arrange(after, tx_field):
-    return pl.pallas_call(
-        arrange_kernel,
-        in_specs=[pl.BlockSpec(memory_space=pl.ANY), WHOLE],
-        out_specs=WHOLE,
-        out_shape=jax.ShapeDtypeStruct(tx_field.shape, jnp.float32),
+    )(places, after, rx_field)
+
+
+def gate_kernel(after0_ref, after1_ref, value_ref, o_ref):
+    pass
+
+
+def gate(after, value):
+    anywhere = pl.BlockSpec(memory_space=pl.ANY)
+    return pl.pallas_call(
+        gate_kernel,
+        in_specs=[anywhere] * 3,
+        out_specs=anywhere,
+        out_shape=jax.ShapeDtypeStruct(value.shape, value.dtype),
+        input_output_aliases={2: 0},
+        compiler_params=limit(2),
+        name="gate",
+    )(*after, value)
+
+
+def collect_kernel(own_ref, own_c_ref, flipped_ref, flipped_c_ref, o_ref):
+    o_ref[...] = jnp.zeros_like(o_ref)
+    for part in range(2):
+        for g, value in enumerate((own_ref, own_c_ref, flipped_ref, flipped_c_ref)):
+            o_ref[part, ROWS * g : ROWS * g + 100, :] = value[:, part, :]
+
+
+def collect(*fields):
+    return pl.pallas_call(
+        collect_kernel,
+        in_specs=[WHOLE] * 4,
+        out_specs=WHOLE,
+        out_shape=jax.ShapeDtypeStruct((2, 4 * ROWS, fields[0].shape[2]), jnp.float32),
         compiler_params=limit(4),
-        name="arrange",
-    )(after, tx_field.transpose(1, 0, 2))
+        name="collect",
+    )(*fields)
 
 
 def lane_group():
     return lax.broadcasted_iota(jnp.int32, (ROWS, 128), 1) // 32
 
 
-def product_kernel(
-    group_index, index_ref, own0, own1, above, below, far0, far1, t0, t1, t2, t3, field, before, o_ref, w_scr, wh_scr, wl_scr
-):
+def product_kernel(half, sources, index_ref, *refs):
+    blocks, (tx, field, before, o_ref, w_scr, wh_scr, wl_scr) = refs[:-7], refs[-7:]
     tx_index = index_ref[0]
     group = lane_group()
-    own, far, txs = (own0, own1), (far0, far1), (t0, t1, t2, t3)
     for part in range(2):
-        for k in range(2):
-            blocks = [own[k][part], above[k, part], far[k][part], below[k, part]]
-            rolled = [b if s == 0 else pltpu.roll(b, 32 * s, 1) for s, b in enumerate(blocks)]
+        for s in range(2):
+            rolled = []
+            for k, (ref, place) in enumerate(sources[s]):
+                block = blocks[ref][part] if place is None else blocks[ref][place, part]
+                rolled.append(pltpu.roll(block, 32 * k, 1) if k else block)
             for g in range(4):
                 mixed = rolled[(0 - g) % 4]
                 for lane in range(1, 4):
@@ -121,7 +141,7 @@
                 if g:
                     mixed = pltpu.roll(mixed, 128 - 32 * g, 1)
                 row = pl.multiple_of(jnp.bitwise_xor(tx_index, g) * ROWS, 8)
-                w_scr[part, pl.ds(row, ROWS), 128 * k : 128 * (k + 1)] = mixed
+                w_scr[part, pl.ds(row, ROWS), 128 * s : 128 * (s + 1)] = mixed
     real, imag = w_scr[0], w_scr[1]
     for n, value in enumerate((real + imag, real, imag)):
         high, low = split(value)
@@ -132,26 +152,22 @@
         cols = slice(256 * tile, 256 * (tile + 1))
         products = []
         for n in range(3):
-            both = field[group_index, n, :, :, cols].reshape(512, 256)
-            high = field[group_index, n, 1, :, cols]
+            both = field[half, n, :, :, cols].reshape(512, 256)
+            high = field[half, n, 1, :, cols]
             products.append(
                 jnp.dot(wh_scr[n], both, preferred_element_type=jnp.float32)
                 + jnp.dot(wl_scr[n], high, preferred_element_type=jnp.float32)
             )
-        total = before[:, cols]
-        for g in range(4):
-            rows = slice(ROWS * g, ROWS * g + 100)
-            a, b = txs[g][0, :, cols], txs[g][1, :, cols]
-            term = (a - b) * products[0][rows] - b * products[1][rows] - a * products[2][rows]
-            total = total + jnp.sum(term, axis=0, keepdims=True)
-        o_ref[:, cols] = total
-
-
-def product(index, blocks, txs, fields, group, before):
+        a, b = tx[0, :, cols], tx[1, :, cols]
+        term = (a - b) * products[0] - b * products[1] - a * products[2]
+        o_ref[:, cols] = before[:, cols] + jnp.sum(term, axis=0, keepdims=True)
+
+
+def product(half, sources, index, blocks, tx, fields, before):
     edges = fields.shape[4]
     return pl.pallas_call(
-        functools.partial(product_kernel, group),
-        in_specs=[SCALARS] + [WHOLE] * 12,
+        functools.partial(product_kernel, half, sources),
+        in_specs=[SCALARS] + [WHOLE] * (len(blocks) + 3),
         out_specs=WHOLE,
         scratch_shapes=[
             pltpu.VMEM((2, 4 * ROWS, 256), jnp.float32),
@@ -162,7 +178,7 @@
         compiler_params=limit(12),
         cost_estimate=pl.CostEstimate(flops=3_000_000_000, bytes_accessed=6_000_000, transcendentals=0),
         name="product",
-    )(index, *blocks, *txs, fields, before)
+    )(index, *blocks, tx, fields, before)
 
 
 def onehot_kernel(index_ref, cells_ref, component_ref, hot_ref, row_ref):
@@ -268,12 +284,22 @@
     return x_hi, z, y, 1 - x_lo, 1 - core
 
 
-def z_source(k):
-    return lambda x_hi, z, y, x_lo, core: (x_lo, 4 * core + (z + k) % 4, y, x_hi, z // 4)
-
-
-def y_source(step):
-    return lambda x_hi, z, y, x_lo, core: (x_hi, z, y + step, x_lo, core)
+def z_source(turn):
+    return lambda x_hi, z, y, x_lo, core: (
+        x_lo,
+        4 * core + ((z % 4) ^ turn),
+        y,
+        x_hi,
+        1 - core if z // 4 == core else core,
+    )
+
+
+def y_partner(pairs, y):
+    return (y ^ 1) if pairs == 0 else (y + 2 * (y % 2) - 1) % SIZE_Y
+
+
+def y_source(pairs):
+    return lambda x_hi, z, y, x_lo, core: (x_hi, z, y_partner(pairs, y), x_lo, core)
 
 
 def shards(tx_field, rx_field, misfit_weight, incidence, component):
@@ -281,26 +307,28 @@
     tx_index = lax.axis_index("tx")
     z, y = (mesh_index // 4) % 8, mesh_index % 4
     packed = pack_weight(misfit_weight)
-    tx_x = fetch(tx_field, flip_x)
-    from_z = [fetch(packed, z_source(k)) for k in range(4)]
-    steps = jnp.arange(4, dtype=jnp.int32)
-    places = jnp.concatenate([(z + steps) % 4, (y + steps) % 4]).astype(jnp.int32)
-    fields = prepare_fields(places, rx_field)
-    tx_own = arrange(fields, tx_field)
-    txs = [tx_own, fetch(tx_own, flip_core), tx_x, fetch(tx_x, flip_core)]
+    tx_own = tx_field.transpose(1, 0, 2)
+    tx_x = fetch(tx_own, flip_x)
+    from_z = [fetch(packed, z_source(turn)) for turn in TURNS]
+    y_places = [y, y_partner(0, y), y_partner(1, y), (y + 2) % SIZE_Y]
+    places = jnp.stack([(z % 4) ^ turn for turn in TURNS] + y_places).astype(jnp.int32)
     index = jnp.stack([tx_index, tx_index // 2, tx_index % 2, (mesh_index - 1) * CELL_TILE]).astype(jnp.int32)
     hot, row = onehots(index, incidence, component)
 
+    stacked = [jnp.stack(from_z[2 * g : 2 * g + 2]) for g in range(2)]
+    tx_c = fetch(tx_own, flip_core)
+    tx_x = gate(stacked, tx_x)
+    tx_xc = fetch(tx_x, flip_core)
+    near = [fetch(stacked[g], y_source(0)) for g in range(2)]
+    far = [fetch(stacked[g], y_source(1)) for g in range(2)]
+    last = [fetch(near[0], y_source(1)), fetch(far[1], y_source(0))]
+    fields = prepare_fields(places, stacked[1], rx_field)
+    tx = collect(tx_own, tx_c, tx_x, tx_xc)
     edge = jnp.zeros((1, tx_field.shape[2]), jnp.float32)
-    for group in range(2):
-        own = from_z[2 * group : 2 * group + 2]
-        stacked = jnp.stack(own)
-        above = fetch(stacked, y_source(1))
-        below = fetch(stacked, y_source(-1))
-        far0 = fetch(above[0], y_source(1))
-        far1 = fetch(below[1], y_source(-1))
-        blocks = [own[0], own[1], above, below, far0, far1]
-        edge = product(index, blocks, txs, fields, group, edge)
+    early = [[(k, None) for k in range(4)], [(4, 0), (4, 1), (5, 0), (5, 1)]]
+    late = [[(0, 0), (0, 1), (1, 0), (1, 1)], [(2, 0), (2, 1), (3, 0), (3, 1)]]
+    edge = product(0, early, index, from_z + near, tx, fields, edge)
+    edge = product(1, late, index, far + last, tx, fields, edge)
     terms = [edge, fetch(edge, flip_core), fetch(edge, flip_x), fetch(edge, flip_both)]
     own, send = scatter(terms, hot, row)
     received = neighbour_parts(send)

time: 67.4 us -> 62.3 us (0.924); the launches traced: 66.6 us -> 62.2 us
  starting transfers between devices: 36.2 us -> 26.4 us
  waiting for transfers between devices: 15.7 us -> 23.5 us
  local copies, waits for them, and re-layouts: 5.44 us -> 2.91 us
    ppermute x19 -> x17, starting transfers between devices: 34.2 us -> 24.5 us  [fetch(): return lax.ppermute(block, AXES, route)]
    ppermute x19 -> x17, waiting for transfers between devices: 7.54 us -> 15.4 us  [fetch(): return lax.ppermute(block, AXES, route)]
    unnamed x14 -> x10, local copies, waits for them, and re-layouts: 4.95 us -> 2.81 us
    pallas_call x4 -> x5, Pallas kernels: 6.86 us -> 7.16 us  [the longest x2 5.38 us: product(): pl.pallas_call(functools.partial(product_kernel, half, sources), in_specs...]
  transfers between devices with their start and end apart: 20 -> 18, of which waited for: 7 -> 10; matrix products, arithmetic and copies ran while one was open for 1% -> 0% of each run, Pallas kernels for 7% -> 9%
where the time goes in v4:
time: 62.3 us; the launch traced here: 62.2 us
  starting transfers between devices  26.4 us (42%)
  waiting for transfers between devices  23.5 us (38%)
  Pallas kernels  9.05 us (15%)
  local copies, waits for them, and re-layouts  2.91 us (5%)
    ppermute x17, starting transfers between devices, fetch(): return lax.ppermute(block, AXES, route)  24.5 us
    ppermute x17, waiting for transfers between devices, fetch(): return lax.ppermute(block, AXES, route)  15.4 us
    ppermute x1, waiting for transfers between devices, neighbour_parts(): return lax.ppermute(block, AXES, route)  8.15 us
    pallas_call x2, Pallas kernels, product(): pl.pallas_call(functools.partial(product_kernel, half, sources), in_specs...  5.38 us
    unnamed x10, local copies, waits for them, and re-layouts  2.81 us
    ppermute x1, starting transfers between devices, neighbour_parts(): return lax.ppermute(block, AXES, route)  1.94 us
  transfers between devices with their start and end apart: 18, of which 10 were waited for; matrix products, arithmetic and copies ran while one was open for 0% of the time, Pallas kernels for 9%

profile of v4, /device:TPU:7, one launch (start us, length us, event | category | flops | bytes accessed | tf_op | source)
XLA Modules:
  0.0 62.2 jit_solution(9559608548244415926)
XLA Ops:
  0.6 0.9 %copy-done.2 = f32[2,400,32]{1,2,0:T(8,128)S(1)} copy-done((f32[2,400,32]{1,2,0:T(8,128)S(1)}, f32[2,400,32]{1,2,0:T(8,128)}, u32[]{:S(2)}) %copy-start.2) | copy-done | bytes 102424
  1.7 2.6 %collective-permute-start.1 = (f32[2,104,128]{2,1,0:T(8,128)S(1)}, f32[2,104,128]{2,1,0:T(8,128)S(1)}, u32[]{:S(2)}, u32[]{:S(2)}) collective-permute-start(f32[2,104,128]{2,1,0:T(8,128)S(1)} %pack_weight.1), channel_id=1, source_target_pairs={{17,0},{81,1},{145,2},{209,3},{21,4},{85,5},{149,6},{213,7},{25,8}... | collective-permute-start | bytes 319496 | tf_op jit(solution)/shard_map/ppermute | solution.py:35
  4.3 5.2 %collective-permute-start = (f32[2,104,128]{2,1,0:T(8,128)S(1)}, f32[2,104,128]{2,1,0:T(8,128)S(1)}, u32[]{:S(2)}, u32[]{:S(2)}) collective-permute-start(f32[2,104,128]{2,1,0:T(8,128)S(1)} %pack_weight.1), channel_id=1, source_target_pairs={{1,0},{65,1},{129,2},{193,3},{5,4},{69,5},{133,6},{197,7},{9,8},{7... | collective-permute-start | bytes 319496 | tf_op jit(solution)/shard_map/ppermute | solution.py:35
  9.5 2.1 %collective-permute-start.4 = (f32[2,104,128]{2,1,0:T(8,128)S(1)}, f32[2,104,128]{2,1,0:T(8,128)S(1)}, u32[]{:S(2)}, u32[]{:S(2)}) collective-permute-start(f32[2,104,128]{2,1,0:T(8,128)S(1)} %pack_weight.1), channel_id=1, source_target_pairs={{49,0},{113,1},{177,2},{241,3},{53,4},{117,5},{181,6},{245,7},{57,... | collective-permute-start | bytes 319496 | tf_op jit(solution)/shard_map/ppermute | solution.py:35
  11.8 0.8 %collective-permute-done.refs_0_ = f32[2,104,128]{2,1,0:T(8,128)S(1)} collective-permute-done((f32[2,104,128]{2,1,0:T(8,128)S(1)}, f32[2,104,128]{2,1,0:T(8,128)S(1)}, u32[]{:S(2)}, u32[]{:S(2)}) %collective-permute-start) | collective-permute-done | bytes 106528 | tf_op jit(solution)/shard_map/ppermute | solution.py:35
  12.6 3.4 %collective-permute-done.4.refs_3_ = f32[2,104,128]{2,1,0:T(8,128)S(1)} collective-permute-done((f32[2,104,128]{2,1,0:T(8,128)S(1)}, f32[2,104,128]{2,1,0:T(8,128)S(1)}, u32[]{:S(2)}, u32[]{:S(2)}) %collective-permute-start.4) | collective-permute-done | bytes 106528 | tf_op jit(solution)/shard_map/ppermute | solution.py:35
  16.1 1.7 %collective-permute-done.3.refs_2_ = f32[2,104,128]{2,1,0:T(8,128)S(1)} collective-permute-done((f32[2,104,128]{2,1,0:T(8,128)S(1)}, f32[2,104,128]{2,1,0:T(8,128)S(1)}, u32[]{:S(2)}, u32[]{:S(2)}) %collective-permute-start.3) | collective-permute-done | bytes 106528 | tf_op jit(solution)/shard_map/ppermute | solution.py:35
  17.8 2.2 %collective-permute-start.11 = (f32[100,2,768]{2,1,0:T(2,128)S(1)}, f32[100,2,768]{2,1,0:T(2,128)S(1)}, u32[]{:S(2)}, u32[]{:S(2)}) collective-permute-start(f32[100,2,768]{2,1,0:T(2,128)S(1)} %gate.1.flipped_ref), channel_id=1, source_target_pairs={{1,0},{0,1},{3,2},{2,3},{5,4},{4,5},{7,6},{6,7},{9,8},{8,9},{11,10... | collective-permute-start | bytes 1843208 | tf_op jit(solution)/shard_map/ppermute | solution.py:35
  20.0 2.8 %collective-permute-start.5 = (f32[2,2,104,128]{3,2,1,0:T(8,128)S(1)}, f32[2,2,104,128]{3,2,1,0:T(8,128)S(1)}, u32[]{:S(2)}, u32[]{:S(2)}) collective-permute-start(f32[2,2,104,128]{3,2,1,0:T(8,128)S(1)} %pad_maximum_fusion.1.after1_ref.after_ref), channel_id=1, source_target_pairs={{12,0},{13,1},{14,2},{15,3},{8,4},{9,5},{10,6},{11,7},{4,8},{5,9},... | collective-permute-start | bytes 638984 | tf_op jit(solution)/shard_map/ppermute | solution.py:35
  22.8 1.5 %collective-permute-start.12 = (f32[2,2,104,128]{3,2,1,0:T(8,128)S(1)}, f32[2,2,104,128]{3,2,1,0:T(8,128)S(1)}, u32[]{:S(2)}, u32[]{:S(2)}) collective-permute-start(f32[2,2,104,128]{3,2,1,0:T(8,128)S(1)} %pad_maximum_fusion.1.after1_ref.after_ref), channel_id=1, source_target_pairs={{4,0},{5,1},{6,2},{7,3},{0,4},{1,5},{2,6},{3,7},{12,8},{13,9},{14,... | collective-permute-start | bytes 638984 | tf_op jit(solution)/shard_map/ppermute | solution.py:35
  24.4 1.9 %copy-done = f32[2,512,768]{2,1,0:T(8,128)S(1)} copy-done((f32[2,512,768]{2,1,0:T(8,128)S(1)}, f32[2,512,768]{2,1,0:T(8,128)}, u32[]{:S(2)}) %copy-start) | copy-done | bytes 3145752
  26.3 1.2 %prepare_fields.1.refs_7_.refs_5_ = bf16[2,3,2,256,768]{4,3,2,1,0:T(8,128)(2,1)S(1)} custom-call(s32[8]{0:T(128)S(1)} %stack.79.place_ref, f32[2,2,104,128]{3,2,1,0:T(8,128)S(1)} %pad_maximum_fusion.1.after1_ref.after_ref, f32[2,512,768]{2,1,0:T(8,128)S(1)} %copy-done), custom_call_target="tpu_custom_call" | custom-call | flops 10000000 | bytes 8000000 | tf_op jit(solution)/shard_map/prepare_fields/pallas_call | solution.py:77
  28.1 2.6 %collective-permute-start.2 = (f32[2,2,104,128]{3,2,1,0:T(8,128)S(1)}, f32[2,2,104,128]{3,2,1,0:T(8,128)S(1)}, u32[]{:S(2)}, u32[]{:S(2)}) collective-permute-start(f32[2,2,104,128]{3,2,1,0:T(8,128)S(1)} %pad_maximum_fusion.after0_ref), channel_id=1, source_target_pairs={{12,0},{13,1},{14,2},{15,3},{8,4},{9,5},{10,6},{11,7},{4,8},{5,9},... | collective-permute-start | bytes 638984 | tf_op jit(solution)/shard_map/ppermute | solution.py:35
  31.6 2.2 %collective-permute-done.12.refs_5_ = f32[2,2,104,128]{3,2,1,0:T(8,128)S(1)} collective-permute-done((f32[2,2,104,128]{3,2,1,0:T(8,128)S(1)}, f32[2,2,104,128]{3,2,1,0:T(8,128)S(1)}, u32[]{:S(2)}, u32[]{:S(2)}) %collective-permute-start.12) | collective-permute-done | bytes 213024 | tf_op jit(solution)/shard_map/ppermute | solution.py:35
  33.8 2.7 %product.2.refs_6_ = f32[1,768]{1,0:T(1,128)S(1)} custom-call(s32[4]{0:T(128)S(1)} %pad_add_fusion.index_ref, f32[2,104,128]{2,1,0:T(8,128)S(1)} %collective-permute-done.refs_0_, f32[2,104,128]{2,1,0:T(8,128)S(1)} %collective-permute-done.1.refs_1_, f32[2,104,128]{2,1,0:T(8,128)S(1)} %collective-permute-done.3.refs_2_, ...), custom_call_target="tpu_custom_call" | custom-call | flops 3000000000 | bytes 6000000 | tf_op jit(solution)/shard_map/product/pallas_call | solution.py:168
  36.5 3.3 %collective-permute-done.7.refs_2_ = f32[2,2,104,128]{3,2,1,0:T(8,128)S(1)} collective-permute-done((f32[2,2,104,128]{3,2,1,0:T(8,128)S(1)}, f32[2,2,104,128]{3,2,1,0:T(8,128)S(1)}, u32[]{:S(2)}, u32[]{:S(2)}) %collective-permute-start.7) | collective-permute-done | bytes 213024 | tf_op jit(solution)/shard_map/ppermute | solution.py:35
  39.9 2.7 %product.3.e0 = f32[1,768]{1,0:T(1,128)S(1)} custom-call(s32[4]{0:T(128)S(1)} %pad_add_fusion.index_ref, f32[2,2,104,128]{3,2,1,0:T(8,128)S(1)} %collective-permute-done.2.refs_0_, f32[2,2,104,128]{3,2,1,0:T(8,128)S(1)} %collective-permute-done.5.refs_1_, f32[2,2,104,128]{3,2,1,0:T(8,128)S(1)} %collective-permute-done.7.refs_2_, ...), custom_call_target="tpu_custom_call" | custom-call | flops 3000000000 | bytes 6000000 | tf_op jit(solution)/shard_map/product/pallas_call | solution.py:168
  42.6 1.8 %collective-permute-start.13 = (f32[1,768]{1,0:T(1,128)S(1)}, f32[1,768]{1,0:T(1,128)S(1)}, u32[]{:S(2)}, u32[]{:S(2)}) collective-permute-start(f32[1,768]{1,0:T(1,128)S(1)} %product.3.e0), channel_id=1, source_target_pairs={{1,0},{0,1},{3,2},{2,3},{5,4},{4,5},{7,6},{6,7},{9,8},{8,9},{11,10... | collective-permute-start | bytes 9224 | tf_op jit(solution)/shard_map/ppermute | solution.py:35
  44.4 2.6 %collective-permute-start.14 = (f32[1,768]{1,0:T(1,128)S(1)}, f32[1,768]{1,0:T(1,128)S(1)}, u32[]{:S(2)}, u32[]{:S(2)}) collective-permute-start(f32[1,768]{1,0:T(1,128)S(1)} %product.3.e0), channel_id=1, source_target_pairs={{2,0},{3,1},{0,2},{1,3},{6,4},{7,5},{4,6},{5,7},{10,8},{11,9},{8,1... | collective-permute-start | bytes 9224 | tf_op jit(solution)/shard_map/ppermute | solution.py:35
  47.1 0.7 %onehots.1 = (bf16[4,128,768]{2,1,0:T(8,128)(2,1)S(1)}, s32[4,768]{1,0:T(4,128)S(1)}) custom-call(s32[4]{0:T(128)S(1)} %pad_add_fusion.index_ref, s32[4,768]{1,0:T(4,128)S(1)} %bitcast.29, s32[1,768]{1,0:T(1,128)S(1)} %broadcast_in_dim.7.component_ref), custom_call_target="tpu_custom_call" | custom-call | tf_op jit(solution)/shard_map/onehots/pallas_call | solution.py:204
  48.0 2.1 %collective-permute-done.15.e3 = f32[1,768]{1,0:T(1,128)S(1)} collective-permute-done((f32[1,768]{1,0:T(1,128)S(1)}, f32[1,768]{1,0:T(1,128)S(1)}, u32[]{:S(2)}, u32[]{:S(2)}) %collective-permute-start.15) | collective-permute-done | bytes 3104 | tf_op jit(solution)/shard_map/ppermute | solution.py:35
  50.3 1.9 %collective-permute-start.16 = (f32[2,3,128]{2,1,0:T(4,128)S(1)}, f32[2,3,128]{2,1,0:T(4,128)S(1)}, u32[]{:S(2)}, u32[]{:S(2)}) collective-permute-start(f32[2,3,128]{2,1,0:T(4,128)S(1)} %get-tuple-element.12), channel_id=1, source_target_pairs={{4,0},{6,2},{8,4},{1,5},{10,6},{3,7},{12,8},{5,9},{14,10},{7,11},{... | collective-permute-start | bytes 9224 | tf_op jit(solution)/shard_map/ppermute | solution.py:272
  52.3 8.1 %collective-permute-done.16.received_ref = f32[2,3,128]{2,1,0:T(4,128)S(1)} collective-permute-done((f32[2,3,128]{2,1,0:T(4,128)S(1)}, f32[2,3,128]{2,1,0:T(4,128)S(1)}, u32[]{:S(2)}, u32[]{:S(2)}) %collective-permute-start.16) | collective-permute-done | bytes 3104 | tf_op jit(solution)/shard_map/ppermute | solution.py:272
  60.4 1.2 %collective-permute-done.17.passed_ref = f32[3,128]{1,0:T(4,128)S(1)} collective-permute-done((f32[3,128]{1,0:T(4,128)S(1)}, f32[3,128]{1,0:T(4,128)S(1)}, u32[]{:S(2)}, u32[]{:S(2)}) %collective-permute-start.17) | collective-permute-done | bytes 1568 | tf_op jit(solution)/shard_map/ppermute | solution.py:35
  (38 shorter events, 3.8 us)
Async XLA Ops:
  0.0 17.8 %collective-permute-start.10 = (f32[100,2,768]{2,1,0:T(2,128)}, f32[100,2,768]{2,1,0:T(2,128)S(1)}, u32[]{:S(2)}, u32[]{:S(2)}) collective-permute-start(f32[100,2,768]{2,1,0:T(2,128)} %bitcast.21), channel_id=1, source_target_pairs={{2,0},{3,1},{0,2},{1,3},{6,4},{7,5},{4,6},{5,7},{10,8},{11,9},{8,1... | collective-permute-start | bytes 1843208 | tf_op jit(solution)/shard_map/ppermute | solution.py:35
  0.5 0.9 %copy-start.2 = (f32[2,400,32]{1,2,0:T(8,128)S(1)}, f32[2,400,32]{1,2,0:T(8,128)}, u32[]{:S(2)}) copy-start(f32[2,400,32]{1,2,0:T(8,128)} %param.7) | copy-start | bytes 307204
  1.7 9.9 %collective-permute-start.1 = (f32[2,104,128]{2,1,0:T(8,128)S(1)}, f32[2,104,128]{2,1,0:T(8,128)S(1)}, u32[]{:S(2)}, u32[]{:S(2)}) collective-permute-start(f32[2,104,128]{2,1,0:T(8,128)S(1)} %pack_weight.1), channel_id=1, source_target_pairs={{17,0},{81,1},{145,2},{209,3},{21,4},{85,5},{149,6},{213,7},{25,8}... | collective-permute-start | bytes 319496 | tf_op jit(solution)/shard_map/ppermute | solution.py:35
  4.3 8.3 %collective-permute-start = (f32[2,104,128]{2,1,0:T(8,128)S(1)}, f32[2,104,128]{2,1,0:T(8,128)S(1)}, u32[]{:S(2)}, u32[]{:S(2)}) collective-permute-start(f32[2,104,128]{2,1,0:T(8,128)S(1)} %pack_weight.1), channel_id=1, source_target_pairs={{1,0},{65,1},{129,2},{193,3},{5,4},{69,5},{133,6},{197,7},{9,8},{7... | collective-permute-start | bytes 319496 | tf_op jit(solution)/shard_map/ppermute | solution.py:35
  9.5 6.5 %collective-permute-start.4 = (f32[2,104,128]{2,1,0:T(8,128)S(1)}, f32[2,104,128]{2,1,0:T(8,128)S(1)}, u32[]{:S(2)}, u32[]{:S(2)}) collective-permute-start(f32[2,104,128]{2,1,0:T(8,128)S(1)} %pack_weight.1), channel_id=1, source_target_pairs={{49,0},{113,1},{177,2},{241,3},{53,4},{117,5},{181,6},{245,7},{57,... | collective-permute-start | bytes 319496 | tf_op jit(solution)/shard_map/ppermute | solution.py:35
  11.7 6.1 %collective-permute-start.3 = (f32[2,104,128]{2,1,0:T(8,128)S(1)}, f32[2,104,128]{2,1,0:T(8,128)S(1)}, u32[]{:S(2)}, u32[]{:S(2)}) collective-permute-start(f32[2,104,128]{2,1,0:T(8,128)S(1)} %pack_weight.1), channel_id=1, source_target_pairs={{33,0},{97,1},{161,2},{225,3},{37,4},{101,5},{165,6},{229,7},{41,8... | collective-permute-start | bytes 319496 | tf_op jit(solution)/shard_map/ppermute | solution.py:35
  11.7 19.1 %collective-permute-start.9 = (f32[100,2,768]{2,1,0:T(2,128)}, f32[100,2,768]{2,1,0:T(2,128)S(1)}, u32[]{:S(2)}, u32[]{:S(2)}) collective-permute-start(f32[100,2,768]{2,1,0:T(2,128)} %bitcast.22), channel_id=1, source_target_pairs={{1,0},{0,1},{3,2},{2,3},{5,4},{4,5},{7,6},{6,7},{9,8},{8,9},{11,10... | collective-permute-start | bytes 1843208 | tf_op jit(solution)/shard_map/ppermute | solution.py:35
  17.8 13.3 %collective-permute-start.11 = (f32[100,2,768]{2,1,0:T(2,128)S(1)}, f32[100,2,768]{2,1,0:T(2,128)S(1)}, u32[]{:S(2)}, u32[]{:S(2)}) collective-permute-start(f32[100,2,768]{2,1,0:T(2,128)S(1)} %gate.1.flipped_ref), channel_id=1, source_target_pairs={{1,0},{0,1},{3,2},{2,3},{5,4},{4,5},{7,6},{6,7},{9,8},{8,9},{11,10... | collective-permute-start | bytes 1843208 | tf_op jit(solution)/shard_map/ppermute | solution.py:35
  20.0 8.1 %collective-permute-start.5 = (f32[2,2,104,128]{3,2,1,0:T(8,128)S(1)}, f32[2,2,104,128]{3,2,1,0:T(8,128)S(1)}, u32[]{:S(2)}, u32[]{:S(2)}) collective-permute-start(f32[2,2,104,128]{3,2,1,0:T(8,128)S(1)} %pad_maximum_fusion.1.after1_ref.after_ref), channel_id=1, source_target_pairs={{12,0},{13,1},{14,2},{15,3},{8,4},{9,5},{10,6},{11,7},{4,8},{5,9},... | collective-permute-start | bytes 638984 | tf_op jit(solution)/shard_map/ppermute | solution.py:35
  22.8 8.0 %collective-permute-start.6 = (f32[2,2,104,128]{3,2,1,0:T(8,128)S(1)}, f32[2,2,104,128]{3,2,1,0:T(8,128)S(1)}, u32[]{:S(2)}, u32[]{:S(2)}) collective-permute-start(f32[2,2,104,128]{3,2,1,0:T(8,128)S(1)} %pad_maximum_fusion.after0_ref), channel_id=1, source_target_pairs={{4,0},{5,1},{6,2},{7,3},{0,4},{1,5},{2,6},{3,7},{12,8},{13,9},{14,... | collective-permute-start | bytes 638984 | tf_op jit(solution)/shard_map/ppermute | solution.py:35
  22.8 11.0 %collective-permute-start.12 = (f32[2,2,104,128]{3,2,1,0:T(8,128)S(1)}, f32[2,2,104,128]{3,2,1,0:T(8,128)S(1)}, u32[]{:S(2)}, u32[]{:S(2)}) collective-permute-start(f32[2,2,104,128]{3,2,1,0:T(8,128)S(1)} %pad_maximum_fusion.1.after1_ref.after_ref), channel_id=1, source_target_pairs={{4,0},{5,1},{6,2},{7,3},{0,4},{1,5},{2,6},{3,7},{12,8},{13,9},{14,... | collective-permute-start | bytes 638984 | tf_op jit(solution)/shard_map/ppermute | solution.py:35
  24.4 1.9 %copy-start = (f32[2,512,768]{2,1,0:T(8,128)S(1)}, f32[2,512,768]{2,1,0:T(8,128)}, u32[]{:S(2)}) copy-start(f32[2,512,768]{2,1,0:T(8,128)} %rx_ref.1) | copy-start | bytes 9437188
  26.3 4.8 %copy-start.1 = (f32[2,100,768]{2,0,1:T(2,128)S(1)}, f32[2,100,768]{2,0,1:T(2,128)}, u32[]{:S(2)}) copy-start(f32[2,100,768]{2,0,1:T(2,128)} %param.5) | copy-start | bytes 1843204
  28.1 8.4 %collective-permute-start.2 = (f32[2,2,104,128]{3,2,1,0:T(8,128)S(1)}, f32[2,2,104,128]{3,2,1,0:T(8,128)S(1)}, u32[]{:S(2)}, u32[]{:S(2)}) collective-permute-start(f32[2,2,104,128]{3,2,1,0:T(8,128)S(1)} %pad_maximum_fusion.after0_ref), channel_id=1, source_target_pairs={{12,0},{13,1},{14,2},{15,3},{8,4},{9,5},{10,6},{11,7},{4,8},{5,9},... | collective-permute-start | bytes 638984 | tf_op jit(solution)/shard_map/ppermute | solution.py:35
  30.8 9.1 %collective-permute-start.7 = (f32[2,2,104,128]{3,2,1,0:T(8,128)S(1)}, f32[2,2,104,128]{3,2,1,0:T(8,128)S(1)}, u32[]{:S(2)}, u32[]{:S(2)}) collective-permute-start(f32[2,2,104,128]{3,2,1,0:T(8,128)S(1)} %collective-permute-done.6.refs_4_), channel_id=1, source_target_pairs={{12,0},{13,1},{14,2},{15,3},{8,4},{9,5},{10,6},{11,7},{4,8},{5,9},... | collective-permute-start | bytes 638984 | tf_op jit(solution)/shard_map/ppermute | solution.py:35
  30.8 9.0 %collective-permute-start.8 = (f32[2,2,104,128]{3,2,1,0:T(8,128)S(1)}, f32[2,2,104,128]{3,2,1,0:T(8,128)S(1)}, u32[]{:S(2)}, u32[]{:S(2)}) collective-permute-start(f32[2,2,104,128]{3,2,1,0:T(8,128)S(1)} %collective-permute-done.5.refs_1_), channel_id=1, source_target_pairs={{4,0},{5,1},{6,2},{7,3},{0,4},{1,5},{2,6},{3,7},{12,8},{13,9},{14,... | collective-permute-start | bytes 638984 | tf_op jit(solution)/shard_map/ppermute | solution.py:35
  36.5 10.5 %copy-start.4 = (s32[768]{0:T(1024)S(1)}, s32[768]{0:T(1024)}, u32[]{:S(2)}) copy-start(s32[768]{0:T(1024)} %param.9) | copy-start | bytes 9220
  36.5 10.5 %copy-start.3 = (s32[768,4]{0,1:T(4,128)S(1)}, s32[768,4]{0,1:T(4,128)}, u32[]{:S(2)}) copy-start(s32[768,4]{0,1:T(4,128)} %param.8) | copy-start | bytes 36868
  42.6 5.2 %collective-permute-start.13 = (f32[1,768]{1,0:T(1,128)S(1)}, f32[1,768]{1,0:T(1,128)S(1)}, u32[]{:S(2)}, u32[]{:S(2)}) collective-permute-start(f32[1,768]{1,0:T(1,128)S(1)} %product.3.e0), channel_id=1, source_target_pairs={{1,0},{0,1},{3,2},{2,3},{5,4},{4,5},{7,6},{6,7},{9,8},{8,9},{11,10... | collective-permute-start | bytes 9224 | tf_op jit(solution)/shard_map/ppermute | solution.py:35
  44.4 3.6 %collective-permute-start.14 = (f32[1,768]{1,0:T(1,128)S(1)}, f32[1,768]{1,0:T(1,128)S(1)}, u32[]{:S(2)}, u32[]{:S(2)}) collective-permute-start(f32[1,768]{1,0:T(1,128)S(1)} %product.3.e0), channel_id=1, source_target_pairs={{2,0},{3,1},{0,2},{1,3},{6,4},{7,5},{4,6},{5,7},{10,8},{11,9},{8,1... | collective-permute-start | bytes 9224 | tf_op jit(solution)/shard_map/ppermute | solution.py:35
  47.0 3.0 %collective-permute-start.15 = (f32[1,768]{1,0:T(1,128)S(1)}, f32[1,768]{1,0:T(1,128)S(1)}, u32[]{:S(2)}, u32[]{:S(2)}) collective-permute-start(f32[1,768]{1,0:T(1,128)S(1)} %product.3.e0), channel_id=1, source_target_pairs={{3,0},{2,1},{1,2},{0,3},{7,4},{6,5},{5,6},{4,7},{11,8},{10,9},{9,1... | collective-permute-start | bytes 9224 | tf_op jit(solution)/shard_map/ppermute | solution.py:35
  50.3 10.1 %collective-permute-start.16 = (f32[2,3,128]{2,1,0:T(4,128)S(1)}, f32[2,3,128]{2,1,0:T(4,128)S(1)}, u32[]{:S(2)}, u32[]{:S(2)}) collective-permute-start(f32[2,3,128]{2,1,0:T(4,128)S(1)} %get-tuple-element.12), channel_id=1, source_target_pairs={{4,0},{6,2},{8,4},{1,5},{10,6},{3,7},{12,8},{5,9},{14,10},{7,11},{... | collective-permute-start | bytes 9224 | tf_op jit(solution)/shard_map/ppermute | solution.py:272
  60.4 1.2 %collective-permute-start.17 = (f32[3,128]{1,0:T(4,128)S(1)}, f32[3,128]{1,0:T(4,128)S(1)}, u32[]{:S(2)}, u32[]{:S(2)}) collective-permute-start(f32[3,128]{1,0:T(4,128)S(1)} %slice_bitcast_fusion), channel_id=1, source_target_pairs={{1,0},{0,1},{3,2},{2,3},{5,4},{4,5},{7,6},{6,7},{9,8},{8,9},{11,10... | collective-permute-start | bytes 4616 | tf_op jit(solution)/shard_map/ppermute | solution.py:35

commit v5 on v4

--- a/solution.py
+++ b/solution.py
@@ -10,7 +10,7 @@
 CELL_TILE = 512
 AXES = ("mesh", "tx")
 SIZE_Z, SIZE_Y = 8, 4
-TURNS = (0, 1, 2, 3)
+TURNS = (3, 2, 1, 0)
 ROWS = 104
 MIB = 1024 * 1024
 WHOLE = pl.BlockSpec(memory_space=pltpu.VMEM)
@@ -39,8 +39,7 @@
     for part in range(2):
         value = w_ref[part].T
         pieces = [value[100 * g : 100 * (g + 1), :] for g in range(4)]
-        o_ref[part, 0:100, :] = jnp.concatenate(pieces, axis=1)
-        o_ref[part, 100:ROWS, :] = jnp.zeros((ROWS - 100, 128), jnp.float32)
+        o_ref[100 * part : 100 * (part + 1), :] = jnp.concatenate(pieces, axis=1)
 
 
 def pack_weight(misfit_weight):
@@ -48,7 +47,7 @@
         pack_kernel,
         in_specs=[WHOLE],
         out_specs=WHOLE,
-        out_shape=jax.ShapeDtypeStruct((2, ROWS, 128), jnp.float32),
+        out_shape=jax.ShapeDtypeStruct((200, 128), jnp.float32),
         compiler_params=limit(2),
         name="pack_weight",
     )(misfit_weight.transpose(0, 2, 1))
@@ -60,16 +59,17 @@
     return high, low
 
 
-def prepare_kernel(place_ref, after_ref, rx_ref, o_ref):
+def prepare_kernel(place_ref, after_ref, rx_ref, early_ref, late_ref):
     for s in range(4):
         for k in range(4):
             row = pl.multiple_of(place_ref[k] * 128 + place_ref[4 + s] * 32, 32)
             real, imag = rx_ref[0, pl.ds(row, 32), :], rx_ref[1, pl.ds(row, 32), :]
-            rows = slice(128 * (s % 2) + 32 * k, 128 * (s % 2) + 32 * (k + 1))
+            out, first = (early_ref, 128 * s) if s < 2 else (late_ref, 128 * (s - 2))
+            rows = slice(first + 32 * k, first + 32 * (k + 1))
             for n, value in enumerate((real, imag - real, real + imag)):
                 high, low = split(value)
-                o_ref[s // 2, n, 0, rows, :] = low
-                o_ref[s // 2, n, 1, rows, :] = high
+                out[n, 0, rows, :] = low
+                out[n, 1, rows, :] = high
 
 
 def prepare_fields(places, after, rx_field):
@@ -77,8 +77,8 @@
     return pl.pallas_call(
         prepare_kernel,
         in_specs=[SCALARS, pl.BlockSpec(memory_space=pl.ANY), WHOLE],
-        out_specs=WHOLE,
-        out_shape=jax.ShapeDtypeStruct((2, 3, 2, 256, edges), jnp.bfloat16),
+        out_specs=(WHOLE, WHOLE),
+        out_shape=tuple(jax.ShapeDtypeStruct((3, 2, rows, edges), jnp.bfloat16) for rows in (256, 256)),
         compiler_params=limit(4),
         cost_estimate=pl.CostEstimate(flops=10_000_000, bytes_accessed=8_000_000, transcendentals=0),
         name="prepare_fields",
@@ -121,18 +121,21 @@
 
 
 def lane_group():
-    return lax.broadcasted_iota(jnp.int32, (ROWS, 128), 1) // 32
-
-
-def product_kernel(half, sources, index_ref, *refs):
+    return lax.broadcasted_iota(jnp.int32, (100, 128), 1) // 32
+
+
+def product_kernel(sources, index_ref, *refs):
     blocks, (tx, field, before, o_ref, w_scr, wh_scr, wl_scr) = refs[:-7], refs[-7:]
     tx_index = index_ref[0]
     group = lane_group()
+    for g in range(4):
+        w_scr[:, ROWS * g + 100 : ROWS * (g + 1), :] = jnp.zeros((2, ROWS - 100, w_scr.shape[2]), jnp.float32)
     for part in range(2):
-        for s in range(2):
+        for s in range(len(sources)):
             rolled = []
             for k, (ref, place) in enumerate(sources[s]):
-                block = blocks[ref][part] if place is None else blocks[ref][place, part]
+                rows = pl.ds(100 * part, 100)
+                block = blocks[ref][rows, :] if place is None else blocks[ref][place, rows, :]
                 rolled.append(pltpu.roll(block, 32 * k, 1) if k else block)
             for g in range(4):
                 mixed = rolled[(0 - g) % 4]
@@ -141,19 +144,20 @@
                 if g:
                     mixed = pltpu.roll(mixed, 128 - 32 * g, 1)
                 row = pl.multiple_of(jnp.bitwise_xor(tx_index, g) * ROWS, 8)
-                w_scr[part, pl.ds(row, ROWS), 128 * s : 128 * (s + 1)] = mixed
+                w_scr[part, pl.ds(row, 100), 128 * s : 128 * (s + 1)] = mixed
+    depth = 128 * len(sources)
     real, imag = w_scr[0], w_scr[1]
     for n, value in enumerate((real + imag, real, imag)):
         high, low = split(value)
-        wh_scr[n, :, 0:256] = high
-        wh_scr[n, :, 256:512] = high
+        wh_scr[n, :, 0:depth] = high
+        wh_scr[n, :, depth:] = high
         wl_scr[n] = low
-    for tile in range(field.shape[4] // 256):
+    for tile in range(field.shape[3] // 256):
         cols = slice(256 * tile, 256 * (tile + 1))
         products = []
         for n in range(3):
-            both = field[half, n, :, :, cols].reshape(512, 256)
-            high = field[half, n, 1, :, cols]
+            both = field[n, :, :, cols].reshape(2 * depth, 256)
+            high = field[n, 1, :, cols]
             products.append(
                 jnp.dot(wh_scr[n], both, preferred_element_type=jnp.float32)
                 + jnp.dot(wl_scr[n], high, preferred_element_type=jnp.float32)
@@ -163,16 +167,16 @@
         o_ref[:, cols] = before[:, cols] + jnp.sum(term, axis=0, keepdims=True)
 
 
-def product(half, sources, index, blocks, tx, fields, before):
-    edges = fields.shape[4]
-    return pl.pallas_call(
-        functools.partial(product_kernel, half, sources),
+def product(sources, index, blocks, tx, fields, before):
+    edges, depth = fields.shape[3], fields.shape[2]
+    return pl.pallas_call(
+        functools.partial(product_kernel, sources),
         in_specs=[SCALARS] + [WHOLE] * (len(blocks) + 3),
         out_specs=WHOLE,
         scratch_shapes=[
-            pltpu.VMEM((2, 4 * ROWS, 256), jnp.float32),
-            pltpu.VMEM((3, 4 * ROWS, 512), jnp.bfloat16),
-            pltpu.VMEM((3, 4 * ROWS, 256), jnp.bfloat16),
+            pltpu.VMEM((2, 4 * ROWS, depth), jnp.float32),
+            pltpu.VMEM((3, 4 * ROWS, 2 * depth), jnp.bfloat16),
+            pltpu.VMEM((3, 4 * ROWS, depth), jnp.bfloat16),
         ],
         out_shape=jax.ShapeDtypeStruct((1, edges), jnp.float32),
         compiler_params=limit(12),
@@ -182,7 +186,7 @@
 
 
 def onehot_kernel(index_ref, cells_ref, component_ref, hot_ref, row_ref):
-    x_lo, core, base = index_ref[1], index_ref[2], index_ref[3]
+    x_lo, core, base, send_x_lo = index_ref[1], index_ref[2], index_ref[3], index_ref[4]
     cells = cells_ref[...] - base
     edges = cells.shape[1]
     lanes = lax.broadcasted_iota(jnp.int32, (128, edges), 0)
@@ -191,7 +195,7 @@
         hot_ref[j] = jnp.where(hit, 1.0, 0.0).astype(jnp.bfloat16)
     block = cells >> 7
     row = component_ref[...] * 3
-    other = 8 * core + 2 * x_lo
+    other = 8 * core + 2 * send_x_lo
     row_ref[...] = jnp.where(
         block == 4 + 2 * x_lo + core,
         row,
@@ -267,8 +271,9 @@
     for m in range(64):
         for j in range(4):
             source = m + 1 if j % 2 == 0 else m - 1
+            flip = 2 if {m, source} == {31, 32} else 0
             if 0 <= source < 64:
-                route.append((source * 4 + j, m * 4 + j))
+                route.append((source * 4 + (j ^ flip), m * 4 + j))
     return lax.ppermute(block, AXES, route)
 
 
@@ -312,7 +317,10 @@
     from_z = [fetch(packed, z_source(turn)) for turn in TURNS]
     y_places = [y, y_partner(0, y), y_partner(1, y), (y + 2) % SIZE_Y]
     places = jnp.stack([(z % 4) ^ turn for turn in TURNS] + y_places).astype(jnp.int32)
-    index = jnp.stack([tx_index, tx_index // 2, tx_index % 2, (mesh_index - 1) * CELL_TILE]).astype(jnp.int32)
+    x_lo, core = tx_index // 2, tx_index % 2
+    flipped = mesh_index == jnp.where(core == 0, 32, 31)
+    send_x_lo = jnp.where(flipped, 1 - x_lo, x_lo)
+    index = jnp.stack([tx_index, x_lo, core, (mesh_index - 1) * CELL_TILE, send_x_lo]).astype(jnp.int32)
     hot, row = onehots(index, incidence, component)
 
     stacked = [jnp.stack(from_z[2 * g : 2 * g + 2]) for g in range(2)]
@@ -325,10 +333,10 @@
     fields = prepare_fields(places, stacked[1], rx_field)
     tx = collect(tx_own, tx_c, tx_x, tx_xc)
     edge = jnp.zeros((1, tx_field.shape[2]), jnp.float32)
-    early = [[(k, None) for k in range(4)], [(4, 0), (4, 1), (5, 0), (5, 1)]]
-    late = [[(0, 0), (0, 1), (1, 0), (1, 1)], [(2, 0), (2, 1), (3, 0), (3, 1)]]
-    edge = product(0, early, index, from_z + near, tx, fields, edge)
-    edge = product(1, late, index, far + last, tx, fields, edge)
+    pairs = lambda first: [(first, 0), (first, 1), (first + 1, 0), (first + 1, 1)]
+    early = [[(k, None) for k in range(4)], pairs(4)]
+    edge = product(early, index, from_z + near, tx, fields[0], edge)
+    edge = product([pairs(0), pairs(2)], index, far + last, tx, fields[1], edge)
     terms = [edge, fetch(edge, flip_core), fetch(edge, flip_x), fetch(edge, flip_both)]
     own, send = scatter(terms, hot, row)
     received = neighbour_parts(send)

time: 62.3 us -> 60.9 us (0.978)
  waiting for transfers between devices: 23.5 us -> 21.3 us
    ppermute x17, waiting for transfers between devices: 15.4 us -> 13.5 us  [fetch(): return lax.ppermute(block, AXES, route)]
  transfers between devices with their start and end apart: 18 -> 18, of which waited for: 10 -> 9; matrix products, arithmetic and copies ran while one was open for 0% -> 0% of each run, Pallas kernels for 9% -> 10%
where the time goes in v5:
time: 60.9 us; the launch traced here: 60.7 us
  starting transfers between devices  26.5 us (44%)
  waiting for transfers between devices  21.3 us (35%)
  Pallas kernels  9.66 us (16%)
  local copies, waits for them, and re-layouts  2.99 us (5%)
    ppermute x17, starting transfers between devices, fetch(): return lax.ppermute(block, AXES, route)  24.6 us
    ppermute x17, waiting for transfers between devices, fetch(): return lax.ppermute(block, AXES, route)  13.5 us
    ppermute x1, waiting for transfers between devices, neighbour_parts(): return lax.ppermute(block, AXES, route)  7.85 us
    pallas_call x2, Pallas kernels, product(): pl.pallas_call(functools.partial(product_kernel, sources), in_specs=[SCAL...  6 us
    unnamed x10, local copies, waits for them, and re-layouts  2.81 us
    ppermute x1, starting transfers between devices, neighbour_parts(): return lax.ppermute(block, AXES, route)  1.94 us
    pallas_call x1, Pallas kernels, prepare_fields(): pl.pallas_call(prepare_kernel, in_specs=[SCALARS, pl.BlockSpec(memory_spa...  1.23 us
  transfers between devices with their start and end apart: 18, of which 9 were waited for; matrix products, arithmetic and copies ran while one was open for 0% of the time, Pallas kernels for 10%

profile of v5, /device:TPU:7, one launch (start us, length us, event | category | flops | bytes accessed | tf_op | source)
XLA Modules:
  0.0 60.7 jit_solution(13404121419002949952)
XLA Ops:
  0.0 0.5 collective-permute-start.10
  0.6 0.9 %copy-done.2 = f32[2,400,32]{1,2,0:T(8,128)S(1)} copy-done((f32[2,400,32]{1,2,0:T(8,128)S(1)}, f32[2,400,32]{1,2,0:T(8,128)}, u32[]{:S(2)}) %copy-start.2) | copy-done | bytes 102424
  1.7 3.9 %collective-permute-start.1 = (f32[200,128]{1,0:T(8,128)S(1)}, f32[200,128]{1,0:T(8,128)S(1)}, u32[]{:S(2)}, u32[]{:S(2)}) collective-permute-start(f32[200,128]{1,0:T(8,128)S(1)} %pack_weight.1), channel_id=1, source_target_pairs={{33,0},{97,1},{161,2},{225,3},{37,4},{101,5},{165,6},{229,7},{41,8... | collective-permute-start | bytes 307208 | tf_op jit(solution)/shard_map/ppermute | solution.py:35
  5.7 4.9 %collective-permute-start = (f32[200,128]{1,0:T(8,128)S(1)}, f32[200,128]{1,0:T(8,128)S(1)}, u32[]{:S(2)}, u32[]{:S(2)}) collective-permute-start(f32[200,128]{1,0:T(8,128)S(1)} %pack_weight.1), channel_id=1, source_target_pairs={{49,0},{113,1},{177,2},{241,3},{53,4},{117,5},{181,6},{245,7},{57,... | collective-permute-start | bytes 307208 | tf_op jit(solution)/shard_map/ppermute | solution.py:35
  10.6 0.6 %collective-permute-start.3 = (f32[200,128]{1,0:T(8,128)S(1)}, f32[200,128]{1,0:T(8,128)S(1)}, u32[]{:S(2)}, u32[]{:S(2)}) collective-permute-start(f32[200,128]{1,0:T(8,128)S(1)} %pack_weight.1), channel_id=1, source_target_pairs={{17,0},{81,1},{145,2},{209,3},{21,4},{85,5},{149,6},{213,7},{25,8}... | collective-permute-start | bytes 307208 | tf_op jit(solution)/shard_map/ppermute | solution.py:35
  11.2 2.5 %collective-permute-start.9 = (f32[100,2,768]{2,1,0:T(2,128)}, f32[100,2,768]{2,1,0:T(2,128)S(1)}, u32[]{:S(2)}, u32[]{:S(2)}) collective-permute-start(f32[100,2,768]{2,1,0:T(2,128)} %bitcast.23), channel_id=1, source_target_pairs={{1,0},{0,1},{3,2},{2,3},{5,4},{4,5},{7,6},{6,7},{9,8},{8,9},{11,10... | collective-permute-start | bytes 1843208 | tf_op jit(solution)/shard_map/ppermute | solution.py:35
  14.2 5.2 %collective-permute-done.4.refs_3_ = f32[200,128]{1,0:T(8,128)S(1)} collective-permute-done((f32[200,128]{1,0:T(8,128)S(1)}, f32[200,128]{1,0:T(8,128)S(1)}, u32[]{:S(2)}, u32[]{:S(2)}) %collective-permute-start.4) | collective-permute-done | bytes 102432 | tf_op jit(solution)/shard_map/ppermute | solution.py:35
  19.5 2.8 %collective-permute-start.5 = (f32[2,200,128]{2,1,0:T(8,128)S(1)}, f32[2,200,128]{2,1,0:T(8,128)S(1)}, u32[]{:S(2)}, u32[]{:S(2)}) collective-permute-start(f32[2,200,128]{2,1,0:T(8,128)S(1)} %pad_maximum_fusion.1.after1_ref.after_ref), channel_id=1, source_target_pairs={{12,0},{13,1},{14,2},{15,3},{8,4},{9,5},{10,6},{11,7},{4,8},{5,9},... | collective-permute-start | bytes 614408 | tf_op jit(solution)/shard_map/ppermute | solution.py:35
  22.3 1.5 %collective-permute-start.12 = (f32[2,200,128]{2,1,0:T(8,128)S(1)}, f32[2,200,128]{2,1,0:T(8,128)}, u32[]{:S(2)}, u32[]{:S(2)}) collective-permute-start(f32[2,200,128]{2,1,0:T(8,128)S(1)} %pad_maximum_fusion.1.after1_ref.after_ref), channel_id=1, source_target_pairs={{4,0},{5,1},{6,2},{7,3},{0,4},{1,5},{2,6},{3,7},{12,8},{13,9},{14,... | collective-permute-start | bytes 614408 | tf_op jit(solution)/shard_map/ppermute | solution.py:35
  24.0 1.9 %copy-done = f32[2,512,768]{2,1,0:T(8,128)S(1)} copy-done((f32[2,512,768]{2,1,0:T(8,128)S(1)}, f32[2,512,768]{2,1,0:T(8,128)}, u32[]{:S(2)}) %copy-start) | copy-done | bytes 3145752
  25.9 1.2 %prepare_fields.1 = (bf16[3,2,256,768]{3,2,1,0:T(8,128)(2,1)S(1)}, bf16[3,2,256,768]{3,2,1,0:T(8,128)(2,1)S(1)}) custom-call(s32[8]{0:T(128)S(1)} %stack.83.place_ref, f32[2,200,128]{2,1,0:T(8,128)S(1)} %pad_maximum_fusion.1.after1_ref.after_ref, f32[2,512,768]{2,1,0:T(8,128)S(1)} %copy-done), custom_call_target="tpu_custom_call" | custom-call | flops 10000000 | bytes 8000000 | tf_op jit(solution)/shard_map/prepare_fields/pallas_call | solution.py:77
  27.2 2.6 %collective-permute-start.2 = (f32[2,200,128]{2,1,0:T(8,128)S(1)}, f32[2,200,128]{2,1,0:T(8,128)S(1)}, u32[]{:S(2)}, u32[]{:S(2)}) collective-permute-start(f32[2,200,128]{2,1,0:T(8,128)S(1)} %pad_maximum_fusion.after0_ref), channel_id=1, source_target_pairs={{12,0},{13,1},{14,2},{15,3},{8,4},{9,5},{10,6},{11,7},{4,8},{5,9},... | collective-permute-start | bytes 614408 | tf_op jit(solution)/shard_map/ppermute | solution.py:35
  30.7 2.1 %collective-permute-done.12.refs_5_ = f32[2,200,128]{2,1,0:T(8,128)} collective-permute-done((f32[2,200,128]{2,1,0:T(8,128)S(1)}, f32[2,200,128]{2,1,0:T(8,128)}, u32[]{:S(2)}, u32[]{:S(2)}) %collective-permute-start.12) | collective-permute-done | bytes 204832 | tf_op jit(solution)/shard_map/ppermute | solution.py:35
  32.8 3.2 %product.2.refs_6_ = f32[1,768]{1,0:T(1,128)S(1)} custom-call(s32[5]{0:T(128)S(1)} %stack.68.index_ref, f32[200,128]{1,0:T(8,128)S(1)} %collective-permute-done.refs_0_, f32[200,128]{1,0:T(8,128)S(1)} %collective-permute-done.1.refs_1_, f32[200,128]{1,0:T(8,128)S(1)} %collective-permute-done.3.refs_2_, f32[200,128]{1,0:T(8,128)S(1)} %collective-permute-done.4.refs_3_, ...), custom_call_target="tpu_custom_call" | custom-call | flops 3000000000 | bytes 6000000 | tf_op jit(solution)/shard_map/product/pallas_call | solution.py:172
  36.0 2.3 %collective-permute-done.7.refs_2_ = f32[2,200,128]{2,1,0:T(8,128)S(1)} collective-permute-done((f32[2,200,128]{2,1,0:T(8,128)}, f32[2,200,128]{2,1,0:T(8,128)S(1)}, u32[]{:S(2)}, u32[]{:S(2)}) %collective-permute-start.7) | collective-permute-done | bytes 204832 | tf_op jit(solution)/shard_map/ppermute | solution.py:35
  38.3 2.8 %product.3.e0 = f32[1,768]{1,0:T(1,128)S(1)} custom-call(s32[5]{0:T(128)S(1)} %stack.68.index_ref, f32[2,200,128]{2,1,0:T(8,128)S(1)} %collective-permute-done.2.refs_0_, f32[2,200,128]{2,1,0:T(8,128)S(1)} %collective-permute-done.5.refs_1_, f32[2,200,128]{2,1,0:T(8,128)S(1)} %collective-permute-done.7.refs_2_, ...), custom_call_target="tpu_custom_call" | custom-call | flops 3000000000 | bytes 6000000 | tf_op jit(solution)/shard_map/product/pallas_call | solution.py:172
  41.1 2.1 %collective-permute-start.13 = (f32[1,768]{1,0:T(1,128)S(1)}, f32[1,768]{1,0:T(1,128)S(1)}, u32[]{:S(2)}, u32[]{:S(2)}) collective-permute-start(f32[1,768]{1,0:T(1,128)S(1)} %product.3.e0), channel_id=1, source_target_pairs={{1,0},{0,1},{3,2},{2,3},{5,4},{4,5},{7,6},{6,7},{9,8},{8,9},{11,10... | collective-permute-start | bytes 9224 | tf_op jit(solution)/shard_map/ppermute | solution.py:35
  43.1 2.7 %collective-permute-start.14 = (f32[1,768]{1,0:T(1,128)S(1)}, f32[1,768]{1,0:T(1,128)S(1)}, u32[]{:S(2)}, u32[]{:S(2)}) collective-permute-start(f32[1,768]{1,0:T(1,128)S(1)} %product.3.e0), channel_id=1, source_target_pairs={{2,0},{3,1},{0,2},{1,3},{6,4},{7,5},{4,6},{5,7},{10,8},{11,9},{8,1... | collective-permute-start | bytes 9224 | tf_op jit(solution)/shard_map/ppermute | solution.py:35
  45.9 0.7 %onehots.1 = (bf16[4,128,768]{2,1,0:T(8,128)(2,1)S(1)}, s32[4,768]{1,0:T(4,128)S(1)}) custom-call(s32[5]{0:T(128)S(1)} %stack.68.index_ref, s32[4,768]{1,0:T(4,128)S(1)} %bitcast.30, s32[1,768]{1,0:T(1,128)S(1)} %broadcast_in_dim.7.component_ref), custom_call_target="tpu_custom_call" | custom-call | tf_op jit(solution)/shard_map/onehots/pallas_call | solution.py:208
  46.8 2.1 %collective-permute-done.15.e3 = f32[1,768]{1,0:T(1,128)S(1)} collective-permute-done((f32[1,768]{1,0:T(1,128)S(1)}, f32[1,768]{1,0:T(1,128)S(1)}, u32[]{:S(2)}, u32[]{:S(2)}) %collective-permute-start.15) | collective-permute-done | bytes 3104 | tf_op jit(solution)/shard_map/ppermute | solution.py:35
  49.2 1.9 %collective-permute-start.16 = (f32[2,3,128]{2,1,0:T(4,128)S(1)}, f32[2,3,128]{2,1,0:T(4,128)S(1)}, u32[]{:S(2)}, u32[]{:S(2)}) collective-permute-start(f32[2,3,128]{2,1,0:T(4,128)S(1)} %get-tuple-element.16), channel_id=1, source_target_pairs={{4,0},{6,2},{8,4},{1,5},{10,6},{3,7},{12,8},{5,9},{14,10},{7,11},{... | collective-permute-start | bytes 9224 | tf_op jit(solution)/shard_map/ppermute | solution.py:277
  51.1 7.9 %collective-permute-done.16.received_ref = f32[2,3,128]{2,1,0:T(4,128)S(1)} collective-permute-done((f32[2,3,128]{2,1,0:T(4,128)S(1)}, f32[2,3,128]{2,1,0:T(4,128)S(1)}, u32[]{:S(2)}, u32[]{:S(2)}) %collective-permute-start.16) | collective-permute-done | bytes 3104 | tf_op jit(solution)/shard_map/ppermute | solution.py:277
  59.0 1.2 %collective-permute-done.17.passed_ref = f32[3,128]{1,0:T(4,128)S(1)} collective-permute-done((f32[3,128]{1,0:T(4,128)S(1)}, f32[3,128]{1,0:T(4,128)S(1)}, u32[]{:S(2)}, u32[]{:S(2)}) %collective-permute-start.17) | collective-permute-done | bytes 1568 | tf_op jit(solution)/shard_map/ppermute | solution.py:35
  60.1 0.6 total.1
  (38 shorter events, 2.5 us)
Async XLA Ops:
  0.0 19.4 %collective-permute-start.10 = (f32[100,2,768]{2,1,0:T(2,128)}, f32[100,2,768]{2,1,0:T(2,128)S(1)}, u32[]{:S(2)}, u32[]{:S(2)}) collective-permute-start(f32[100,2,768]{2,1,0:T(2,128)} %bitcast.22), channel_id=1, source_target_pairs={{2,0},{3,1},{0,2},{1,3},{6,4},{7,5},{4,6},{5,7},{10,8},{11,9},{8,1... | collective-permute-start | bytes 1843208 | tf_op jit(solution)/shard_map/ppermute | solution.py:35
  0.5 0.9 %copy-start.2 = (f32[2,400,32]{1,2,0:T(8,128)S(1)}, f32[2,400,32]{1,2,0:T(8,128)}, u32[]{:S(2)}) copy-start(f32[2,400,32]{1,2,0:T(8,128)} %param.7) | copy-start | bytes 307204
  1.7 9.5 %collective-permute-start.1 = (f32[200,128]{1,0:T(8,128)S(1)}, f32[200,128]{1,0:T(8,128)S(1)}, u32[]{:S(2)}, u32[]{:S(2)}) collective-permute-start(f32[200,128]{1,0:T(8,128)S(1)} %pack_weight.1), channel_id=1, source_target_pairs={{33,0},{97,1},{161,2},{225,3},{37,4},{101,5},{165,6},{229,7},{41,8... | collective-permute-start | bytes 307208 | tf_op jit(solution)/shard_map/ppermute | solution.py:35
  5.7 8.5 %collective-permute-start = (f32[200,128]{1,0:T(8,128)S(1)}, f32[200,128]{1,0:T(8,128)S(1)}, u32[]{:S(2)}, u32[]{:S(2)}) collective-permute-start(f32[200,128]{1,0:T(8,128)S(1)} %pack_weight.1), channel_id=1, source_target_pairs={{49,0},{113,1},{177,2},{241,3},{53,4},{117,5},{181,6},{245,7},{57,... | collective-permute-start | bytes 307208 | tf_op jit(solution)/shard_map/ppermute | solution.py:35
  10.6 8.8 %collective-permute-start.4 = (f32[200,128]{1,0:T(8,128)S(1)}, f32[200,128]{1,0:T(8,128)S(1)}, u32[]{:S(2)}, u32[]{:S(2)}) collective-permute-start(f32[200,128]{1,0:T(8,128)S(1)} %pack_weight.1), channel_id=1, source_target_pairs={{1,0},{65,1},{129,2},{193,3},{5,4},{69,5},{133,6},{197,7},{9,8},{7... | collective-permute-start | bytes 307208 | tf_op jit(solution)/shard_map/ppermute | solution.py:35
  10.6 8.8 %collective-permute-start.3 = (f32[200,128]{1,0:T(8,128)S(1)}, f32[200,128]{1,0:T(8,128)S(1)}, u32[]{:S(2)}, u32[]{:S(2)}) collective-permute-start(f32[200,128]{1,0:T(8,128)S(1)} %pack_weight.1), channel_id=1, source_target_pairs={{17,0},{81,1},{145,2},{209,3},{21,4},{85,5},{149,6},{213,7},{25,8}... | collective-permute-start | bytes 307208 | tf_op jit(solution)/shard_map/ppermute | solution.py:35
  11.2 18.6 %collective-permute-start.9 = (f32[100,2,768]{2,1,0:T(2,128)}, f32[100,2,768]{2,1,0:T(2,128)S(1)}, u32[]{:S(2)}, u32[]{:S(2)}) collective-permute-start(f32[100,2,768]{2,1,0:T(2,128)} %bitcast.23), channel_id=1, source_target_pairs={{1,0},{0,1},{3,2},{2,3},{5,4},{4,5},{7,6},{6,7},{9,8},{8,9},{11,10... | collective-permute-start | bytes 1843208 | tf_op jit(solution)/shard_map/ppermute | solution.py:35
  19.4 10.7 %copy-start.1 = (f32[2,100,768]{2,0,1:T(2,128)S(1)}, f32[2,100,768]{2,0,1:T(2,128)}, u32[]{:S(2)}) copy-start(f32[2,100,768]{2,0,1:T(2,128)} %param.5) | copy-start | bytes 1843204
  19.4 10.7 %collective-permute-start.11 = (f32[100,2,768]{2,1,0:T(2,128)S(1)}, f32[100,2,768]{2,1,0:T(2,128)S(1)}, u32[]{:S(2)}, u32[]{:S(2)}) collective-permute-start(f32[100,2,768]{2,1,0:T(2,128)S(1)} %gate.1.flipped_ref), channel_id=1, source_target_pairs={{1,0},{0,1},{3,2},{2,3},{5,4},{4,5},{7,6},{6,7},{9,8},{8,9},{11,10... | collective-permute-start | bytes 1843208 | tf_op jit(solution)/shard_map/ppermute | solution.py:35
  19.5 7.7 %collective-permute-start.5 = (f32[2,200,128]{2,1,0:T(8,128)S(1)}, f32[2,200,128]{2,1,0:T(8,128)S(1)}, u32[]{:S(2)}, u32[]{:S(2)}) collective-permute-start(f32[2,200,128]{2,1,0:T(8,128)S(1)} %pad_maximum_fusion.1.after1_ref.after_ref), channel_id=1, source_target_pairs={{12,0},{13,1},{14,2},{15,3},{8,4},{9,5},{10,6},{11,7},{4,8},{5,9},... | collective-permute-start | bytes 614408 | tf_op jit(solution)/shard_map/ppermute | solution.py:35
  22.3 7.5 %collective-permute-start.6 = (f32[2,200,128]{2,1,0:T(8,128)S(1)}, f32[2,200,128]{2,1,0:T(8,128)}, u32[]{:S(2)}, u32[]{:S(2)}) collective-permute-start(f32[2,200,128]{2,1,0:T(8,128)S(1)} %pad_maximum_fusion.after0_ref), channel_id=1, source_target_pairs={{4,0},{5,1},{6,2},{7,3},{0,4},{1,5},{2,6},{3,7},{12,8},{13,9},{14,... | collective-permute-start | bytes 614408 | tf_op jit(solution)/shard_map/ppermute | solution.py:35
  22.3 10.4 %collective-permute-start.12 = (f32[2,200,128]{2,1,0:T(8,128)S(1)}, f32[2,200,128]{2,1,0:T(8,128)}, u32[]{:S(2)}, u32[]{:S(2)}) collective-permute-start(f32[2,200,128]{2,1,0:T(8,128)S(1)} %pad_maximum_fusion.1.after1_ref.after_ref), channel_id=1, source_target_pairs={{4,0},{5,1},{6,2},{7,3},{0,4},{1,5},{2,6},{3,7},{12,8},{13,9},{14,... | collective-permute-start | bytes 614408 | tf_op jit(solution)/shard_map/ppermute | solution.py:35
  24.0 1.9 %copy-start = (f32[2,512,768]{2,1,0:T(8,128)S(1)}, f32[2,512,768]{2,1,0:T(8,128)}, u32[]{:S(2)}) copy-start(f32[2,512,768]{2,1,0:T(8,128)} %rx_ref.1) | copy-start | bytes 9437188
  27.2 8.8 %collective-permute-start.2 = (f32[2,200,128]{2,1,0:T(8,128)S(1)}, f32[2,200,128]{2,1,0:T(8,128)S(1)}, u32[]{:S(2)}, u32[]{:S(2)}) collective-permute-start(f32[2,200,128]{2,1,0:T(8,128)S(1)} %pad_maximum_fusion.after0_ref), channel_id=1, source_target_pairs={{12,0},{13,1},{14,2},{15,3},{8,4},{9,5},{10,6},{11,7},{4,8},{5,9},... | collective-permute-start | bytes 614408 | tf_op jit(solution)/shard_map/ppermute | solution.py:35
  29.8 8.5 %collective-permute-start.7 = (f32[2,200,128]{2,1,0:T(8,128)}, f32[2,200,128]{2,1,0:T(8,128)S(1)}, u32[]{:S(2)}, u32[]{:S(2)}) collective-permute-start(f32[2,200,128]{2,1,0:T(8,128)} %collective-permute-done.6.refs_4_), channel_id=1, source_target_pairs={{12,0},{13,1},{14,2},{15,3},{8,4},{9,5},{10,6},{11,7},{4,8},{5,9},... | collective-permute-start | bytes 614408 | tf_op jit(solution)/shard_map/ppermute | solution.py:35
  29.9 8.4 %collective-permute-start.8 = (f32[2,200,128]{2,1,0:T(8,128)S(1)}, f32[2,200,128]{2,1,0:T(8,128)S(1)}, u32[]{:S(2)}, u32[]{:S(2)}) collective-permute-start(f32[2,200,128]{2,1,0:T(8,128)S(1)} %collective-permute-done.5.refs_1_), channel_id=1, source_target_pairs={{4,0},{5,1},{6,2},{7,3},{0,4},{1,5},{2,6},{3,7},{12,8},{13,9},{14,... | collective-permute-start | bytes 614408 | tf_op jit(solution)/shard_map/ppermute | solution.py:35
  38.3 7.6 %copy-start.4 = (s32[768]{0:T(1024)S(1)}, s32[768]{0:T(1024)}, u32[]{:S(2)}) copy-start(s32[768]{0:T(1024)} %param.9) | copy-start | bytes 9220
  38.3 7.6 %copy-start.3 = (s32[768,4]{0,1:T(4,128)S(1)}, s32[768,4]{0,1:T(4,128)}, u32[]{:S(2)}) copy-start(s32[768,4]{0,1:T(4,128)} %param.8) | copy-start | bytes 36868
  41.1 5.5 %collective-permute-start.13 = (f32[1,768]{1,0:T(1,128)S(1)}, f32[1,768]{1,0:T(1,128)S(1)}, u32[]{:S(2)}, u32[]{:S(2)}) collective-permute-start(f32[1,768]{1,0:T(1,128)S(1)} %product.3.e0), channel_id=1, source_target_pairs={{1,0},{0,1},{3,2},{2,3},{5,4},{4,5},{7,6},{6,7},{9,8},{8,9},{11,10... | collective-permute-start | bytes 9224 | tf_op jit(solution)/shard_map/ppermute | solution.py:35
  43.1 3.6 %collective-permute-start.14 = (f32[1,768]{1,0:T(1,128)S(1)}, f32[1,768]{1,0:T(1,128)S(1)}, u32[]{:S(2)}, u32[]{:S(2)}) collective-permute-start(f32[1,768]{1,0:T(1,128)S(1)} %product.3.e0), channel_id=1, source_target_pairs={{2,0},{3,1},{0,2},{1,3},{6,4},{7,5},{4,6},{5,7},{10,8},{11,9},{8,1... | collective-permute-start | bytes 9224 | tf_op jit(solution)/shard_map/ppermute | solution.py:35
  45.8 3.0 %collective-permute-start.15 = (f32[1,768]{1,0:T(1,128)S(1)}, f32[1,768]{1,0:T(1,128)S(1)}, u32[]{:S(2)}, u32[]{:S(2)}) collective-permute-start(f32[1,768]{1,0:T(1,128)S(1)} %product.3.e0), channel_id=1, source_target_pairs={{3,0},{2,1},{1,2},{0,3},{7,4},{6,5},{5,6},{4,7},{11,8},{10,9},{9,1... | collective-permute-start | bytes 9224 | tf_op jit(solution)/shard_map/ppermute | solution.py:35
  49.2 9.8 %collective-permute-start.16 = (f32[2,3,128]{2,1,0:T(4,128)S(1)}, f32[2,3,128]{2,1,0:T(4,128)S(1)}, u32[]{:S(2)}, u32[]{:S(2)}) collective-permute-start(f32[2,3,128]{2,1,0:T(4,128)S(1)} %get-tuple-element.16), channel_id=1, source_target_pairs={{4,0},{6,2},{8,4},{1,5},{10,6},{3,7},{12,8},{5,9},{14,10},{7,11},{... | collective-permute-start | bytes 9224 | tf_op jit(solution)/shard_map/ppermute | solution.py:277
  59.0 1.2 %collective-permute-start.17 = (f32[3,128]{1,0:T(4,128)S(1)}, f32[3,128]{1,0:T(4,128)S(1)}, u32[]{:S(2)}, u32[]{:S(2)}) collective-permute-start(f32[3,128]{1,0:T(4,128)S(1)} %slice_bitcast_fusion), channel_id=1, source_target_pairs={{1,0},{0,1},{3,2},{2,3},{5,4},{4,5},{7,6},{6,7},{9,8},{8,9},{11,10... | collective-permute-start | bytes 4616 | tf_op jit(solution)/shard_map/ppermute | solution.py:35

commit v6 on v5

--- a/solution.py
+++ b/solution.py
@@ -10,7 +10,8 @@
 CELL_TILE = 512
 AXES = ("mesh", "tx")
 SIZE_Z, SIZE_Y = 8, 4
-TURNS = (3, 2, 1, 0)
+FAR_TURNS = (3, 2, 0, 1)
+NEAR_TURNS = (3, 2, 0, 1)
 ROWS = 104
 MIB = 1024 * 1024
 WHOLE = pl.BlockSpec(memory_space=pltpu.VMEM)
@@ -59,10 +60,11 @@
     return high, low
 
 
-def prepare_kernel(place_ref, after_ref, rx_ref, early_ref, late_ref):
+def prepare_kernel(place_ref, rx_ref, early_ref, late_ref):
     for s in range(4):
         for k in range(4):
-            row = pl.multiple_of(place_ref[k] * 128 + place_ref[4 + s] * 32, 32)
+            turned = 3 - s if s in (1, 2) and k >= 2 else s
+            row = pl.multiple_of(place_ref[k] * 128 + place_ref[4 + turned] * 32, 32)
             real, imag = rx_ref[0, pl.ds(row, 32), :], rx_ref[1, pl.ds(row, 32), :]
             out, first = (early_ref, 128 * s) if s < 2 else (late_ref, 128 * (s - 2))
             rows = slice(first + 32 * k, first + 32 * (k + 1))
@@ -72,20 +74,20 @@
                 out[n, 1, rows, :] = high
 
 
-def prepare_fields(places, after, rx_field):
+def prepare_fields(places, rx_field):
     edges = rx_field.shape[2]
     return pl.pallas_call(
         prepare_kernel,
-        in_specs=[SCALARS, pl.BlockSpec(memory_space=pl.ANY), WHOLE],
+        in_specs=[SCALARS, WHOLE],
         out_specs=(WHOLE, WHOLE),
         out_shape=tuple(jax.ShapeDtypeStruct((3, 2, rows, edges), jnp.bfloat16) for rows in (256, 256)),
         compiler_params=limit(4),
         cost_estimate=pl.CostEstimate(flops=10_000_000, bytes_accessed=8_000_000, transcendentals=0),
         name="prepare_fields",
-    )(places, after, rx_field)
-
-
-def gate_kernel(after0_ref, after1_ref, value_ref, o_ref):
+    )(places, rx_field)
+
+
+def gate_kernel(*refs):
     pass
 
 
@@ -93,10 +95,10 @@
     anywhere = pl.BlockSpec(memory_space=pl.ANY)
     return pl.pallas_call(
         gate_kernel,
-        in_specs=[anywhere] * 3,
+        in_specs=[anywhere] * (len(after) + 1),
         out_specs=anywhere,
         out_shape=jax.ShapeDtypeStruct(value.shape, value.dtype),
-        input_output_aliases={2: 0},
+        input_output_aliases={len(after): 0},
         compiler_params=limit(2),
         name="gate",
     )(*after, value)
@@ -289,14 +291,13 @@
     return x_hi, z, y, 1 - x_lo, 1 - core
 
 
-def z_source(turn):
-    return lambda x_hi, z, y, x_lo, core: (
-        x_lo,
-        4 * core + ((z % 4) ^ turn),
-        y,
-        x_hi,
-        1 - core if z // 4 == core else core,
-    )
+def z_source(k):
+    def source(x_hi, z, y, x_lo, core):
+        if z // 4 == core:
+            return x_lo, 4 * core + ((z % 4) ^ NEAR_TURNS[k]), y, x_hi, 1 - core
+        return x_lo, 4 * core + ((z % 4) ^ FAR_TURNS[k]), y, x_hi, core
+
+    return source
 
 
 def y_partner(pairs, y):
@@ -314,9 +315,11 @@
     packed = pack_weight(misfit_weight)
     tx_own = tx_field.transpose(1, 0, 2)
     tx_x = fetch(tx_own, flip_x)
-    from_z = [fetch(packed, z_source(turn)) for turn in TURNS]
+    from_z = [fetch(packed, z_source(k)) for k in range(4)]
     y_places = [y, y_partner(0, y), y_partner(1, y), (y + 2) % SIZE_Y]
-    places = jnp.stack([(z % 4) ^ turn for turn in TURNS] + y_places).astype(jnp.int32)
+    same_half = z // 4 == tx_index % 2
+    z_places = [(z % 4) ^ jnp.where(same_half, NEAR_TURNS[k], FAR_TURNS[k]) for k in range(4)]
+    places = jnp.stack(z_places + y_places).astype(jnp.int32)
     x_lo, core = tx_index // 2, tx_index % 2
     flipped = mesh_index == jnp.where(core == 0, 32, 31)
     send_x_lo = jnp.where(flipped, 1 - x_lo, x_lo)
@@ -330,13 +333,13 @@
     near = [fetch(stacked[g], y_source(0)) for g in range(2)]
     far = [fetch(stacked[g], y_source(1)) for g in range(2)]
     last = [fetch(near[0], y_source(1)), fetch(far[1], y_source(0))]
-    fields = prepare_fields(places, stacked[1], rx_field)
+    fields = prepare_fields(places, rx_field)
     tx = collect(tx_own, tx_c, tx_x, tx_xc)
     edge = jnp.zeros((1, tx_field.shape[2]), jnp.float32)
     pairs = lambda first: [(first, 0), (first, 1), (first + 1, 0), (first + 1, 1)]
     early = [[(k, None) for k in range(4)], pairs(4)]
-    edge = product(early, index, from_z + near, tx, fields[0], edge)
-    edge = product([pairs(0), pairs(2)], index, far + last, tx, fields[1], edge)
+    edge = product(early, index, from_z + [near[0], far[1]], tx, fields[0], edge)
+    edge = product([pairs(0), pairs(2)], index, [far[0], near[1]] + last, tx, fields[1], edge)
     terms = [edge, fetch(edge, flip_core), fetch(edge, flip_x), fetch(edge, flip_both)]
     own, send = scatter(terms, hot, row)
     received = neighbour_parts(send)

time: 60.9 us -> 59.2 us (0.972)
  starting transfers between devices: 26.5 us -> 24.5 us
    ppermute x17, starting transfers between devices: 24.6 us -> 22.6 us  [fetch(): return lax.ppermute(block, AXES, route)]
where the time goes in v6:
time: 59.2 us; the launch traced here: 59 us
  starting transfers between devices  24.5 us (41%)
  waiting for transfers between devices  21.7 us (37%)
  Pallas kernels  9.56 us (16%)
  local copies, waits for them, and re-layouts  2.99 us (5%)
    ppermute x17, starting transfers between devices, fetch(): return lax.ppermute(block, AXES, route)  22.6 us
    ppermute x17, waiting for transfers between devices, fetch(): return lax.ppermute(block, AXES, route)  13.9 us
    ppermute x1, waiting for transfers between devices, neighbour_parts(): return lax.ppermute(block, AXES, route)  7.85 us
    pallas_call x2, Pallas kernels, product(): pl.pallas_call(functools.partial(product_kernel, sources), in_specs=[SCAL...  5.9 us
    unnamed x10, local copies, waits for them, and re-layouts  2.81 us
    ppermute x1, starting transfers between devices, neighbour_parts(): return lax.ppermute(block, AXES, route)  1.94 us
    pallas_call x1, Pallas kernels, prepare_fields(): pl.pallas_call(prepare_kernel, in_specs=[SCALARS, WHOLE], out_specs=(WHOL...  1.23 us
  transfers between devices with their start and end apart: 18, of which 9 were waited for; matrix products, arithmetic and copies ran while one was open for 0% of the time, Pallas kernels for 10%

profile of v6, /device:TPU:7, one launch (start us, length us, event | category | flops | bytes accessed | tf_op | source)
XLA Modules:
  0.0 59.0 jit_solution(17062455724044657207)
XLA Ops:
  0.6 0.9 %copy-done.2 = f32[2,400,32]{1,2,0:T(8,128)S(1)} copy-done((f32[2,400,32]{1,2,0:T(8,128)S(1)}, f32[2,400,32]{1,2,0:T(8,128)}, u32[]{:S(2)}) %copy-start.2) | copy-done | bytes 102424
  1.7 3.9 %collective-permute-start.1 = (f32[200,128]{1,0:T(8,128)S(1)}, f32[200,128]{1,0:T(8,128)S(1)}, u32[]{:S(2)}, u32[]{:S(2)}) collective-permute-start(f32[200,128]{1,0:T(8,128)S(1)} %pack_weight.1), channel_id=1, source_target_pairs={{33,0},{97,1},{161,2},{225,3},{37,4},{101,5},{165,6},{229,7},{41,8... | collective-permute-start | bytes 307208 | tf_op jit(solution)/shard_map/ppermute | solution.py:36
  5.7 4.9 %collective-permute-start = (f32[200,128]{1,0:T(8,128)S(1)}, f32[200,128]{1,0:T(8,128)S(1)}, u32[]{:S(2)}, u32[]{:S(2)}) collective-permute-start(f32[200,128]{1,0:T(8,128)S(1)} %pack_weight.1), channel_id=1, source_target_pairs={{49,0},{113,1},{177,2},{241,3},{53,4},{117,5},{181,6},{245,7},{57,... | collective-permute-start | bytes 307208 | tf_op jit(solution)/shard_map/ppermute | solution.py:36
  10.8 1.5 %collective-permute-start.10 = (f32[100,2,768]{2,1,0:T(2,128)}, f32[100,2,768]{2,1,0:T(2,128)S(1)}, u32[]{:S(2)}, u32[]{:S(2)}) collective-permute-start(f32[100,2,768]{2,1,0:T(2,128)} %bitcast.23), channel_id=1, source_target_pairs={{1,0},{0,1},{3,2},{2,3},{5,4},{4,5},{7,6},{6,7},{9,8},{8,9},{11,10... | collective-permute-start | bytes 1843208 | tf_op jit(solution)/shard_map/ppermute | solution.py:36
  12.3 1.2 %collective-permute-done.refs_0_ = f32[200,128]{1,0:T(8,128)S(1)} collective-permute-done((f32[200,128]{1,0:T(8,128)S(1)}, f32[200,128]{1,0:T(8,128)S(1)}, u32[]{:S(2)}, u32[]{:S(2)}) %collective-permute-start) | collective-permute-done | bytes 102432 | tf_op jit(solution)/shard_map/ppermute | solution.py:36
  13.5 3.8 %collective-permute-done.4.refs_3_ = f32[200,128]{1,0:T(8,128)S(1)} collective-permute-done((f32[200,128]{1,0:T(8,128)S(1)}, f32[200,128]{1,0:T(8,128)S(1)}, u32[]{:S(2)}, u32[]{:S(2)}) %collective-permute-start.4) | collective-permute-done | bytes 102432 | tf_op jit(solution)/shard_map/ppermute | solution.py:36
  17.2 1.1 %collective-permute-done.3.refs_2_ = f32[200,128]{1,0:T(8,128)S(1)} collective-permute-done((f32[200,128]{1,0:T(8,128)S(1)}, f32[200,128]{1,0:T(8,128)S(1)}, u32[]{:S(2)}, u32[]{:S(2)}) %collective-permute-start.3) | collective-permute-done | bytes 102432 | tf_op jit(solution)/shard_map/ppermute | solution.py:36
  18.4 0.7 %collective-permute-start.12 = (f32[100,2,768]{2,1,0:T(2,128)S(1)}, f32[100,2,768]{2,1,0:T(2,128)S(1)}, u32[]{:S(2)}, u32[]{:S(2)}) collective-permute-start(f32[100,2,768]{2,1,0:T(2,128)S(1)} %gate.1.flipped_ref), channel_id=1, source_target_pairs={{1,0},{0,1},{3,2},{2,3},{5,4},{4,5},{7,6},{6,7},{9,8},{8,9},{11,10... | collective-permute-start | bytes 1843208 | tf_op jit(solution)/shard_map/ppermute | solution.py:36
  19.1 1.3 %collective-permute-start.6 = (f32[2,200,128]{2,1,0:T(8,128)S(1)}, f32[2,200,128]{2,1,0:T(8,128)S(1)}, u32[]{:S(2)}, u32[]{:S(2)}) collective-permute-start(f32[2,200,128]{2,1,0:T(8,128)S(1)} %pad_maximum_fusion.refs_0_), channel_id=1, source_target_pairs={{4,0},{5,1},{6,2},{7,3},{0,4},{1,5},{2,6},{3,7},{12,8},{13,9},{14,... | collective-permute-start | bytes 614408 | tf_op jit(solution)/shard_map/ppermute | solution.py:36
  20.4 1.9 %collective-permute-start.8 = (f32[2,200,128]{2,1,0:T(8,128)S(1)}, f32[2,200,128]{2,1,0:T(8,128)}, u32[]{:S(2)}, u32[]{:S(2)}) collective-permute-start(f32[2,200,128]{2,1,0:T(8,128)S(1)} %pad_maximum_fusion.1.refs_1_), channel_id=1, source_target_pairs={{12,0},{13,1},{14,2},{15,3},{8,4},{9,5},{10,6},{11,7},{4,8},{5,9},... | collective-permute-start | bytes 614408 | tf_op jit(solution)/shard_map/ppermute | solution.py:36
  22.5 1.9 %copy-done = f32[2,512,768]{2,1,0:T(8,128)S(1)} copy-done((f32[2,512,768]{2,1,0:T(8,128)S(1)}, f32[2,512,768]{2,1,0:T(8,128)}, u32[]{:S(2)}) %copy-start) | copy-done | bytes 3145752
  24.4 1.2 %prepare_fields.1 = (bf16[3,2,256,768]{3,2,1,0:T(8,128)(2,1)S(1)}, bf16[3,2,256,768]{3,2,1,0:T(8,128)(2,1)S(1)}) custom-call(s32[8]{0:T(128)S(1)} %stack.83.place_ref, f32[2,512,768]{2,1,0:T(8,128)S(1)} %copy-done), custom_call_target="tpu_custom_call" | custom-call | flops 10000000 | bytes 8000000 | tf_op jit(solution)/shard_map/prepare_fields/pallas_call | solution.py:79
  25.6 0.9 %collective-permute-start.2 = (f32[2,200,128]{2,1,0:T(8,128)S(1)}, f32[2,200,128]{2,1,0:T(8,128)S(1)}, u32[]{:S(2)}, u32[]{:S(2)}) collective-permute-start(f32[2,200,128]{2,1,0:T(8,128)S(1)} %pad_maximum_fusion.refs_0_), channel_id=1, source_target_pairs={{12,0},{13,1},{14,2},{15,3},{8,4},{9,5},{10,6},{11,7},{4,8},{5,9},... | collective-permute-start | bytes 614408 | tf_op jit(solution)/shard_map/ppermute | solution.py:36
  27.2 0.9 %collective-permute-done.8.refs_5_ = f32[2,200,128]{2,1,0:T(8,128)} collective-permute-done((f32[2,200,128]{2,1,0:T(8,128)S(1)}, f32[2,200,128]{2,1,0:T(8,128)}, u32[]{:S(2)}, u32[]{:S(2)}) %collective-permute-start.8) | collective-permute-done | bytes 204832 | tf_op jit(solution)/shard_map/ppermute | solution.py:36
  28.1 1.9 %collective-permute-start.7 = (f32[2,200,128]{2,1,0:T(8,128)S(1)}, f32[2,200,128]{2,1,0:T(8,128)S(1)}, u32[]{:S(2)}, u32[]{:S(2)}) collective-permute-start(f32[2,200,128]{2,1,0:T(8,128)S(1)} %collective-permute-done.6.refs_4_), channel_id=1, source_target_pairs={{12,0},{13,1},{14,2},{15,3},{8,4},{9,5},{10,6},{11,7},{4,8},{5,9},... | collective-permute-start | bytes 614408 | tf_op jit(solution)/shard_map/ppermute | solution.py:36
  30.5 3.1 %product.2.refs_6_ = f32[1,768]{1,0:T(1,128)S(1)} custom-call(s32[5]{0:T(128)S(1)} %stack.68.index_ref, f32[200,128]{1,0:T(8,128)S(1)} %collective-permute-done.refs_0_, f32[200,128]{1,0:T(8,128)S(1)} %collective-permute-done.1.refs_1_, f32[200,128]{1,0:T(8,128)S(1)} %collective-permute-done.3.refs_2_, f32[200,128]{1,0:T(8,128)S(1)} %collective-permute-done.4.refs_3_, ...), custom_call_target="tpu_custom_call" | custom-call | flops 3000000000 | bytes 6000000 | tf_op jit(solution)/shard_map/product/pallas_call | solution.py:174
  33.7 3.6 %collective-permute-done.7.refs_2_ = f32[2,200,128]{2,1,0:T(8,128)S(1)} collective-permute-done((f32[2,200,128]{2,1,0:T(8,128)S(1)}, f32[2,200,128]{2,1,0:T(8,128)S(1)}, u32[]{:S(2)}, u32[]{:S(2)}) %collective-permute-start.7) | collective-permute-done | bytes 204832 | tf_op jit(solution)/shard_map/ppermute | solution.py:36
  37.3 2.8 %product.3.e0 = f32[1,768]{1,0:T(1,128)S(1)} custom-call(s32[5]{0:T(128)S(1)} %stack.68.index_ref, f32[2,200,128]{2,1,0:T(8,128)S(1)} %collective-permute-done.2.refs_0_, f32[2,200,128]{2,1,0:T(8,128)S(1)} %collective-permute-done.5.refs_1_, f32[2,200,128]{2,1,0:T(8,128)S(1)} %collective-permute-done.7.refs_2_, ...), custom_call_target="tpu_custom_call" | custom-call | flops 3000000000 | bytes 6000000 | tf_op jit(solution)/shard_map/product/pallas_call | solution.py:174
  40.1 1.6 %collective-permute-start.13 = (f32[1,768]{1,0:T(1,128)S(1)}, f32[1,768]{1,0:T(1,128)S(1)}, u32[]{:S(2)}, u32[]{:S(2)}) collective-permute-start(f32[1,768]{1,0:T(1,128)S(1)} %product.3.e0), channel_id=1, source_target_pairs={{1,0},{0,1},{3,2},{2,3},{5,4},{4,5},{7,6},{6,7},{9,8},{8,9},{11,10... | collective-permute-start | bytes 9224 | tf_op jit(solution)/shard_map/ppermute | solution.py:36
  41.7 2.4 %collective-permute-start.14 = (f32[1,768]{1,0:T(1,128)S(1)}, f32[1,768]{1,0:T(1,128)S(1)}, u32[]{:S(2)}, u32[]{:S(2)}) collective-permute-start(f32[1,768]{1,0:T(1,128)S(1)} %product.3.e0), channel_id=1, source_target_pairs={{2,0},{3,1},{0,2},{1,3},{6,4},{7,5},{4,6},{5,7},{10,8},{11,9},{8,1... | collective-permute-start | bytes 9224 | tf_op jit(solution)/shard_map/ppermute | solution.py:36
  45.1 2.1 %collective-permute-done.15.e3 = f32[1,768]{1,0:T(1,128)S(1)} collective-permute-done((f32[1,768]{1,0:T(1,128)S(1)}, f32[1,768]{1,0:T(1,128)S(1)}, u32[]{:S(2)}, u32[]{:S(2)}) %collective-permute-start.15) | collective-permute-done | bytes 3104 | tf_op jit(solution)/shard_map/ppermute | solution.py:36
  47.5 1.9 %collective-permute-start.16 = (f32[2,3,128]{2,1,0:T(4,128)S(1)}, f32[2,3,128]{2,1,0:T(4,128)S(1)}, u32[]{:S(2)}, u32[]{:S(2)}) collective-permute-start(f32[2,3,128]{2,1,0:T(4,128)S(1)} %get-tuple-element.16), channel_id=1, source_target_pairs={{4,0},{6,2},{8,4},{1,5},{10,6},{3,7},{12,8},{5,9},{14,10},{7,11},{... | collective-permute-start | bytes 9224 | tf_op jit(solution)/shard_map/ppermute | solution.py:279
  49.4 7.9 %collective-permute-done.16.received_ref = f32[2,3,128]{2,1,0:T(4,128)S(1)} collective-permute-done((f32[2,3,128]{2,1,0:T(4,128)S(1)}, f32[2,3,128]{2,1,0:T(4,128)S(1)}, u32[]{:S(2)}, u32[]{:S(2)}) %collective-permute-start.16) | collective-permute-done | bytes 3104 | tf_op jit(solution)/shard_map/ppermute | solution.py:279
  57.3 1.2 %collective-permute-done.17.passed_ref = f32[3,128]{1,0:T(4,128)S(1)} collective-permute-done((f32[3,128]{1,0:T(4,128)S(1)}, f32[3,128]{1,0:T(4,128)S(1)}, u32[]{:S(2)}, u32[]{:S(2)}) %collective-permute-start.17) | collective-permute-done | bytes 1568 | tf_op jit(solution)/shard_map/ppermute | solution.py:36
  (38 shorter events, 4.3 us)
Async XLA Ops:
  0.0 18.4 %collective-permute-start.11 = (f32[100,2,768]{2,1,0:T(2,128)}, f32[100,2,768]{2,1,0:T(2,128)S(1)}, u32[]{:S(2)}, u32[]{:S(2)}) collective-permute-start(f32[100,2,768]{2,1,0:T(2,128)} %bitcast.22), channel_id=1, source_target_pairs={{2,0},{3,1},{0,2},{1,3},{6,4},{7,5},{4,6},{5,7},{10,8},{11,9},{8,1... | collective-permute-start | bytes 1843208 | tf_op jit(solution)/shard_map/ppermute | solution.py:36
  0.5 0.9 %copy-start.2 = (f32[2,400,32]{1,2,0:T(8,128)S(1)}, f32[2,400,32]{1,2,0:T(8,128)}, u32[]{:S(2)}) copy-start(f32[2,400,32]{1,2,0:T(8,128)} %param.7) | copy-start | bytes 307204
  1.7 9.0 %collective-permute-start.1 = (f32[200,128]{1,0:T(8,128)S(1)}, f32[200,128]{1,0:T(8,128)S(1)}, u32[]{:S(2)}, u32[]{:S(2)}) collective-permute-start(f32[200,128]{1,0:T(8,128)S(1)} %pack_weight.1), channel_id=1, source_target_pairs={{33,0},{97,1},{161,2},{225,3},{37,4},{101,5},{165,6},{229,7},{41,8... | collective-permute-start | bytes 307208 | tf_op jit(solution)/shard_map/ppermute | solution.py:36
  5.7 7.8 %collective-permute-start = (f32[200,128]{1,0:T(8,128)S(1)}, f32[200,128]{1,0:T(8,128)S(1)}, u32[]{:S(2)}, u32[]{:S(2)}) collective-permute-start(f32[200,128]{1,0:T(8,128)S(1)} %pack_weight.1), channel_id=1, source_target_pairs={{49,0},{113,1},{177,2},{241,3},{53,4},{117,5},{181,6},{245,7},{57,... | collective-permute-start | bytes 307208 | tf_op jit(solution)/shard_map/ppermute | solution.py:36
  10.6 6.6 %collective-permute-start.4 = (f32[200,128]{1,0:T(8,128)S(1)}, f32[200,128]{1,0:T(8,128)S(1)}, u32[]{:S(2)}, u32[]{:S(2)}) collective-permute-start(f32[200,128]{1,0:T(8,128)S(1)} %pack_weight.1), channel_id=1, source_target_pairs={{17,0},{81,1},{145,2},{209,3},{21,4},{85,5},{149,6},{213,7},{25,8}... | collective-permute-start | bytes 307208 | tf_op jit(solution)/shard_map/ppermute | solution.py:36
  10.8 7.6 %collective-permute-start.3 = (f32[200,128]{1,0:T(8,128)S(1)}, f32[200,128]{1,0:T(8,128)S(1)}, u32[]{:S(2)}, u32[]{:S(2)}) collective-permute-start(f32[200,128]{1,0:T(8,128)S(1)} %pack_weight.1), channel_id=1, source_target_pairs={{1,0},{65,1},{129,2},{193,3},{5,4},{69,5},{133,6},{197,7},{9,8},{7... | collective-permute-start | bytes 307208 | tf_op jit(solution)/shard_map/ppermute | solution.py:36
  10.8 19.2 %collective-permute-start.10 = (f32[100,2,768]{2,1,0:T(2,128)}, f32[100,2,768]{2,1,0:T(2,128)S(1)}, u32[]{:S(2)}, u32[]{:S(2)}) collective-permute-start(f32[100,2,768]{2,1,0:T(2,128)} %bitcast.23), channel_id=1, source_target_pairs={{1,0},{0,1},{3,2},{2,3},{5,4},{4,5},{7,6},{6,7},{9,8},{8,9},{11,10... | collective-permute-start | bytes 1843208 | tf_op jit(solution)/shard_map/ppermute | solution.py:36
  18.3 11.6 %copy-start.1 = (f32[2,100,768]{2,0,1:T(2,128)S(1)}, f32[2,100,768]{2,0,1:T(2,128)}, u32[]{:S(2)}) copy-start(f32[2,100,768]{2,0,1:T(2,128)} %param.5) | copy-start | bytes 1843204
  18.4 11.6 %collective-permute-start.12 = (f32[100,2,768]{2,1,0:T(2,128)S(1)}, f32[100,2,768]{2,1,0:T(2,128)S(1)}, u32[]{:S(2)}, u32[]{:S(2)}) collective-permute-start(f32[100,2,768]{2,1,0:T(2,128)S(1)} %gate.1.flipped_ref), channel_id=1, source_target_pairs={{1,0},{0,1},{3,2},{2,3},{5,4},{4,5},{7,6},{6,7},{9,8},{8,9},{11,10... | collective-permute-start | bytes 1843208 | tf_op jit(solution)/shard_map/ppermute | solution.py:36
  19.1 7.4 %collective-permute-start.6 = (f32[2,200,128]{2,1,0:T(8,128)S(1)}, f32[2,200,128]{2,1,0:T(8,128)S(1)}, u32[]{:S(2)}, u32[]{:S(2)}) collective-permute-start(f32[2,200,128]{2,1,0:T(8,128)S(1)} %pad_maximum_fusion.refs_0_), channel_id=1, source_target_pairs={{4,0},{5,1},{6,2},{7,3},{0,4},{1,5},{2,6},{3,7},{12,8},{13,9},{14,... | collective-permute-start | bytes 614408 | tf_op jit(solution)/shard_map/ppermute | solution.py:36
  20.4 7.6 %collective-permute-start.8 = (f32[2,200,128]{2,1,0:T(8,128)S(1)}, f32[2,200,128]{2,1,0:T(8,128)}, u32[]{:S(2)}, u32[]{:S(2)}) collective-permute-start(f32[2,200,128]{2,1,0:T(8,128)S(1)} %pad_maximum_fusion.1.refs_1_), channel_id=1, source_target_pairs={{12,0},{13,1},{14,2},{15,3},{8,4},{9,5},{10,6},{11,7},{4,8},{5,9},... | collective-permute-start | bytes 614408 | tf_op jit(solution)/shard_map/ppermute | solution.py:36
  22.5 1.9 %copy-start = (f32[2,512,768]{2,1,0:T(8,128)S(1)}, f32[2,512,768]{2,1,0:T(8,128)}, u32[]{:S(2)}) copy-start(f32[2,512,768]{2,1,0:T(8,128)} %rx_ref.1) | copy-start | bytes 9437188
  25.6 8.1 %collective-permute-start.2 = (f32[2,200,128]{2,1,0:T(8,128)S(1)}, f32[2,200,128]{2,1,0:T(8,128)S(1)}, u32[]{:S(2)}, u32[]{:S(2)}) collective-permute-start(f32[2,200,128]{2,1,0:T(8,128)S(1)} %pad_maximum_fusion.refs_0_), channel_id=1, source_target_pairs={{12,0},{13,1},{14,2},{15,3},{8,4},{9,5},{10,6},{11,7},{4,8},{5,9},... | collective-permute-start | bytes 614408 | tf_op jit(solution)/shard_map/ppermute | solution.py:36
  26.5 7.2 %collective-permute-start.5 = (f32[2,200,128]{2,1,0:T(8,128)S(1)}, f32[2,200,128]{2,1,0:T(8,128)S(1)}, u32[]{:S(2)}, u32[]{:S(2)}) collective-permute-start(f32[2,200,128]{2,1,0:T(8,128)S(1)} %pad_maximum_fusion.1.refs_1_), channel_id=1, source_target_pairs={{4,0},{5,1},{6,2},{7,3},{0,4},{1,5},{2,6},{3,7},{12,8},{13,9},{14,... | collective-permute-start | bytes 614408 | tf_op jit(solution)/shard_map/ppermute | solution.py:36
  28.1 9.3 %collective-permute-start.7 = (f32[2,200,128]{2,1,0:T(8,128)S(1)}, f32[2,200,128]{2,1,0:T(8,128)S(1)}, u32[]{:S(2)}, u32[]{:S(2)}) collective-permute-start(f32[2,200,128]{2,1,0:T(8,128)S(1)} %collective-permute-done.6.refs_4_), channel_id=1, source_target_pairs={{12,0},{13,1},{14,2},{15,3},{8,4},{9,5},{10,6},{11,7},{4,8},{5,9},... | collective-permute-start | bytes 614408 | tf_op jit(solution)/shard_map/ppermute | solution.py:36
  30.0 7.4 %collective-permute-start.9 = (f32[2,200,128]{2,1,0:T(8,128)}, f32[2,200,128]{2,1,0:T(8,128)S(1)}, u32[]{:S(2)}, u32[]{:S(2)}) collective-permute-start(f32[2,200,128]{2,1,0:T(8,128)} %collective-permute-done.8.refs_5_), channel_id=1, source_target_pairs={{4,0},{5,1},{6,2},{7,3},{0,4},{1,5},{2,6},{3,7},{12,8},{13,9},{14,... | collective-permute-start | bytes 614408 | tf_op jit(solution)/shard_map/ppermute | solution.py:36
  37.3 6.9 %copy-start.4 = (s32[768]{0:T(1024)S(1)}, s32[768]{0:T(1024)}, u32[]{:S(2)}) copy-start(s32[768]{0:T(1024)} %param.9) | copy-start | bytes 9220
  37.3 6.9 %copy-start.3 = (s32[768,4]{0,1:T(4,128)S(1)}, s32[768,4]{0,1:T(4,128)}, u32[]{:S(2)}) copy-start(s32[768,4]{0,1:T(4,128)} %param.8) | copy-start | bytes 36868
  40.1 4.8 %collective-permute-start.13 = (f32[1,768]{1,0:T(1,128)S(1)}, f32[1,768]{1,0:T(1,128)S(1)}, u32[]{:S(2)}, u32[]{:S(2)}) collective-permute-start(f32[1,768]{1,0:T(1,128)S(1)} %product.3.e0), channel_id=1, source_target_pairs={{1,0},{0,1},{3,2},{2,3},{5,4},{4,5},{7,6},{6,7},{9,8},{8,9},{11,10... | collective-permute-start | bytes 9224 | tf_op jit(solution)/shard_map/ppermute | solution.py:36
  41.7 3.4 %collective-permute-start.14 = (f32[1,768]{1,0:T(1,128)S(1)}, f32[1,768]{1,0:T(1,128)S(1)}, u32[]{:S(2)}, u32[]{:S(2)}) collective-permute-start(f32[1,768]{1,0:T(1,128)S(1)} %product.3.e0), channel_id=1, source_target_pairs={{2,0},{3,1},{0,2},{1,3},{6,4},{7,5},{4,6},{5,7},{10,8},{11,9},{8,1... | collective-permute-start | bytes 9224 | tf_op jit(solution)/shard_map/ppermute | solution.py:36
  44.1 3.0 %collective-permute-start.15 = (f32[1,768]{1,0:T(1,128)S(1)}, f32[1,768]{1,0:T(1,128)S(1)}, u32[]{:S(2)}, u32[]{:S(2)}) collective-permute-start(f32[1,768]{1,0:T(1,128)S(1)} %product.3.e0), channel_id=1, source_target_pairs={{3,0},{2,1},{1,2},{0,3},{7,4},{6,5},{5,6},{4,7},{11,8},{10,9},{9,1... | collective-permute-start | bytes 9224 | tf_op jit(solution)/shard_map/ppermute | solution.py:36
  47.5 9.8 %collective-permute-start.16 = (f32[2,3,128]{2,1,0:T(4,128)S(1)}, f32[2,3,128]{2,1,0:T(4,128)S(1)}, u32[]{:S(2)}, u32[]{:S(2)}) collective-permute-start(f32[2,3,128]{2,1,0:T(4,128)S(1)} %get-tuple-element.16), channel_id=1, source_target_pairs={{4,0},{6,2},{8,4},{1,5},{10,6},{3,7},{12,8},{5,9},{14,10},{7,11},{... | collective-permute-start | bytes 9224 | tf_op jit(solution)/shard_map/ppermute | solution.py:279
  57.3 1.2 %collective-permute-start.17 = (f32[3,128]{1,0:T(4,128)S(1)}, f32[3,128]{1,0:T(4,128)S(1)}, u32[]{:S(2)}, u32[]{:S(2)}) collective-permute-start(f32[3,128]{1,0:T(4,128)S(1)} %slice_bitcast_fusion), channel_id=1, source_target_pairs={{1,0},{0,1},{3,2},{2,3},{5,4},{4,5},{7,6},{6,7},{9,8},{8,9},{11,10... | collective-permute-start | bytes 4616 | tf_op jit(solution)/shard_map/ppermute | solution.py:36

commit v7 on v6

--- a/solution.py
+++ b/solution.py
@@ -340,7 +340,7 @@
     early = [[(k, None) for k in range(4)], pairs(4)]
     edge = product(early, index, from_z + [near[0], far[1]], tx, fields[0], edge)
     edge = product([pairs(0), pairs(2)], index, [far[0], near[1]] + last, tx, fields[1], edge)
-    terms = [edge, fetch(edge, flip_core), fetch(edge, flip_x), fetch(edge, flip_both)]
+    terms = [edge, fetch(edge, flip_x), fetch(edge, flip_both), fetch(edge, flip_core)]
     own, send = scatter(terms, hot, row)
     received = neighbour_parts(send)
     return total(own, received, fetch(received[1], flip_core))

time: 59.2 us -> 57.6 us (0.973)
  waiting for transfers between devices: 21.7 us -> 20 us
    ppermute x17, waiting for transfers between devices: 13.9 us -> 12.1 us  [fetch(): return lax.ppermute(block, AXES, route)]
  transfers between devices with their start and end apart: 18 -> 18, of which waited for: 9 -> 8; matrix products, arithmetic and copies ran while one was open for 0% -> 0% of each run, Pallas kernels for 10% -> 10%
where the time goes in v7:
time: 57.6 us; the launch traced here: 57.4 us
  starting transfers between devices  24.7 us (43%)
  waiting for transfers between devices  20 us (35%)
  Pallas kernels  9.56 us (17%)
  local copies, waits for them, and re-layouts  2.99 us (5%)
    ppermute x17, starting transfers between devices, fetch(): return lax.ppermute(block, AXES, route)  22.8 us
    ppermute x17, waiting for transfers between devices, fetch(): return lax.ppermute(block, AXES, route)  12.1 us
    ppermute x1, waiting for transfers between devices, neighbour_parts(): return lax.ppermute(block, AXES, route)  7.85 us
    pallas_call x2, Pallas kernels, product(): pl.pallas_call(functools.partial(product_kernel, sources), in_specs=[SCAL...  5.9 us
    unnamed x10, local copies, waits for them, and re-layouts  2.81 us
    ppermute x1, starting transfers between devices, neighbour_parts(): return lax.ppermute(block, AXES, route)  1.94 us
    pallas_call x1, Pallas kernels, prepare_fields(): pl.pallas_call(prepare_kernel, in_specs=[SCALARS, WHOLE], out_specs=(WHOL...  1.23 us
  transfers between devices with their start and end apart: 18, of which 8 were waited for; matrix products, arithmetic and copies ran while one was open for 0% of the time, Pallas kernels for 10%

profile of v7, /device:TPU:7, one launch (start us, length us, event | category | flops | bytes accessed | tf_op | source)
XLA Modules:
  0.0 57.4 jit_solution(15364584071324948247)
XLA Ops:
  0.6 0.9 %copy-done.2 = f32[2,400,32]{1,2,0:T(8,128)S(1)} copy-done((f32[2,400,32]{1,2,0:T(8,128)S(1)}, f32[2,400,32]{1,2,0:T(8,128)}, u32[]{:S(2)}) %copy-start.2) | copy-done | bytes 102424
  1.7 3.9 %collective-permute-start.1 = (f32[200,128]{1,0:T(8,128)S(1)}, f32[200,128]{1,0:T(8,128)S(1)}, u32[]{:S(2)}, u32[]{:S(2)}) collective-permute-start(f32[200,128]{1,0:T(8,128)S(1)} %pack_weight.1), channel_id=1, source_target_pairs={{33,0},{97,1},{161,2},{225,3},{37,4},{101,5},{165,6},{229,7},{41,8... | collective-permute-start | bytes 307208 | tf_op jit(solution)/shard_map/ppermute | solution.py:36
  5.7 4.9 %collective-permute-start = (f32[200,128]{1,0:T(8,128)S(1)}, f32[200,128]{1,0:T(8,128)S(1)}, u32[]{:S(2)}, u32[]{:S(2)}) collective-permute-start(f32[200,128]{1,0:T(8,128)S(1)} %pack_weight.1), channel_id=1, source_target_pairs={{49,0},{113,1},{177,2},{241,3},{53,4},{117,5},{181,6},{245,7},{57,... | collective-permute-start | bytes 307208 | tf_op jit(solution)/shard_map/ppermute | solution.py:36
  10.8 1.5 %collective-permute-start.10 = (f32[100,2,768]{2,1,0:T(2,128)}, f32[100,2,768]{2,1,0:T(2,128)S(1)}, u32[]{:S(2)}, u32[]{:S(2)}) collective-permute-start(f32[100,2,768]{2,1,0:T(2,128)} %bitcast.23), channel_id=1, source_target_pairs={{1,0},{0,1},{3,2},{2,3},{5,4},{4,5},{7,6},{6,7},{9,8},{8,9},{11,10... | collective-permute-start | bytes 1843208 | tf_op jit(solution)/shard_map/ppermute | solution.py:36
  12.3 1.2 %collective-permute-done.refs_0_ = f32[200,128]{1,0:T(8,128)S(1)} collective-permute-done((f32[200,128]{1,0:T(8,128)S(1)}, f32[200,128]{1,0:T(8,128)S(1)}, u32[]{:S(2)}, u32[]{:S(2)}) %collective-permute-start) | collective-permute-done | bytes 102432 | tf_op jit(solution)/shard_map/ppermute | solution.py:36
  13.5 3.8 %collective-permute-done.4.refs_3_ = f32[200,128]{1,0:T(8,128)S(1)} collective-permute-done((f32[200,128]{1,0:T(8,128)S(1)}, f32[200,128]{1,0:T(8,128)S(1)}, u32[]{:S(2)}, u32[]{:S(2)}) %collective-permute-start.4) | collective-permute-done | bytes 102432 | tf_op jit(solution)/shard_map/ppermute | solution.py:36
  17.2 1.1 %collective-permute-done.3.refs_2_ = f32[200,128]{1,0:T(8,128)S(1)} collective-permute-done((f32[200,128]{1,0:T(8,128)S(1)}, f32[200,128]{1,0:T(8,128)S(1)}, u32[]{:S(2)}, u32[]{:S(2)}) %collective-permute-start.3) | collective-permute-done | bytes 102432 | tf_op jit(solution)/shard_map/ppermute | solution.py:36
  18.4 0.7 %collective-permute-start.12 = (f32[100,2,768]{2,1,0:T(2,128)S(1)}, f32[100,2,768]{2,1,0:T(2,128)S(1)}, u32[]{:S(2)}, u32[]{:S(2)}) collective-permute-start(f32[100,2,768]{2,1,0:T(2,128)S(1)} %gate.1.flipped_ref), channel_id=1, source_target_pairs={{1,0},{0,1},{3,2},{2,3},{5,4},{4,5},{7,6},{6,7},{9,8},{8,9},{11,10... | collective-permute-start | bytes 1843208 | tf_op jit(solution)/shard_map/ppermute | solution.py:36
  19.1 1.3 %collective-permute-start.6 = (f32[2,200,128]{2,1,0:T(8,128)S(1)}, f32[2,200,128]{2,1,0:T(8,128)S(1)}, u32[]{:S(2)}, u32[]{:S(2)}) collective-permute-start(f32[2,200,128]{2,1,0:T(8,128)S(1)} %pad_maximum_fusion.refs_0_), channel_id=1, source_target_pairs={{4,0},{5,1},{6,2},{7,3},{0,4},{1,5},{2,6},{3,7},{12,8},{13,9},{14,... | collective-permute-start | bytes 614408 | tf_op jit(solution)/shard_map/ppermute | solution.py:36
  20.4 1.9 %collective-permute-start.8 = (f32[2,200,128]{2,1,0:T(8,128)S(1)}, f32[2,200,128]{2,1,0:T(8,128)}, u32[]{:S(2)}, u32[]{:S(2)}) collective-permute-start(f32[2,200,128]{2,1,0:T(8,128)S(1)} %pad_maximum_fusion.1.refs_1_), channel_id=1, source_target_pairs={{12,0},{13,1},{14,2},{15,3},{8,4},{9,5},{10,6},{11,7},{4,8},{5,9},... | collective-permute-start | bytes 614408 | tf_op jit(solution)/shard_map/ppermute | solution.py:36
  22.5 1.9 %copy-done = f32[2,512,768]{2,1,0:T(8,128)S(1)} copy-done((f32[2,512,768]{2,1,0:T(8,128)S(1)}, f32[2,512,768]{2,1,0:T(8,128)}, u32[]{:S(2)}) %copy-start) | copy-done | bytes 3145752
  24.4 1.2 %prepare_fields.1 = (bf16[3,2,256,768]{3,2,1,0:T(8,128)(2,1)S(1)}, bf16[3,2,256,768]{3,2,1,0:T(8,128)(2,1)S(1)}) custom-call(s32[8]{0:T(128)S(1)} %stack.83.place_ref, f32[2,512,768]{2,1,0:T(8,128)S(1)} %copy-done), custom_call_target="tpu_custom_call" | custom-call | flops 10000000 | bytes 8000000 | tf_op jit(solution)/shard_map/prepare_fields/pallas_call | solution.py:79
  25.6 0.9 %collective-permute-start.2 = (f32[2,200,128]{2,1,0:T(8,128)S(1)}, f32[2,200,128]{2,1,0:T(8,128)S(1)}, u32[]{:S(2)}, u32[]{:S(2)}) collective-permute-start(f32[2,200,128]{2,1,0:T(8,128)S(1)} %pad_maximum_fusion.refs_0_), channel_id=1, source_target_pairs={{12,0},{13,1},{14,2},{15,3},{8,4},{9,5},{10,6},{11,7},{4,8},{5,9},... | collective-permute-start | bytes 614408 | tf_op jit(solution)/shard_map/ppermute | solution.py:36
  27.2 0.9 %collective-permute-done.8.refs_5_ = f32[2,200,128]{2,1,0:T(8,128)} collective-permute-done((f32[2,200,128]{2,1,0:T(8,128)S(1)}, f32[2,200,128]{2,1,0:T(8,128)}, u32[]{:S(2)}, u32[]{:S(2)}) %collective-permute-start.8) | collective-permute-done | bytes 204832 | tf_op jit(solution)/shard_map/ppermute | solution.py:36
  28.1 1.9 %collective-permute-start.7 = (f32[2,200,128]{2,1,0:T(8,128)S(1)}, f32[2,200,128]{2,1,0:T(8,128)S(1)}, u32[]{:S(2)}, u32[]{:S(2)}) collective-permute-start(f32[2,200,128]{2,1,0:T(8,128)S(1)} %collective-permute-done.6.refs_4_), channel_id=1, source_target_pairs={{12,0},{13,1},{14,2},{15,3},{8,4},{9,5},{10,6},{11,7},{4,8},{5,9},... | collective-permute-start | bytes 614408 | tf_op jit(solution)/shard_map/ppermute | solution.py:36
  30.5 3.1 %product.2.refs_6_ = f32[1,768]{1,0:T(1,128)S(1)} custom-call(s32[5]{0:T(128)S(1)} %stack.68.index_ref, f32[200,128]{1,0:T(8,128)S(1)} %collective-permute-done.refs_0_, f32[200,128]{1,0:T(8,128)S(1)} %collective-permute-done.1.refs_1_, f32[200,128]{1,0:T(8,128)S(1)} %collective-permute-done.3.refs_2_, f32[200,128]{1,0:T(8,128)S(1)} %collective-permute-done.4.refs_3_, ...), custom_call_target="tpu_custom_call" | custom-call | flops 3000000000 | bytes 6000000 | tf_op jit(solution)/shard_map/product/pallas_call | solution.py:174
  33.7 3.6 %collective-permute-done.7.refs_2_ = f32[2,200,128]{2,1,0:T(8,128)S(1)} collective-permute-done((f32[2,200,128]{2,1,0:T(8,128)S(1)}, f32[2,200,128]{2,1,0:T(8,128)S(1)}, u32[]{:S(2)}, u32[]{:S(2)}) %collective-permute-start.7) | collective-permute-done | bytes 204832 | tf_op jit(solution)/shard_map/ppermute | solution.py:36
  37.3 2.8 %product.3.e0 = f32[1,768]{1,0:T(1,128)S(1)} custom-call(s32[5]{0:T(128)S(1)} %stack.68.index_ref, f32[2,200,128]{2,1,0:T(8,128)S(1)} %collective-permute-done.2.refs_0_, f32[2,200,128]{2,1,0:T(8,128)S(1)} %collective-permute-done.5.refs_1_, f32[2,200,128]{2,1,0:T(8,128)S(1)} %collective-permute-done.7.refs_2_, ...), custom_call_target="tpu_custom_call" | custom-call | flops 3000000000 | bytes 6000000 | tf_op jit(solution)/shard_map/product/pallas_call | solution.py:174
  40.1 2.1 %collective-permute-start.13 = (f32[1,768]{1,0:T(1,128)S(1)}, f32[1,768]{1,0:T(1,128)S(1)}, u32[]{:S(2)}, u32[]{:S(2)}) collective-permute-start(f32[1,768]{1,0:T(1,128)S(1)} %product.3.e0), channel_id=1, source_target_pairs={{2,0},{3,1},{0,2},{1,3},{6,4},{7,5},{4,6},{5,7},{10,8},{11,9},{8,1... | collective-permute-start | bytes 9224 | tf_op jit(solution)/shard_map/ppermute | solution.py:36
  42.2 1.9 %collective-permute-start.14 = (f32[1,768]{1,0:T(1,128)S(1)}, f32[1,768]{1,0:T(1,128)S(1)}, u32[]{:S(2)}, u32[]{:S(2)}) collective-permute-start(f32[1,768]{1,0:T(1,128)S(1)} %product.3.e0), channel_id=1, source_target_pairs={{3,0},{2,1},{1,2},{0,3},{7,4},{6,5},{5,6},{4,7},{11,8},{10,9},{9,1... | collective-permute-start | bytes 9224 | tf_op jit(solution)/shard_map/ppermute | solution.py:36
  44.4 0.7 %onehots.1 = (bf16[4,128,768]{2,1,0:T(8,128)(2,1)S(1)}, s32[4,768]{1,0:T(4,128)S(1)}) custom-call(s32[5]{0:T(128)S(1)} %stack.68.index_ref, s32[4,768]{1,0:T(4,128)S(1)} %bitcast.30, s32[1,768]{1,0:T(1,128)S(1)} %broadcast_in_dim.7.component_ref), custom_call_target="tpu_custom_call" | custom-call | tf_op jit(solution)/shard_map/onehots/pallas_call | solution.py:210
  45.9 1.9 %collective-permute-start.16 = (f32[2,3,128]{2,1,0:T(4,128)S(1)}, f32[2,3,128]{2,1,0:T(4,128)S(1)}, u32[]{:S(2)}, u32[]{:S(2)}) collective-permute-start(f32[2,3,128]{2,1,0:T(4,128)S(1)} %get-tuple-element.16), channel_id=1, source_target_pairs={{4,0},{6,2},{8,4},{1,5},{10,6},{3,7},{12,8},{5,9},{14,10},{7,11},{... | collective-permute-start | bytes 9224 | tf_op jit(solution)/shard_map/ppermute | solution.py:279
  47.8 7.9 %collective-permute-done.16.received_ref = f32[2,3,128]{2,1,0:T(4,128)S(1)} collective-permute-done((f32[2,3,128]{2,1,0:T(4,128)S(1)}, f32[2,3,128]{2,1,0:T(4,128)S(1)}, u32[]{:S(2)}, u32[]{:S(2)}) %collective-permute-start.16) | collective-permute-done | bytes 3104 | tf_op jit(solution)/shard_map/ppermute | solution.py:279
  55.7 1.2 %collective-permute-done.17.passed_ref = f32[3,128]{1,0:T(4,128)S(1)} collective-permute-done((f32[3,128]{1,0:T(4,128)S(1)}, f32[3,128]{1,0:T(4,128)S(1)}, u32[]{:S(2)}, u32[]{:S(2)}) %collective-permute-start.17) | collective-permute-done | bytes 1568 | tf_op jit(solution)/shard_map/ppermute | solution.py:36
  (38 shorter events, 4.1 us)
Async XLA Ops:
  0.0 18.4 %collective-permute-start.11 = (f32[100,2,768]{2,1,0:T(2,128)}, f32[100,2,768]{2,1,0:T(2,128)S(1)}, u32[]{:S(2)}, u32[]{:S(2)}) collective-permute-start(f32[100,2,768]{2,1,0:T(2,128)} %bitcast.22), channel_id=1, source_target_pairs={{2,0},{3,1},{0,2},{1,3},{6,4},{7,5},{4,6},{5,7},{10,8},{11,9},{8,1... | collective-permute-start | bytes 1843208 | tf_op jit(solution)/shard_map/ppermute | solution.py:36
  0.5 0.9 %copy-start.2 = (f32[2,400,32]{1,2,0:T(8,128)S(1)}, f32[2,400,32]{1,2,0:T(8,128)}, u32[]{:S(2)}) copy-start(f32[2,400,32]{1,2,0:T(8,128)} %param.7) | copy-start | bytes 307204
  1.7 9.0 %collective-permute-start.1 = (f32[200,128]{1,0:T(8,128)S(1)}, f32[200,128]{1,0:T(8,128)S(1)}, u32[]{:S(2)}, u32[]{:S(2)}) collective-permute-start(f32[200,128]{1,0:T(8,128)S(1)} %pack_weight.1), channel_id=1, source_target_pairs={{33,0},{97,1},{161,2},{225,3},{37,4},{101,5},{165,6},{229,7},{41,8... | collective-permute-start | bytes 307208 | tf_op jit(solution)/shard_map/ppermute | solution.py:36
  5.7 7.8 %collective-permute-start = (f32[200,128]{1,0:T(8,128)S(1)}, f32[200,128]{1,0:T(8,128)S(1)}, u32[]{:S(2)}, u32[]{:S(2)}) collective-permute-start(f32[200,128]{1,0:T(8,128)S(1)} %pack_weight.1), channel_id=1, source_target_pairs={{49,0},{113,1},{177,2},{241,3},{53,4},{117,5},{181,6},{245,7},{57,... | collective-permute-start | bytes 307208 | tf_op jit(solution)/shard_map/ppermute | solution.py:36
  10.6 6.6 %collective-permute-start.4 = (f32[200,128]{1,0:T(8,128)S(1)}, f32[200,128]{1,0:T(8,128)S(1)}, u32[]{:S(2)}, u32[]{:S(2)}) collective-permute-start(f32[200,128]{1,0:T(8,128)S(1)} %pack_weight.1), channel_id=1, source_target_pairs={{17,0},{81,1},{145,2},{209,3},{21,4},{85,5},{149,6},{213,7},{25,8}... | collective-permute-start | bytes 307208 | tf_op jit(solution)/shard_map/ppermute | solution.py:36
  10.8 7.6 %collective-permute-start.3 = (f32[200,128]{1,0:T(8,128)S(1)}, f32[200,128]{1,0:T(8,128)S(1)}, u32[]{:S(2)}, u32[]{:S(2)}) collective-permute-start(f32[200,128]{1,0:T(8,128)S(1)} %pack_weight.1), channel_id=1, source_target_pairs={{1,0},{65,1},{129,2},{193,3},{5,4},{69,5},{133,6},{197,7},{9,8},{7... | collective-permute-start | bytes 307208 | tf_op jit(solution)/shard_map/ppermute | solution.py:36
  10.8 19.2 %collective-permute-start.10 = (f32[100,2,768]{2,1,0:T(2,128)}, f32[100,2,768]{2,1,0:T(2,128)S(1)}, u32[]{:S(2)}, u32[]{:S(2)}) collective-permute-start(f32[100,2,768]{2,1,0:T(2,128)} %bitcast.23), channel_id=1, source_target_pairs={{1,0},{0,1},{3,2},{2,3},{5,4},{4,5},{7,6},{6,7},{9,8},{8,9},{11,10... | collective-permute-start | bytes 1843208 | tf_op jit(solution)/shard_map/ppermute | solution.py:36
  18.3 11.6 %copy-start.1 = (f32[2,100,768]{2,0,1:T(2,128)S(1)}, f32[2,100,768]{2,0,1:T(2,128)}, u32[]{:S(2)}) copy-start(f32[2,100,768]{2,0,1:T(2,128)} %param.5) | copy-start | bytes 1843204
  18.4 11.6 %collective-permute-start.12 = (f32[100,2,768]{2,1,0:T(2,128)S(1)}, f32[100,2,768]{2,1,0:T(2,128)S(1)}, u32[]{:S(2)}, u32[]{:S(2)}) collective-permute-start(f32[100,2,768]{2,1,0:T(2,128)S(1)} %gate.1.flipped_ref), channel_id=1, source_target_pairs={{1,0},{0,1},{3,2},{2,3},{5,4},{4,5},{7,6},{6,7},{9,8},{8,9},{11,10... | collective-permute-start | bytes 1843208 | tf_op jit(solution)/shard_map/ppermute | solution.py:36
  19.1 7.4 %collective-permute-start.6 = (f32[2,200,128]{2,1,0:T(8,128)S(1)}, f32[2,200,128]{2,1,0:T(8,128)S(1)}, u32[]{:S(2)}, u32[]{:S(2)}) collective-permute-start(f32[2,200,128]{2,1,0:T(8,128)S(1)} %pad_maximum_fusion.refs_0_), channel_id=1, source_target_pairs={{4,0},{5,1},{6,2},{7,3},{0,4},{1,5},{2,6},{3,7},{12,8},{13,9},{14,... | collective-permute-start | bytes 614408 | tf_op jit(solution)/shard_map/ppermute | solution.py:36
  20.4 7.6 %collective-permute-start.8 = (f32[2,200,128]{2,1,0:T(8,128)S(1)}, f32[2,200,128]{2,1,0:T(8,128)}, u32[]{:S(2)}, u32[]{:S(2)}) collective-permute-start(f32[2,200,128]{2,1,0:T(8,128)S(1)} %pad_maximum_fusion.1.refs_1_), channel_id=1, source_target_pairs={{12,0},{13,1},{14,2},{15,3},{8,4},{9,5},{10,6},{11,7},{4,8},{5,9},... | collective-permute-start | bytes 614408 | tf_op jit(solution)/shard_map/ppermute | solution.py:36
  22.5 1.9 %copy-start = (f32[2,512,768]{2,1,0:T(8,128)S(1)}, f32[2,512,768]{2,1,0:T(8,128)}, u32[]{:S(2)}) copy-start(f32[2,512,768]{2,1,0:T(8,128)} %rx_ref.1) | copy-start | bytes 9437188
  25.6 8.1 %collective-permute-start.2 = (f32[2,200,128]{2,1,0:T(8,128)S(1)}, f32[2,200,128]{2,1,0:T(8,128)S(1)}, u32[]{:S(2)}, u32[]{:S(2)}) collective-permute-start(f32[2,200,128]{2,1,0:T(8,128)S(1)} %pad_maximum_fusion.refs_0_), channel_id=1, source_target_pairs={{12,0},{13,1},{14,2},{15,3},{8,4},{9,5},{10,6},{11,7},{4,8},{5,9},... | collective-permute-start | bytes 614408 | tf_op jit(solution)/shard_map/ppermute | solution.py:36
  26.5 7.2 %collective-permute-start.5 = (f32[2,200,128]{2,1,0:T(8,128)S(1)}, f32[2,200,128]{2,1,0:T(8,128)S(1)}, u32[]{:S(2)}, u32[]{:S(2)}) collective-permute-start(f32[2,200,128]{2,1,0:T(8,128)S(1)} %pad_maximum_fusion.1.refs_1_), channel_id=1, source_target_pairs={{4,0},{5,1},{6,2},{7,3},{0,4},{1,5},{2,6},{3,7},{12,8},{13,9},{14,... | collective-permute-start | bytes 614408 | tf_op jit(solution)/shard_map/ppermute | solution.py:36
  28.1 9.3 %collective-permute-start.7 = (f32[2,200,128]{2,1,0:T(8,128)S(1)}, f32[2,200,128]{2,1,0:T(8,128)S(1)}, u32[]{:S(2)}, u32[]{:S(2)}) collective-permute-start(f32[2,200,128]{2,1,0:T(8,128)S(1)} %collective-permute-done.6.refs_4_), channel_id=1, source_target_pairs={{12,0},{13,1},{14,2},{15,3},{8,4},{9,5},{10,6},{11,7},{4,8},{5,9},... | collective-permute-start | bytes 614408 | tf_op jit(solution)/shard_map/ppermute | solution.py:36
  30.0 7.4 %collective-permute-start.9 = (f32[2,200,128]{2,1,0:T(8,128)}, f32[2,200,128]{2,1,0:T(8,128)S(1)}, u32[]{:S(2)}, u32[]{:S(2)}) collective-permute-start(f32[2,200,128]{2,1,0:T(8,128)} %collective-permute-done.8.refs_5_), channel_id=1, source_target_pairs={{4,0},{5,1},{6,2},{7,3},{0,4},{1,5},{2,6},{3,7},{12,8},{13,9},{14,... | collective-permute-start | bytes 614408 | tf_op jit(solution)/shard_map/ppermute | solution.py:36
  37.3 7.1 %copy-start.4 = (s32[768]{0:T(1024)S(1)}, s32[768]{0:T(1024)}, u32[]{:S(2)}) copy-start(s32[768]{0:T(1024)} %param.9) | copy-start | bytes 9220
  37.3 7.1 %copy-start.3 = (s32[768,4]{0,1:T(4,128)S(1)}, s32[768,4]{0,1:T(4,128)}, u32[]{:S(2)}) copy-start(s32[768,4]{0,1:T(4,128)} %param.8) | copy-start | bytes 36868
  40.1 5.0 %collective-permute-start.13 = (f32[1,768]{1,0:T(1,128)S(1)}, f32[1,768]{1,0:T(1,128)S(1)}, u32[]{:S(2)}, u32[]{:S(2)}) collective-permute-start(f32[1,768]{1,0:T(1,128)S(1)} %product.3.e0), channel_id=1, source_target_pairs={{2,0},{3,1},{0,2},{1,3},{6,4},{7,5},{4,6},{5,7},{10,8},{11,9},{8,1... | collective-permute-start | bytes 9224 | tf_op jit(solution)/shard_map/ppermute | solution.py:36
  42.2 3.3 %collective-permute-start.14 = (f32[1,768]{1,0:T(1,128)S(1)}, f32[1,768]{1,0:T(1,128)S(1)}, u32[]{:S(2)}, u32[]{:S(2)}) collective-permute-start(f32[1,768]{1,0:T(1,128)S(1)} %product.3.e0), channel_id=1, source_target_pairs={{3,0},{2,1},{1,2},{0,3},{7,4},{6,5},{5,6},{4,7},{11,8},{10,9},{9,1... | collective-permute-start | bytes 9224 | tf_op jit(solution)/shard_map/ppermute | solution.py:36
  44.1 1.5 %collective-permute-start.15 = (f32[1,768]{1,0:T(1,128)S(1)}, f32[1,768]{1,0:T(1,128)S(1)}, u32[]{:S(2)}, u32[]{:S(2)}) collective-permute-start(f32[1,768]{1,0:T(1,128)S(1)} %product.3.e0), channel_id=1, source_target_pairs={{1,0},{0,1},{3,2},{2,3},{5,4},{4,5},{7,6},{6,7},{9,8},{8,9},{11,10... | collective-permute-start | bytes 9224 | tf_op jit(solution)/shard_map/ppermute | solution.py:36
  45.9 9.8 %collective-permute-start.16 = (f32[2,3,128]{2,1,0:T(4,128)S(1)}, f32[2,3,128]{2,1,0:T(4,128)S(1)}, u32[]{:S(2)}, u32[]{:S(2)}) collective-permute-start(f32[2,3,128]{2,1,0:T(4,128)S(1)} %get-tuple-element.16), channel_id=1, source_target_pairs={{4,0},{6,2},{8,4},{1,5},{10,6},{3,7},{12,8},{5,9},{14,10},{7,11},{... | collective-permute-start | bytes 9224 | tf_op jit(solution)/shard_map/ppermute | solution.py:279
  55.7 1.2 %collective-permute-start.17 = (f32[3,128]{1,0:T(4,128)S(1)}, f32[3,128]{1,0:T(4,128)S(1)}, u32[]{:S(2)}, u32[]{:S(2)}) collective-permute-start(f32[3,128]{1,0:T(4,128)S(1)} %slice_bitcast_fusion), channel_id=1, source_target_pairs={{1,0},{0,1},{3,2},{2,3},{5,4},{4,5},{7,6},{6,7},{9,8},{8,9},{11,10... | collective-permute-start | bytes 4616 | tf_op jit(solution)/shard_map/ppermute | solution.py:36
